TPU v7x, 256 devices: a whole 4x4x8 slice. The times are simulated.
256 devices in a mesh: gx: 8 (over x, core), gy: 32 (over y, z).
Axes of the slice: x: 4, y: 4, z: 8, core: 2. Of those that a mesh axis runs over, the one named last changes fastest.
Arguments:
- positions: float32 [3, 131072], P(None, ('gx', 'gy')), may hold values from 0 to 1
- atom_features: float32 [64, 131072], P(None, ('gx', 'gy')), may hold values from -6 to 6
- pair_neighbor: int32 [8192, 128], P(('gx', 'gy')), may hold values from -1 to 4607, as said below
- offload_slot: int32 [256, 32], P(('gx', 'gy')), may hold values from 0 to 31, each once within a row
- w_center: float32 [64, 256], replicated, may hold values from -0.5 to 0.5
- w_neigh: float32 [64, 256], replicated, may hold values from -0.5 to 0.5
- w_radial: float32 [8, 256], replicated, may hold values from -2 to 2
- w_env: bfloat16 [2, 256, 64], replicated, may hold values from -0.375 to 0.375
- w_latent: bfloat16 [2, 448, 256], replicated, may hold values from -0.25 to 0.25
- w_out: float32 [256], replicated, may hold values from -0.375 to 0.375
Outputs:
- forces: float32 [3, 131072], P(None, ('gx', 'gy'))
- atom_energy: float32 [16384], P(('gx', 'gy'))
- pair_energy: float32 [8192, 128], P(('gx', 'gy'))
Inputs may be any that keep to these rules, and one draw needn't show every extreme that they name: `pair_neighbor`: row b of a device holds the neighbour lists of its atoms 2 * b and 2 * b + 1 in slots 0 to 63 and 64 to 127. Each list has its entries first and -1 after them; an entry n >= 0 names atom n % 512 of the domain at offset (n // 512 // 3 - 1, n // 512 % 3 - 1) along (gx, gy), never the centre itself. A list holds 2 to 64 entries, and some atom of every device has 64. Each device's row is a permutation; row b goes to the device with gy index offload_slot[b] // 1 and the same gx index.
All inputs are finite; a program needn't handle non-finite values.
Results may differ from a plain program's by a relative error of at most 0.008.
Values sent between devices are 32-bit elements; how exact they have to be, the bound alone decides.
No kernel may reach another device: no remote copies, remote signals or barrier semaphores. Data moves between devices by JAX's collectives and lax.ppermute only.
A program may use at most 64 MiB of HBM per device.

v0:
```python
import math

import jax
import jax.numpy as jnp
from jax import lax
from jax.sharding import PartitionSpec as P

SOFTEN = 0.04
CUTOFF = 4.0


def with_halo(cells, sides, width):
    for axis, dim in sides:
        count = lax.axis_size(axis)
        head = lax.slice_in_dim(cells, 0, width, axis=dim)
        tail = lax.slice_in_dim(cells, cells.shape[dim] - width, cells.shape[dim], axis=dim)
        cells = jnp.concatenate(
            [
                lax.ppermute(tail, axis, [(i, (i + 1) % count) for i in range(count)]),
                cells,
                lax.ppermute(head, axis, [((i + 1) % count, i) for i in range(count)]),
            ],
            axis=dim,
        )
    return cells


def harmonics(direction):
    comp_x, comp_y, comp_z = (direction[0], direction[1], direction[2])
    root_three = math.sqrt(3.0)
    root_five = math.sqrt(5.0)
    root_fifteen = math.sqrt(15.0)
    return jnp.stack(
        [
            jnp.ones_like(comp_x),
            root_three * comp_x,
            root_three * comp_y,
            root_three * comp_z,
            root_fifteen * comp_x * comp_y,
            root_fifteen * comp_y * comp_z,
            0.5 * root_five * (3.0 * comp_z * comp_z - 1.0),
            root_fifteen * comp_x * comp_z,
            0.5 * root_fifteen * (comp_x * comp_x - comp_y * comp_y),
        ]
    )


def pair_energies(vectors, centre, neighbor_feat, validity, weights):
    w_center, w_neigh, w_radial, w_env, w_latent, w_out = weights
    nblocks, row_width = validity.shape
    slot_count = row_width // 2
    highest = lax.Precision.HIGHEST
    halves = (
        jnp.arange(row_width, dtype=jnp.int32)[:, None] // slot_count
        == jnp.arange(2, dtype=jnp.int32)[None, :]
    ).astype(jnp.float32)
    distance = jnp.sqrt(jnp.sum(vectors * vectors, axis=0) + SOFTEN)
    direction = vectors / distance
    scaled = distance / CUTOFF
    envelope = validity * jnp.square(1.0 - scaled * scaled)
    orders = jnp.arange(1, w_radial.shape[0] + 1, dtype=jnp.float32)
    radial_basis = jnp.sin(orders[:, None, None] * (jnp.pi * scaled)[None]) / distance[None]
    centre_part = jnp.einsum("fl,fbt->lbt", w_center, centre, precision=highest)
    centre_part = jnp.einsum("lbt,pt->lbp", centre_part, halves, precision=highest)
    preact = centre_part + jnp.einsum("fl,fbp->lbp", w_neigh, neighbor_feat, precision=highest)
    preact = preact + jnp.einsum("nl,nbp->lbp", w_radial, radial_basis, precision=highest)
    latent = jax.nn.silu(preact) * envelope
    harmonic = harmonics(direction)
    layer_count = w_env.shape[0]
    tensor = None
    for layer_index in range(layer_count):
        rounded = latent.astype(jnp.bfloat16)
        weight = (
            jnp.einsum(
                "lc,lbp->cbp", w_env[layer_index], rounded, preferred_element_type=jnp.float32
            )
            * envelope
        )
        product = harmonic[:, None] * weight[None]
        environ = jnp.einsum("kcbp,pt->kcbt", product, halves, precision=highest) / slot_count
        spread = jnp.einsum("kcbt,pt->kcbp", environ, halves, precision=highest)
        if tensor is None:
            tensor = product
        paired = tensor * spread
        scalars = jnp.concatenate(
            [paired[0], jnp.sum(paired[1:4], axis=0), jnp.sum(paired[4:], axis=0)], axis=0
        )
        joined = jnp.concatenate([latent, scalars], axis=0).astype(jnp.bfloat16)
        update = jnp.einsum(
            "kl,kbp->lbp", w_latent[layer_index], joined, preferred_element_type=jnp.float32
        )
        latent = latent + jax.nn.silu(update)
        if layer_index + 1 < layer_count:
            tensor = tensor[0:1] * spread + spread[0:1] * tensor
    return jnp.einsum("l,lbp->bp", w_out, latent, precision=highest) * envelope


def evaluate(vectors, centre, neighbor_feat, validity, weights):
    nblocks = vectors.shape[1]
    row_width = vectors.shape[2]
    group_size = 1
    for candidate in (8, 4, 2):
        if group_size == 1 and nblocks % candidate == 0:
            group_size = candidate
    turn_count = nblocks // group_size

    def take_group(array, first_row):
        return lax.dynamic_slice_in_dim(array, first_row, group_size, 1)

    def step_group(turn_index, loop_state):
        grad_store, energy_store = loop_state
        first_row = turn_index * group_size
        centre_rows = take_group(centre, first_row)
        neighbor_rows = take_group(neighbor_feat, first_row)
        valid_rows = take_group(validity, first_row)[0]

        def energy_of(vector_rows):
            return pair_energies(vector_rows, centre_rows, neighbor_rows, valid_rows, weights)

        out_energy, pullback = jax.vjp(energy_of, take_group(vectors, first_row))
        returned = pullback(jnp.ones_like(out_energy))[0]
        grad_store = lax.dynamic_update_slice_in_dim(grad_store, returned, first_row, 1)
        energy_store = lax.dynamic_update_slice_in_dim(energy_store, out_energy, first_row, 0)
        return (grad_store, energy_store)

    initial = (jnp.zeros_like(vectors), jnp.zeros((nblocks, row_width), jnp.float32))
    return lax.fori_loop(0, turn_count, step_group, initial)


def per_device(
    positions,
    atom_features,
    pair_neighbor,
    offload_slot,
    w_center,
    w_neigh,
    w_radial,
    w_env,
    w_latent,
    w_out,
):
    weights = (w_center, w_neigh, w_radial, w_env, w_latent, w_out)
    atom_count = positions.shape[1]
    feat_width = atom_features.shape[0]
    nblocks = pair_neighbor.shape[0]
    row_width = pair_neighbor.shape[1]
    slot_count = row_width // 2
    peer_count = lax.axis_size("gy")
    send_order = offload_slot[0]
    atom_table = jnp.concatenate([positions, atom_features], axis=0)[:, None, None, :]
    extended = with_halo(atom_table, (("gx", 1), ("gy", 2)), 1)
    offsets = jnp.arange(3, dtype=jnp.float32) - 1.0
    shift_x = jnp.broadcast_to(offsets[:, None, None], (3, 3, atom_count))
    shift_y = jnp.broadcast_to(offsets[None, :, None], (3, 3, atom_count))
    pos_ext = jnp.stack([extended[0] + shift_x, extended[1] + shift_y, extended[2]]).reshape(
        3, 9 * atom_count
    )
    feat_ext = extended[3:].reshape(feat_width, 9 * atom_count)
    neighbor_index = jnp.maximum(pair_neighbor, 0)
    centres = (
        2 * jnp.arange(nblocks, dtype=jnp.int32)[:, None]
        + jnp.arange(row_width, dtype=jnp.int32)[None, :] // slot_count
    )
    vectors = pos_ext[:, neighbor_index] - pos_ext[:, 4 * atom_count + centres]
    neighbor_feat = feat_ext[:, neighbor_index]
    centre = atom_features[:, : 2 * nblocks].reshape(feat_width, nblocks, 2)
    validity = (pair_neighbor >= 0).astype(jnp.float32)[None]
    pair_grads, energies = evaluate(vectors, centre, neighbor_feat, validity, weights)
    centre_energy = energies.reshape(nblocks, 2, slot_count).sum(axis=-1)
    placed = jnp.zeros_like(energies).at[send_order].set(energies)
    placed = placed.reshape(peer_count, nblocks // peer_count, row_width)
    pair_energy = lax.all_to_all(placed, "gy", split_axis=0, concat_axis=0, tiled=True).reshape(
        nblocks, row_width
    )
    grad_ext = (
        jnp.zeros((3, 9 * atom_count), jnp.float32)
        .at[:, neighbor_index.reshape(-1)]
        .add(pair_grads.reshape(3, -1))
    )
    centre_grad = pair_grads.reshape(3, nblocks * 2, slot_count).sum(axis=-1)
    grad_ext = grad_ext.at[:, 4 * atom_count : 4 * atom_count + 2 * nblocks].add(-centre_grad)
    ghost_terms = (-grad_ext).reshape(3, 3, 3, atom_count)
    padded = with_halo(ghost_terms, (("gx", 1), ("gy", 2)), 1)
    forces = padded[:, 0::2, 0::2].sum(axis=(1, 2))
    atom_energy = centre_energy.reshape(2 * nblocks)
    return (forces, atom_energy, pair_energy)


def solution(mesh):
    placed = (
        P(None, ("gx", "gy")),
        P(None, ("gx", "gy")),
        P(("gx", "gy"), None),
        P(("gx", "gy"), None),
        P(),
        P(),
        P(),
        P(),
        P(),
        P(),
    )
    return jax.shard_map(
        per_device,
        mesh=mesh,
        in_specs=placed,
        out_specs=(P(None, ("gx", "gy")), P(("gx", "gy")), P(("gx", "gy"), None)),
        check_vma=False,
    )
```

profile of v0, /device:TPU:8, one launch (start us, length us, event | category | flops | bytes accessed | tf_op | source)
XLA Modules:
  0.0 304.0 jit_solution(18263106068968777530)
XLA Ops:
  1.6 2.9 collective-permute-start.1
  8.8 2.0 collective-permute-start.2
  10.8 3.9 %collective-permute-start.3 = (f32[67,3,1,512]{3,0,2,1:T(8,128)S(1)}, f32[67,3,1,512]{3,0,2,1:T(8,128)S(1)}, u32[]{:S(2)}, u32[]{:S(2)}) collective-permute-start(f32[67,3,1,512]{3,0,2,1:T(8,128)S(1)} %pad_maximum_fusion.4), channel_id=1, source_target_pairs={{1,0},{2,1},{3,2},{4,3},{5,4},{6,5},{7,6},{8,7},{9,8},{10,9},{11,1... | collective-permute-start | bytes 1234952 | tf_op jit(solution)/shard_map/ppermute | solution.py:21
  15.5 8.5 %collective-permute-done.2 = f32[67,3,1,512]{3,0,2,1:T(8,128)S(1)} collective-permute-done((f32[67,3,1,512]{3,0,2,1:T(8,128)S(1)}, f32[67,3,1,512]{3,0,2,1:T(8,128)S(1)}, u32[]{:S(2)}, u32[]{:S(2)}) %collective-permute-start.2) | collective-permute-done | bytes 411680 | tf_op jit(solution)/shard_map/ppermute | solution.py:19
  25.6 14.1 %gather_fusion.1 = f32[4096,3]{1,0:T(8,128)} fusion(f32[3,4608]{0,1:T(8,128)S(1)} %copy.157, s32[4096]{0:T(1024)S(1)} %fusion.183), kind=kCustom, calls=%fused_computation.1 | custom fusion | bytes 114688 | tf_op jit(solution)/shard_map/gather | solution.py:164
  39.7 14.1 %gather_fusion = f32[4096,3]{1,0:T(8,128)} fusion(f32[3,4608]{0,1:T(8,128)S(1)} %copy.157, s32[4096]{0:T(1024)S(1)} %bitcast_clamp_fusion), kind=kCustom, calls=%fused_computation | custom fusion | bytes 114688 | tf_op jit(solution)/shard_map/gather | solution.py:164
  53.8 2.5 sub.116
  56.3 1.2 copy.159
  57.5 1.4 pad_maximum_fusion
  59.8 15.4 %gather_fusion.2 = f32[4096,64]{1,0:T(8,128)} fusion(f32[64,4608]{0,1:T(8,128)S(1)} %bitcast.286, s32[4096]{0:T(1024)} %copy-done.10), kind=kCustom, calls=%fused_computation.2 | custom fusion | bytes 2113536 | tf_op jit(solution)/shard_map/gather | solution.py:165
  75.2 2.2 copy.162
  77.5 168.6 %while.18 = (s32[]{:T(128)}, f32[3,32,128]{2,1,0:T(8,128)S(1)}, f32[32,128]{1,0:T(8,128)S(1)}, f32[3,32,128]{2,1,0:T(8,128)S(1)}, f32[64,32,2]{0,2,1:T(2,128)}, ...) while((s32[]{:T(128)}, f32[3,32,128]{2,1,0:T(8,128)S(1)}, ...), condition=%wide.region_18.19_spmd, body=%wide.region_0.18_spmd.sunk | while | flops 1512813824 | bytes 107684224 | solution.py:127
  98.4 2.3 multiply_convert_fusion.2
  101.1 2.8 fusion.281
  104.2 2.0 fusion.282
  109.4 2.8 fusion.285
  112.4 2.5 fusion.286
  115.6 1.4 fusion.288
  118.0 3.1 %fusion.290 = f32[9,64,8,2]{1,3,2,0:T(2,128)S(1)} fusion(f32[1,64,8,128]{3,1,2,0:T(8,128)S(1)} %get-tuple-element.565, f32[3,64,8,128]{3,1,2,0:T(8,128)S(1)} %broadcast_in_dim.167, f32[5,64,8,128]{3,1,2,0:T(8,128)S(1)} %broadcast_in_dim.168, f32[9,64,8,128]{3,2,1,0:T(8,128)S(1)} %fusion.282, f32[64,8,128]{2,0,1:T(8,128)S(1)} %copy.222, ...), kind=kOutput, calls=%fused_computation.71.clone.1 | convolution fusion | flops 18294016 | bytes 5579264 | tf_op jit(solution)/shard_map/while/body/eval_jaxpr/transpose(jvp(kcbt,pt->kcbp))/dot_general | solution.py:81
  121.2 2.9 fusion.291
  125.4 3.1 %fusion.294 = f32[9,64,8,2]{1,3,2,0:T(2,128)S(1)} fusion(f32[1,64,8,128]{3,1,2,0:T(8,128)S(1)} %bitcast.305, f32[1,64,8,128]{3,1,2,0:T(8,128)S(1)} %get-tuple-element.571, f32[3,64,8,128]{3,1,2,0:T(8,128)S(1)} %broadcast_in_dim.169, f32[5,64,8,128]{3,1,2,0:T(8,128)S(1)} %broadcast_in_dim.170, f32[64,8,128]{2,0,1:T(8,128)S(1)} %slice_bitcast_fusion.7, ...), kind=kOutput, calls=%fused_computation.72.clone.1 | convolution fusion | flops 20063488 | bytes 7938560 | tf_op jit(solution)/shard_map/while/body/eval_jaxpr/transpose(jvp(kcbt,pt->kcbp))/dot_general | solution.py:81
  128.5 2.8 multiply_reduce_fusion.16
  131.8 1.1 fusion.297
  136.0 2.3 multiply_convert_fusion.2
  138.7 2.8 fusion.281
  141.9 2.0 fusion.282
  147.1 2.8 fusion.285
  150.1 2.5 fusion.286
  153.2 1.4 fusion.288
  155.7 3.1 %fusion.290 = f32[9,64,8,2]{1,3,2,0:T(2,128)S(1)} fusion(f32[1,64,8,128]{3,1,2,0:T(8,128)S(1)} %get-tuple-element.565, f32[3,64,8,128]{3,1,2,0:T(8,128)S(1)} %broadcast_in_dim.167, f32[5,64,8,128]{3,1,2,0:T(8,128)S(1)} %broadcast_in_dim.168, f32[9,64,8,128]{3,2,1,0:T(8,128)S(1)} %fusion.282, f32[64,8,128]{2,0,1:T(8,128)S(1)} %copy.222, ...), kind=kOutput, calls=%fused_computation.71.clone.1 | convolution fusion | flops 18294016 | bytes 5579264 | tf_op jit(solution)/shard_map/while/body/eval_jaxpr/transpose(jvp(kcbt,pt->kcbp))/dot_general | solution.py:81
  158.8 2.9 fusion.291
  163.1 3.1 %fusion.294 = f32[9,64,8,2]{1,3,2,0:T(2,128)S(1)} fusion(f32[1,64,8,128]{3,1,2,0:T(8,128)S(1)} %bitcast.305, f32[1,64,8,128]{3,1,2,0:T(8,128)S(1)} %get-tuple-element.571, f32[3,64,8,128]{3,1,2,0:T(8,128)S(1)} %broadcast_in_dim.169, f32[5,64,8,128]{3,1,2,0:T(8,128)S(1)} %broadcast_in_dim.170, f32[64,8,128]{2,0,1:T(8,128)S(1)} %slice_bitcast_fusion.7, ...), kind=kOutput, calls=%fused_computation.72.clone.1 | convolution fusion | flops 20063488 | bytes 7938560 | tf_op jit(solution)/shard_map/while/body/eval_jaxpr/transpose(jvp(kcbt,pt->kcbp))/dot_general | solution.py:81
  166.2 2.8 multiply_reduce_fusion.16
  173.7 2.3 multiply_convert_fusion.2
  176.4 2.8 fusion.281
  179.5 2.0 fusion.282
  184.7 2.8 fusion.285
  187.7 2.5 fusion.286
  190.9 1.4 fusion.288
  193.3 3.1 %fusion.290 = f32[9,64,8,2]{1,3,2,0:T(2,128)S(1)} fusion(f32[1,64,8,128]{3,1,2,0:T(8,128)S(1)} %get-tuple-element.565, f32[3,64,8,128]{3,1,2,0:T(8,128)S(1)} %broadcast_in_dim.167, f32[5,64,8,128]{3,1,2,0:T(8,128)S(1)} %broadcast_in_dim.168, f32[9,64,8,128]{3,2,1,0:T(8,128)S(1)} %fusion.282, f32[64,8,128]{2,0,1:T(8,128)S(1)} %copy.222, ...), kind=kOutput, calls=%fused_computation.71.clone.1 | convolution fusion | flops 18294016 | bytes 5579264 | tf_op jit(solution)/shard_map/while/body/eval_jaxpr/transpose(jvp(kcbt,pt->kcbp))/dot_general | solution.py:81
  196.5 2.9 fusion.291
  200.7 3.1 %fusion.294 = f32[9,64,8,2]{1,3,2,0:T(2,128)S(1)} fusion(f32[1,64,8,128]{3,1,2,0:T(8,128)S(1)} %bitcast.305, f32[1,64,8,128]{3,1,2,0:T(8,128)S(1)} %get-tuple-element.571, f32[3,64,8,128]{3,1,2,0:T(8,128)S(1)} %broadcast_in_dim.169, f32[5,64,8,128]{3,1,2,0:T(8,128)S(1)} %broadcast_in_dim.170, f32[64,8,128]{2,0,1:T(8,128)S(1)} %slice_bitcast_fusion.7, ...), kind=kOutput, calls=%fused_computation.72.clone.1 | convolution fusion | flops 20063488 | bytes 7938560 | tf_op jit(solution)/shard_map/while/body/eval_jaxpr/transpose(jvp(kcbt,pt->kcbp))/dot_general | solution.py:81
  203.8 2.8 multiply_reduce_fusion.16
  211.3 2.3 multiply_convert_fusion.2
  214.0 2.8 fusion.281
  217.2 2.0 fusion.282
  222.4 2.8 fusion.285
  225.4 2.5 fusion.286
  228.5 1.4 fusion.288
  231.0 3.1 %fusion.290 = f32[9,64,8,2]{1,3,2,0:T(2,128)S(1)} fusion(f32[1,64,8,128]{3,1,2,0:T(8,128)S(1)} %get-tuple-element.565, f32[3,64,8,128]{3,1,2,0:T(8,128)S(1)} %broadcast_in_dim.167, f32[5,64,8,128]{3,1,2,0:T(8,128)S(1)} %broadcast_in_dim.168, f32[9,64,8,128]{3,2,1,0:T(8,128)S(1)} %fusion.282, f32[64,8,128]{2,0,1:T(8,128)S(1)} %copy.222, ...), kind=kOutput, calls=%fused_computation.71.clone.1 | convolution fusion | flops 18294016 | bytes 5579264 | tf_op jit(solution)/shard_map/while/body/eval_jaxpr/transpose(jvp(kcbt,pt->kcbp))/dot_general | solution.py:81
  234.1 2.9 fusion.291
  238.4 3.1 %fusion.294 = f32[9,64,8,2]{1,3,2,0:T(2,128)S(1)} fusion(f32[1,64,8,128]{3,1,2,0:T(8,128)S(1)} %bitcast.305, f32[1,64,8,128]{3,1,2,0:T(8,128)S(1)} %get-tuple-element.571, f32[3,64,8,128]{3,1,2,0:T(8,128)S(1)} %broadcast_in_dim.169, f32[5,64,8,128]{3,1,2,0:T(8,128)S(1)} %broadcast_in_dim.170, f32[64,8,128]{2,0,1:T(8,128)S(1)} %slice_bitcast_fusion.7, ...), kind=kOutput, calls=%fused_computation.72.clone.1 | convolution fusion | flops 20063488 | bytes 7938560 | tf_op jit(solution)/shard_map/while/body/eval_jaxpr/transpose(jvp(kcbt,pt->kcbp))/dot_general | solution.py:81
  241.5 2.8 multiply_reduce_fusion.16
  244.7 1.1 fusion.297
  247.1 25.0 %scatter_custom_fusion = f32[3,4608]{0,1:T(8,128)} fusion(s32[4096]{0:T(1024)} %bitcast.303, f32[4096,3]{1,0:T(8,128)S(1)} %bitcast.292, f32[]{:T(128)} %constant.281.clone.1), kind=kCustom, calls=%fused_computation.268 | custom fusion | flops 12288 | bytes 55808 | tf_op jit(solution)/shard_map/scatter-add | solution.py:178
  272.1 2.0 fusion.181
  274.1 1.8 neg.85
  276.9 1.4 copy.194
  278.6 3.0 collective-permute-start.5
  282.4 1.2 scatter_custom_fusion.1
  283.7 10.0 %all-to-all-start = ((f32[32,1,128]{2,1,0:T(1,128)}), f32[32,1,128]{2,1,0:T(1,128)S(1)}, u32[]{:S(2)}, u32[]{:S(2)}) async-start(f32[32,1,128]{2,1,0:T(1,128)} %bitcast.63), calls=%async_computation | async-start | bytes 32768 | tf_op jit(solution)/shard_map/all_to_all | solution.py:172
  293.8 1.5 collective-permute-start.6
  295.3 2.7 collective-permute-start.7
  298.9 3.4 %all-to-all-done = f32[32,1,128]{2,1,0:T(1,128)S(1)} async-done(((f32[32,1,128]{2,1,0:T(1,128)}), f32[32,1,128]{2,1,0:T(1,128)S(1)}, u32[]{:S(2)}, u32[]{:S(2)}) %all-to-all-start) | async-done | bytes 16416 | tf_op jit(solution)/shard_map/all_to_all | solution.py:172
  (303 shorter events, 57.6 us)
Async XLA Ops:
  1.6 22.5 %copy-start.1 = (f32[67,1,1,512]{3,0,2,1:T(8,128)}, f32[67,1,1,512]{3,0,2,1:T(8,128)S(1)}, u32[]{:S(2)}) copy-start(f32[67,1,1,512]{3,0,2,1:T(8,128)S(1)} %maximum_bitcast_fusion) | copy-start | bytes 411652
  1.6 7.2 %collective-permute-start = (f32[67,1,1,512]{3,0,2,1:T(8,128)S(1)}, f32[67,1,1,512]{3,0,2,1:T(8,128)S(1)}, u32[]{:S(2)}, u32[]{:S(2)}) collective-permute-start(f32[67,1,1,512]{3,0,2,1:T(8,128)S(1)} %maximum_bitcast_fusion), channel_id=1, source_target_pairs={{0,32},{32,64},{64,96},{96,128},{128,160},{160,192},{192,224},{224... | collective-permute-start | bytes 411656 | tf_op jit(solution)/shard_map/ppermute | solution.py:19
  1.6 7.1 %collective-permute-start.1 = (f32[67,1,1,512]{3,0,2,1:T(8,128)S(1)}, f32[67,1,1,512]{3,0,2,1:T(8,128)S(1)}, u32[]{:S(2)}, u32[]{:S(2)}) collective-permute-start(f32[67,1,1,512]{3,0,2,1:T(8,128)S(1)} %maximum_bitcast_fusion), channel_id=1, source_target_pairs={{32,0},{64,32},{96,64},{128,96},{160,128},{192,160},{224,192},{0,2... | collective-permute-start | bytes 411656 | tf_op jit(solution)/shard_map/ppermute | solution.py:21
  5.3 34.5 %copy-start.10 = (s32[4096]{0:T(1024)}, s32[4096]{0:T(1024)S(1)}, u32[]{:S(2)}) copy-start(s32[4096]{0:T(1024)S(1)} %bitcast_clamp_fusion) | copy-start | bytes 49156
  8.7 15.3 %copy-start.8 = (f32[67,1,1,512]{3,0,2,1:T(8,128)}, f32[67,1,1,512]{3,0,2,1:T(8,128)S(1)}, u32[]{:S(2)}) copy-start(f32[67,1,1,512]{3,0,2,1:T(8,128)S(1)} %collective-permute-done) | copy-start | bytes 411652
  8.7 15.3 %copy-start.9 = (f32[67,1,1,512]{3,0,2,1:T(8,128)}, f32[67,1,1,512]{3,0,2,1:T(8,128)S(1)}, u32[]{:S(2)}) copy-start(f32[67,1,1,512]{3,0,2,1:T(8,128)S(1)} %collective-permute-done.1) | copy-start | bytes 411652
  8.8 15.2 %collective-permute-start.2 = (f32[67,3,1,512]{3,0,2,1:T(8,128)S(1)}, f32[67,3,1,512]{3,0,2,1:T(8,128)S(1)}, u32[]{:S(2)}, u32[]{:S(2)}) collective-permute-start(f32[67,3,1,512]{3,0,2,1:T(8,128)S(1)} %pad_maximum_fusion.4), channel_id=1, source_target_pairs={{0,1},{1,2},{2,3},{3,4},{4,5},{5,6},{6,7},{7,8},{8,9},{9,10},{10,1... | collective-permute-start | bytes 1234952 | tf_op jit(solution)/shard_map/ppermute | solution.py:19
  10.8 13.2 %collective-permute-start.3 = (f32[67,3,1,512]{3,0,2,1:T(8,128)S(1)}, f32[67,3,1,512]{3,0,2,1:T(8,128)S(1)}, u32[]{:S(2)}, u32[]{:S(2)}) collective-permute-start(f32[67,3,1,512]{3,0,2,1:T(8,128)S(1)} %pad_maximum_fusion.4), channel_id=1, source_target_pairs={{1,0},{2,1},{3,2},{4,3},{5,4},{6,5},{7,6},{8,7},{9,8},{10,9},{11,1... | collective-permute-start | bytes 1234952 | tf_op jit(solution)/shard_map/ppermute | solution.py:21
  23.9 0.8 copy-start.3
  23.9 0.9 copy-start.4
  53.8 3.7 %copy-start.2 = (f32[67,1,1,512]{3,0,2,1:T(8,128)S(1)}, f32[67,1,1,512]{3,0,2,1:T(8,128)}, u32[]{:S(2)}) copy-start(f32[67,1,1,512]{3,0,2,1:T(8,128)} %copy-done.1) | copy-start | bytes 411652
  75.2 2.3 copy-start
  75.2 2.3 copy-start.5
  75.2 2.3 copy-start.6
  75.2 2.3 copy-start.7
  75.2 2.3 copy-start.11
  75.2 2.3 copy-start.13
  107.0 1.0 copy-start.12
  107.0 1.4 copy-start.15
  144.6 1.0 copy-start.12
  144.7 1.4 copy-start.15
  182.3 1.0 copy-start.12
  182.3 1.4 copy-start.15
  219.9 1.0 copy-start.12
  220.0 1.4 copy-start.15
  275.9 5.6 %copy-start.14 = (s32[1,32]{1,0:T(1,128)S(1)}, s32[1,32]{1,0:T(1,128)}, u32[]{:S(2)}) copy-start(s32[1,32]{1,0:T(1,128)} %param.17) | copy-start | bytes 388
  278.3 15.4 %collective-permute-start.4 = (f32[3,1,3,512]{3,1,2,0:T(1,128)S(1)}, f32[3,1,3,512]{3,1,2,0:T(1,128)S(1)}, u32[]{:S(2)}, u32[]{:S(2)}) collective-permute-start(f32[3,1,3,512]{3,1,2,0:T(1,128)S(1)} %copy.194), channel_id=1, source_target_pairs={{0,32},{32,64},{64,96},{96,128},{128,160},{160,192},{192,224},{224... | collective-permute-start | bytes 55304 | tf_op jit(solution)/shard_map/ppermute | solution.py:19
  278.6 15.1 %collective-permute-start.5 = (f32[3,1,3,512]{3,1,2,0:T(1,128)S(1)}, f32[3,1,3,512]{3,1,2,0:T(1,128)S(1)}, u32[]{:S(2)}, u32[]{:S(2)}) collective-permute-start(f32[3,1,3,512]{3,1,2,0:T(1,128)S(1)} %copy.195), channel_id=1, source_target_pairs={{32,0},{64,32},{96,64},{128,96},{160,128},{192,160},{224,192},{0,2... | collective-permute-start | bytes 55304 | tf_op jit(solution)/shard_map/ppermute | solution.py:21
  283.7 18.6 %all-to-all-start = ((f32[32,1,128]{2,1,0:T(1,128)}), f32[32,1,128]{2,1,0:T(1,128)S(1)}, u32[]{:S(2)}, u32[]{:S(2)}) async-start(f32[32,1,128]{2,1,0:T(1,128)} %bitcast.63), calls=%async_computation | async-start | bytes 32768 | tf_op jit(solution)/shard_map/all_to_all | solution.py:172
  293.8 8.5 %collective-permute-start.6 = (f32[3,5,1,512]{3,2,1,0:T(1,128)S(1)}, f32[3,5,1,512]{3,2,1,0:T(1,128)S(1)}, u32[]{:S(2)}, u32[]{:S(2)}) collective-permute-start(f32[3,5,1,512]{3,2,1,0:T(1,128)S(1)} %get-tuple-element.434), channel_id=1, source_target_pairs={{0,1},{1,2},{2,3},{3,4},{4,5},{5,6},{6,7},{7,8},{8,9},{9,10},{10,1... | collective-permute-start | bytes 92168 | tf_op jit(solution)/shard_map/ppermute | solution.py:19
  295.3 6.9 %collective-permute-start.7 = (f32[3,5,1,512]{3,2,1,0:T(1,128)S(1)}, f32[3,5,1,512]{3,2,1,0:T(1,128)S(1)}, u32[]{:S(2)}, u32[]{:S(2)}) collective-permute-start(f32[3,5,1,512]{3,2,1,0:T(1,128)S(1)} %get-tuple-element.435), channel_id=1, source_target_pairs={{1,0},{2,1},{3,2},{4,3},{5,4},{6,5},{7,6},{8,7},{9,8},{10,9},{11,1... | collective-permute-start | bytes 92168 | tf_op jit(solution)/shard_map/ppermute | solution.py:21
where the time goes:
time: 309 us; the launch traced here: 304 us
  matrix products  132 us (43%)
  local copies, waits for them, and re-layouts  69.7 us (23%)
  other arithmetic  43.2 us (14%)
  starting transfers between devices  26 us (8%)
  loops' own time  19.7 us (6%)
  waiting for transfers between devices  11.8 us (4%)
    dot_general x16, matrix products, pair_energies(): jnp.einsum('kcbp,pt->kcbt', product, halves, precision=highest) / slot_count  45.2 us
    dot_general x16, matrix products, pair_energies(): spread = jnp.einsum('kcbt,pt->kcbp', environ, halves, precision=highest)  43 us
    gather x2, local copies, waits for them, and re-layouts, per_device(): vectors = pos_ext[:, neighbor_index] - pos_ext[:, 4 * atom_count + centres]  28.2 us
    scatter-add x1, other arithmetic, per_device(): grad_ext = jnp.zeros((3, 9 * atom_count), jnp.float32).at[:, neighbor_ind...  25 us
    another operation x1, loops' own time, evaluate(): return lax.fori_loop(0, turn_count, step_group, initial)  19.7 us
    gather x2, local copies, waits for them, and re-layouts, per_device(): neighbor_feat = feat_ext[:, neighbor_index]  17.6 us
    dot_general x8, matrix products, pair_energies(): jnp.einsum('nl,nbp->lbp', w_radial, radial_basis, precision=highest)  13.6 us
    ppermute x4, starting transfers between devices, with_halo(): lax.ppermute(head, axis, [((i + 1) % count, i) for i in range(count)])  12.5 us
  transfers between devices with their start and end apart: 9, of which 2 were waited for; matrix products, arithmetic and copies ran while one was open for 3% of the time, Pallas kernels for 0%

commit v1 on v0

v1 whole, which is shorter than its diff:
```python
import math

import jax
import jax.numpy as jnp
from jax import lax
from jax.experimental import pallas as pl
from jax.experimental.pallas import tpu as pltpu
from jax.sharding import PartitionSpec as P

SOFTEN = 0.04
CUTOFF = 4.0
BF = jnp.bfloat16
F32 = jnp.float32
R3 = math.sqrt(3.0)
R5 = math.sqrt(5.0)
R15 = math.sqrt(15.0)
ROWS = 32
WIDTH = 128
SLOTS = 64
ATOMS = 512
NB = 8
M = NB * WIDTH
NT = (((1,), (1,)), ((), ()))
HPAD = 40


def mm(a, b):
    return jnp.dot(a, b, preferred_element_type=F32)


def cat(*xs):
    return jnp.concatenate(xs, axis=1)


def mm_nt(a, b):
    return lax.dot_general(a, b, NT, preferred_element_type=F32)


def split2(x):
    hi = x.astype(BF)
    return hi, (x - hi.astype(F32)).astype(BF)


def kernel(
    idx_s, slot_s, idx_v, t0, t1, t2, t3, t4, t5, t6, t7, t8, cpart, win_ref,
    we0_ref, we1_ref, wl0_ref, wl1_ref, wl0t_ref, wl1t_ref, lat0t_ref, lat1t_ref,
    wout_ref, rad_ref,
    left_ref, mid_ref, right_ref, ae_ref, placed_ref,
    table, gbuf, pos, geo, bgeo, lhs, rhs,
):
    tables = (t0, t1, t2, t3, t4, t5, t6, t7, t8)
    feats = 64
    for o in range(9):
        ref = tables[o]
        shift = jnp.concatenate(
            [jnp.full((1, ATOMS), o // 3 - 1.0, F32), jnp.full((1, ATOMS), o % 3 - 1.0, F32),
             jnp.zeros((1, ATOMS), F32)], axis=0)
        posr = ref[feats:feats + 3, :] + shift
        for q in range(ATOMS // 128):
            block = jnp.concatenate(
                [ref[0:feats, q * 128:(q + 1) * 128], posr[:, q * 128:(q + 1) * 128],
                 jnp.zeros((61, 128), F32)], axis=0)
            table[pl.ds(o * ATOMS + q * 128, 128), :] = block.T

    def gather_row(b, carry):
        base = b * WIDTH
        for t in range(WIDTH):
            n = jnp.maximum(idx_s[b, t], 0)
            gbuf[pl.ds(base + t, 1), :] = table[pl.ds(n, 1), :]
        gt = gbuf[pl.ds(pl.multiple_of(base, WIDTH), WIDTH), :].T
        for c in range(3):
            pos[c, pl.ds(b, 1), :] = gt[feats + c:feats + c + 1, :]
        return carry

    lax.fori_loop(0, ROWS, gather_row, 0)

    lane = lax.broadcasted_iota(jnp.int32, (ROWS, WIDTH), 1)
    own = table[pl.ds(4 * ATOMS, 128), :]
    own_t = own.T
    row_i = lax.broadcasted_iota(jnp.int32, (ROWS, WIDTH), 0)
    vec = []
    for c in range(3):
        line = jnp.broadcast_to(own_t[feats + c:feats + c + 1, :], (ROWS, WIDTH))
        first = jnp.sum(jnp.where(lane == 2 * row_i, line, 0.0), axis=1, keepdims=True)
        second = jnp.sum(jnp.where(lane == 2 * row_i + 1, line, 0.0), axis=1, keepdims=True)
        vec.append(pos[c] - jnp.where(lane < SLOTS, first, second))
    vx, vy, vz = vec
    index = idx_v[...]
    valid = (index >= 0).astype(F32)
    dist = jnp.sqrt(vx * vx + vy * vy + vz * vz + SOFTEN)
    inv = 1.0 / dist
    ux, uy, uz = vx * inv, vy * inv, vz * inv
    scaled = dist * (1.0 / CUTOFF)
    poly = 1.0 - scaled * scaled
    env = valid * (poly * poly)
    theta = math.pi * scaled
    sin1, cos1 = jnp.sin(theta), jnp.cos(theta)
    sins, coss = [sin1], [cos1]
    sprev, cprev = jnp.zeros_like(sin1), jnp.ones_like(cos1)
    for _ in range(7):
        snext = 2.0 * cos1 * sins[-1] - sprev
        cnext = 2.0 * cos1 * coss[-1] - cprev
        sprev, cprev = sins[-1], coss[-1]
        sins.append(snext)
        coss.append(cnext)
    sph = [
        jnp.ones_like(ux), R3 * ux, R3 * uy, R3 * uz, R15 * ux * uy, R15 * uy * uz,
        0.5 * R5 * (3.0 * uz * uz - 1.0), R15 * ux * uz, 0.5 * R15 * (ux * ux - uy * uy),
    ]
    zero = jnp.zeros_like(ux)
    rows = sph + [zero] * 7
    for s in sins:
        rows.append(s * inv)
    rows.append(env)
    rows += [zero] * 7
    for q in range(len(rows)):
        for b in range(ROWS):
            geo[b, q:q + 1, :] = rows[q][b:b + 1, :]

    lane_b = lax.broadcasted_iota(jnp.int32, (16, WIDTH), 1)
    half0 = (lane_b < SLOTS).astype(F32)
    half1 = 1.0 - half0
    kk = lax.broadcasted_iota(jnp.int32, (32, 256), 0) % 16
    gg = lax.broadcasted_iota(jnp.int32, (32, 256), 1) // 64
    group = jnp.where(kk == 0, 0, jnp.where(kk < 4, 1, jnp.where(kk < 9, 2, 4)))
    gmask = (group == gg).astype(F32)
    row0 = (kk == 0).astype(F32)
    upper = (lax.broadcasted_iota(jnp.int32, (32, 128), 1) >= 64)
    upper_m = lax.broadcasted_iota(jnp.int32, (M, 128), 1) >= 64
    first_row = lax.broadcasted_iota(jnp.int32, (32, 1), 0) < 16

    def row0_of(x):
        return jnp.concatenate(
            [jnp.broadcast_to(x[0:1], (16, x.shape[1])), jnp.broadcast_to(x[16:17], (16, x.shape[1]))], axis=0)

    def ksum(x):
        s0 = jnp.sum(x[0:16], axis=0, keepdims=True)
        s1 = jnp.sum(x[16:32], axis=0, keepdims=True)
        return jnp.concatenate(
            [jnp.broadcast_to(s0, (16, x.shape[1])), jnp.broadcast_to(s1, (16, x.shape[1]))], axis=0) * row0

    def fold(x):
        s = x[:, 0:128] + x[:, 128:256]
        return s + pltpu.roll(s, 64, 1)

    def act(h):
        t = jnp.tanh(h)
        u = 1.0 + t
        a = h * u
        return a, u + a * (1.0 - t)

    def chunk(i, carry):
        first = pl.multiple_of(i * M, M)
        g = gbuf[pl.ds(first, M), :]
        ghi, glo = split2(g)
        st, tr, cadd = [], [], []
        centres = cpart[pl.ds(pl.multiple_of(i * 2 * NB, 2 * NB), 2 * NB), :]
        for b in range(NB):
            blk = geo[i * NB + b]
            s0 = blk[0:16] * half0
            s1 = blk[0:16] * half1
            bas = blk[16:24]
            bhi = bas.astype(BF).astype(F32)
            full = jnp.concatenate(
                [s0, s1, bhi, bas - bhi, bhi, blk[24:32], jnp.zeros((64, WIDTH), F32)], axis=0)
            tr.append(full.T)
            st.append(jnp.concatenate([s0, s1], axis=0).astype(BF))
            cadd.append(jnp.broadcast_to(centres[2 * b:2 * b + 1], (SLOTS, 256)))
            cadd.append(jnp.broadcast_to(centres[2 * b + 1:2 * b + 2], (SLOTS, 256)))
        trans = jnp.concatenate(tr, axis=0)
        env1 = jnp.broadcast_to(trans[:, 56:57], (M, 128))
        env2 = jnp.concatenate([env1, env1], axis=1)
        tb = trans.astype(BF)
        sbd = tb[:, 0:32]
        h0 = (
            mm(cat(ghi, glo, ghi, tb), win_ref[...])
            + jnp.concatenate(cadd, axis=0)
        )
        a0, d0 = act(h0)
        lat0 = a0 * env2
        r0 = lat0.astype(BF)
        y0 = mm(r0, we0_ref[...])
        w0 = y0 * env2
        w0b = w0.astype(BF)

        def per_row(fn):
            return [fn(b, slice(b * WIDTH, (b + 1) * WIDTH)) for b in range(NB)]

        e0 = per_row(lambda b, s: mm(st[b], w0b[s]) * (1.0 / SLOTS))
        b0 = [(e * gmask).astype(BF) for e in e0]
        a_0 = jnp.concatenate(per_row(lambda b, s: mm(sbd[s], b0[b])), axis=0)
        sc0 = (w0 * a_0).astype(BF)
        h1 = mm(cat(r0, sc0), wl0_ref[...])
        a1, d1 = act(h1)
        lat1 = lat0 + a1
        r1 = lat1.astype(BF)
        y1 = mm(r1, we1_ref[...])
        w1b = (y1 * env2).astype(BF)
        e1 = per_row(lambda b, s: mm(st[b], w1b[s]) * (1.0 / SLOTS))
        b1 = [row0_of(e0[b]) * e1[b] * gmask + ksum(e0[b] * e1[b] * gmask) for b in range(NB)]
        b1 = [x.astype(BF) for x in b1]
        a_1 = jnp.concatenate(per_row(lambda b, s: mm(sbd[s], b1[b])), axis=0)
        sc1 = (w0 * a_1).astype(BF)
        h2 = mm(cat(r1, sc1), wl1_ref[...])
        a2, d2 = act(h2)
        wo = wout_ref[...]
        pq = (lat1 + a2) * wo
        pqh, pql = split2(pq[:, 0:128] + pq[:, 128:256])
        dlat2 = env2 * wo
        dz1 = (dlat2 * d2).astype(BF)
        dsc1 = mm(dz1, wl1t_ref[...])
        dw0 = dsc1 * a_1
        da1 = dsc1 * w0
        da1 = jnp.concatenate(
            [da1[:, 0:128].astype(BF), jnp.where(upper_m, w1b[:, 128:256].astype(F32), da1[:, 128:256]).astype(BF)], axis=1)
        db1 = per_row(lambda b, s: mm(st[b], da1[s]))
        de1, x0 = [], []
        for b in range(NB):
            head = row0_of(db1[b])
            prod = db1[b] * gmask
            de1.append(fold(gmask * head * e0[b] + prod * row0_of(e0[b])) * (1.0 / SLOTS))
            x0.append(gmask * head * e1[b] + ksum(prod * e1[b]))
        de1 = [jnp.where(upper, x, 0.0).astype(BF) for x in de1]
        b1c = [jnp.concatenate([b1[b][:, 0:128], (b1[b][:, 128:256].astype(F32) + de1[b].astype(F32)).astype(BF)], axis=1) for b in range(NB)]
        ds1 = per_row(lambda b, s: mm_nt(da1[s], b1c[b]))
        dw1 = jnp.concatenate(per_row(lambda b, s: mm(sbd[s], de1[b])), axis=0)
        ev = dw1 * y1[:, 128:256]
        dlat1 = dlat2 + mm(cat(dz1, (dw1 * env1).astype(BF)), lat1t_ref[...])
        dz0 = (dlat1 * d1).astype(BF)
        dsc0 = mm(dz0, wl0t_ref[...])
        dw0 = dw0 + dsc0 * a_0
        da0 = dsc0 * w0
        da0 = jnp.concatenate(
            [da0[:, 0:128].astype(BF), jnp.where(upper_m, w0[:, 128:256], da0[:, 128:256]).astype(BF)], axis=1)
        db0 = per_row(lambda b, s: mm(st[b], da0[s]))
        de0 = [jnp.where(upper, fold(x0[b] + gmask * db0[b]) * (1.0 / SLOTS), 0.0) for b in range(NB)]
        b0c = [jnp.concatenate([b0[b][:, 0:128], (b0[b][:, 128:256].astype(F32) + de0[b]).astype(BF)], axis=1) for b in range(NB)]
        ds = per_row(lambda b, s: ds1[b] + mm_nt(da0[s], b0c[b]))
        dw0e = jnp.concatenate(per_row(lambda b, s: mm(sbd[s], de0[b].astype(BF))), axis=0)
        dw0 = jnp.concatenate([dw0[:, 0:128], dw0[:, 128:256] + dw0e], axis=1)
        dlat0 = dlat1 + mm(cat(dz0, (dw0 * env2).astype(BF)), lat0t_ref[...])
        evl = dlat0 * a0 + dw0 * y0
        ev = ev + evl[:, 0:128] + evl[:, 128:256]
        evh, evo = split2(ev)
        dx0 = (dlat0 * env2 * d0).astype(BF)
        res = mm(cat(dx0, pqh, pql, evh, evo), rad_ref[...])
        for b in range(NB):
            dst = ds[b].T
            bgeo[i * NB + b, 0:16, :] = dst[0:16] * half0 + dst[16:32] * half1
            bgeo[i * NB + b, 16:32, :] = res[b * WIDTH:(b + 1) * WIDTH].T[0:16]
        return carry

    lax.fori_loop(0, ROWS // NB, chunk, 0)

    back = []
    for q in range(26):
        back.append(jnp.concatenate([bgeo[b, q:q + 1, :] for b in range(ROWS)], axis=0))
    gs, gb, q_e, denv = back[0:9], back[16:24], back[24], back[25]
    energy = env * q_e
    denv = denv + q_e
    dux = R3 * gs[1] + R15 * (uy * gs[4] + uz * gs[7] + ux * gs[8])
    duy = R3 * gs[2] + R15 * (ux * gs[4] + uz * gs[5] - uy * gs[8])
    duz = R3 * gs[3] + R15 * (uy * gs[5] + ux * gs[7]) + 3.0 * R5 * uz * gs[6]
    dd = denv * (valid * poly * scaled * (-4.0 / CUTOFF))
    for n in range(8):
        dd = dd + gb[n] * inv * (((n + 1) * math.pi / CUTOFF) * coss[n] - sins[n] * inv)
    dd = dd - (dux * ux + duy * uy + duz * uz) * inv
    dv = [dux * inv + dd * ux, duy * inv + dd * uy, duz * inv + dd * uz]

    safe = jnp.maximum(index, 0)
    nhi = safe // 128
    nlo = safe - nhi * 128
    sub_h = lax.broadcasted_iota(jnp.int32, (HPAD, WIDTH), 0)
    sub_l = lax.broadcasted_iota(jnp.int32, (128, WIDTH), 0)
    half_i = lax.broadcasted_iota(jnp.int32, (128, WIDTH), 1) // SLOTS
    ehi = energy.astype(BF).astype(F32)
    elo = energy - ehi
    dvh = [x.astype(BF).astype(F32) for x in dv]
    dvl = [x - y for x, y in zip(dv, dvh)]
    for b in range(ROWS):
        cols = slice(b * WIDTH, (b + 1) * WIDTH)
        pick = sub_h == nhi[b:b + 1]
        parts = [jnp.where(pick, x[b:b + 1], 0.0) for x in dvh + dvl]
        parts.append(jnp.where(lax.broadcasted_iota(jnp.int32, (16, WIDTH), 0) == 0, ehi[b:b + 1],
                               jnp.where(lax.broadcasted_iota(jnp.int32, (16, WIDTH), 0) == 1, elo[b:b + 1], 0.0)))
        lhs[:, cols] = jnp.concatenate(parts, axis=0).astype(BF)
        low = (sub_l == nlo[b:b + 1]).astype(F32)
        cen = (sub_l == 2 * b + half_i).astype(F32)
        rhs[:, cols] = jnp.concatenate([low, cen], axis=0).astype(BF)
        placed_ref[pl.ds(slot_s[0, b], 1), :] = energy[b:b + 1]
    acc = mm_nt(lhs[...], rhs[...])
    for c in range(3):
        both = acc[c * HPAD:(c + 1) * HPAD] + acc[(3 + c) * HPAD:(4 + c) * HPAD]
        centre = jnp.sum(both[:, 128:256], axis=0, keepdims=True)
        ghost = jnp.where(sub_h == 4 * 4, jnp.broadcast_to(centre, (HPAD, 128)), 0.0) - both[:, 0:128]
        left_ref[12 * c:12 * c + 12] = ghost[0:12]
        mid_ref[12 * c:12 * c + 12] = ghost[12:24]
        right_ref[12 * c:12 * c + 12] = ghost[24:36]
    ae_ref[...] = acc[240:241, 128:192] + acc[241:242, 128:192]


def local_terms(tables, pair_neighbor, offload_slot, cpart, weights):
    vm = pl.BlockSpec(memory_space=pltpu.VMEM)
    sm = pl.BlockSpec(memory_space=pltpu.SMEM)
    operands = [pair_neighbor, offload_slot, pair_neighbor, *tables, cpart, *weights]
    specs = [sm, sm] + [vm] * (len(operands) - 2)
    return pl.pallas_call(
        kernel,
        out_shape=[
            jax.ShapeDtypeStruct((36, 128), F32),
            jax.ShapeDtypeStruct((36, 128), F32),
            jax.ShapeDtypeStruct((36, 128), F32),
            jax.ShapeDtypeStruct((1, 64), F32),
            jax.ShapeDtypeStruct((ROWS, WIDTH), F32),
        ],
        in_specs=specs,
        out_specs=[vm] * 5,
        scratch_shapes=[
            pltpu.VMEM((9 * ATOMS, 128), F32),
            pltpu.VMEM((ROWS * WIDTH, 128), F32),
            pltpu.VMEM((3, ROWS, WIDTH), F32),
            pltpu.VMEM((ROWS, 32, WIDTH), F32),
            pltpu.VMEM((ROWS, 32, WIDTH), F32),
            pltpu.VMEM((256, ROWS * WIDTH), BF),
            pltpu.VMEM((256, ROWS * WIDTH), BF),
        ],
        compiler_params=pltpu.CompilerParams(vmem_limit_bytes=56 * 1024 * 1024),
    )(*operands)


def prepare(atom_features, w_center, w_neigh, w_radial, w_env, w_latent, w_out):
    highest = lax.Precision.HIGHEST
    cpart = 0.5 * jnp.einsum("fc,fl->cl", atom_features[:, : 2 * ROWS], w_center, precision=highest)
    wn = 0.5 * w_neigh
    wn_hi, wn_lo = split2(wn)
    wr = 0.5 * w_radial
    wr_hi, wr_lo = split2(wr)
    z64 = jnp.zeros((64, 256), BF)
    win = jnp.concatenate(
        [wn_hi, z64, wn_hi, z64, wn_lo, z64, jnp.zeros((32, 256), BF), wr_hi, wr_hi, wr_lo, jnp.zeros((72, 256), BF)], axis=0)
    we0 = jnp.tile(w_env[0], (1, 4))
    we1 = jnp.tile(w_env[1], (1, 4))
    half = jnp.asarray(0.5, BF)
    pad = jnp.zeros((64, 256), BF)
    wl0 = jnp.concatenate([w_latent[0] * half, pad], axis=0)
    wl1 = jnp.concatenate([w_latent[1] * half, pad], axis=0)
    wl0t, wl1t = wl0.T, wl1.T
    lat0t = jnp.concatenate([wl0t[:, 0:256], we0.T], axis=0)
    lat1t = jnp.concatenate([wl1t[:, 0:256], we1.T[0:128]], axis=0)
    ones = jnp.ones((256, 1), BF)
    col = lambda j: jnp.pad(ones, ((0, 0), (j, 127 - j)))
    rad = jnp.pad(wr_hi.T, ((0, 0), (0, 120)))
    rad = jnp.concatenate([rad, col(8), col(9)], axis=0)
    return cpart, (win, we0, we1, wl0, wl1, wl0t[:, 256:512], wl1t[:, 256:512], lat0t, lat1t, w_out[None, :], rad)


def per_device(
    positions, atom_features, pair_neighbor, offload_slot,
    w_center, w_neigh, w_radial, w_env, w_latent, w_out,
):
    def shift(x, axis, step):
        n = lax.axis_size(axis)
        return lax.ppermute(x, axis, [(i, (i + step) % n) for i in range(n)])

    own = jnp.concatenate([atom_features, positions], axis=0)
    col = [shift(own, "gy", 1), own, shift(own, "gy", -1)]
    left = [None, shift(own, "gx", 1), None]
    right = [None, shift(own, "gx", -1), None]
    for oy in (0, 2):
        left[oy] = shift(col[oy], "gx", 1)
        right[oy] = shift(col[oy], "gx", -1)
    cpart, weights = prepare(atom_features, w_center, w_neigh, w_radial, w_env, w_latent, w_out)
    g_left, g_mid, g_right, ae, placed = local_terms(
        left + col + right, pair_neighbor, offload_slot, cpart, weights)
    from_left = shift(g_right, "gx", 1)
    from_right = shift(g_left, "gx", -1)
    peers = lax.axis_size("gy")
    pair_energy = lax.all_to_all(
        placed.reshape(peers, ROWS // peers, WIDTH), "gy", split_axis=0, concat_axis=0, tiled=True
    ).reshape(ROWS, WIDTH)
    total = (g_mid + from_left + from_right).reshape(3, 3, 4, 128)
    forces = total[:, 1] + shift(total[:, 2], "gy", 1) + shift(total[:, 0], "gy", -1)
    return forces.reshape(3, ATOMS), ae.reshape(2 * ROWS), pair_energy


def solution(mesh):
    spread = P(None, ("gx", "gy"))
    rows = P(("gx", "gy"), None)
    return jax.shard_map(
        per_device,
        mesh=mesh,
        in_specs=(spread, spread, rows, rows, P(), P(), P(), P(), P(), P()),
        out_specs=(spread, P(("gx", "gy")), rows),
        check_vma=False,
    )
```

time: 309 us -> 93.6 us (0.30); the launches traced: 304 us -> 93.2 us
  matrix products: 132 us -> 1.64 us
  local copies, waits for them, and re-layouts: 69.7 us -> 11.2 us
  other arithmetic: 43.2 us -> 3.06 us
  Pallas kernels: 0 us -> 36.5 us
  loops' own time: 19.7 us -> 0 us
  starting transfers between devices: 26 us -> 30.1 us
    dot_general x88 -> x1, matrix products: 132 us -> 1.64 us  [prepare(): jnp.einsum('fc,fl->cl', atom_features[:, :2 * ROWS], w_center, precision=...]
    gather x4 -> x0, local copies, waits for them, and re-layouts: 45.8 us -> none  [the longest x2 28.2 us: per_device(): vectors = pos_ext[:, neighbor_index] - pos_ext[:, 4 * atom_count + centres]]
    pallas_call x0 -> x1, Pallas kernels: none -> 36.5 us  [local_terms(): pl.pallas_call(kernel, out_shape=[jax.ShapeDtypeStruct((36, 128), F32), j...]
    scatter-add x2 -> x0, other arithmetic: 27 us -> none  [the longest x1 25 us: per_device(): grad_ext = jnp.zeros((3, 9 * atom_count), jnp.float32).at[:, neighbor_ind...]
    another operation x1 -> x0, loops' own time: 19.7 us -> none  [evaluate(): return lax.fori_loop(0, turn_count, step_group, initial)]
    ppermute x8 -> x12, waiting for transfers between devices: 8.47 us -> 1.72 us  [shift(): return lax.ppermute(x, axis, [(i, (i + step) % n) for i in range(n)])]
    ppermute x8 -> x12, starting transfers between devices: 16.1 us -> 21.9 us  [shift(): return lax.ppermute(x, axis, [(i, (i + step) % n) for i in range(n)])]
    while x20 -> x0, local copies, waits for them, and re-layouts: 4.8 us -> none
  transfers between devices with their start and end apart: 9 -> 13, of which waited for: 2 -> 2; matrix products, arithmetic and copies ran while one was open for 3% -> 11% of each run, Pallas kernels for 0% -> 0%
where the time goes in v1:
time: 93.6 us; the launch traced here: 93.2 us
  Pallas kernels  36.5 us (39%)
  starting transfers between devices  30.1 us (32%)
  local copies, waits for them, and re-layouts  11.2 us (12%)
  waiting for transfers between devices  9.62 us (10%)
  other arithmetic  3.06 us (3%)
  matrix products  1.64 us (2%)
  between operations  1 us (1%)
    pallas_call x1, Pallas kernels, local_terms(): pl.pallas_call(kernel, out_shape=[jax.ShapeDtypeStruct((36, 128), F32), j...  36.5 us
    ppermute x12, starting transfers between devices, shift(): return lax.ppermute(x, axis, [(i, (i + step) % n) for i in range(n)])  21.9 us
    all_to_all x1, starting transfers between devices, per_device(): lax.all_to_all(placed.reshape(peers, ROWS // peers, WIDTH), 'gy', split_a...  8.21 us
    all_to_all x1, waiting for transfers between devices, per_device(): lax.all_to_all(placed.reshape(peers, ROWS // peers, WIDTH), 'gy', split_a...  7.9 us
    unnamed x42, local copies, waits for them, and re-layouts  5.64 us
  transfers between devices with their start and end apart: 13, of which 2 were waited for; matrix products, arithmetic and copies ran while one was open for 11% of the time, Pallas kernels for 0%

profile of v1, /device:TPU:8, one launch (start us, length us, event | category | flops | bytes accessed | tf_op | source)
XLA Modules:
  0.0 93.2 jit_solution(41137721767064199)
XLA Ops:
  0.6 0.0 copy-start
  0.6 0.0 copy-start.14
  0.7 1.0 %constant_dynamic-update-slice_fusion.1 = f32[67,512]{1,0:T(8,128)S(1)} fusion(f32[64,512]{1,0:T(8,128)} %param.11), kind=kLoop, calls=%fused_computation.22 | loop fusion | bytes 262144
  1.6 0.0 copy-done.14
  1.6 2.0 %collective-permute-start = (f32[67,512]{1,0:T(8,128)S(1)}, f32[67,512]{1,0:T(8,128)S(1)}, u32[]{:S(2)}, u32[]{:S(2)}) collective-permute-start(f32[67,512]{1,0:T(8,128)S(1)} %constant_dynamic-update-slice_fusion.t4), channel_id=1, source_target_pairs={{0,1},{1,2},{2,3},{3,4},{4,5},{5,6},{6,7},{7,8},{8,9},{9,10},{10,1... | collective-permute-start | bytes 411656 | tf_op jit(solution)/shard_map/ppermute | solution.py:363
  3.6 3.9 %collective-permute-start.3 = (f32[67,512]{1,0:T(8,128)S(1)}, f32[67,512]{1,0:T(8,128)S(1)}, u32[]{:S(2)}, u32[]{:S(2)}) collective-permute-start(f32[67,512]{1,0:T(8,128)S(1)} %constant_dynamic-update-slice_fusion.t4), channel_id=1, source_target_pairs={{0,31},{1,0},{2,1},{3,2},{4,3},{5,4},{6,5},{7,6},{8,7},{9,8},{10,9... | collective-permute-start | bytes 411656 | tf_op jit(solution)/shard_map/ppermute | solution.py:363
  7.6 0.0 collective-permute-start.2
  7.6 3.0 %collective-permute-start.6 = (f32[67,512]{1,0:T(8,128)S(1)}, f32[67,512]{1,0:T(8,128)S(1)}, u32[]{:S(2)}, u32[]{:S(2)}) collective-permute-start(f32[67,512]{1,0:T(8,128)S(1)} %constant_dynamic-update-slice_fusion.t4), channel_id=1, source_target_pairs={{0,224},{32,0},{64,32},{96,64},{128,96},{160,128},{192,160},{224,1... | collective-permute-start | bytes 411656 | tf_op jit(solution)/shard_map/ppermute | solution.py:363
  10.5 1.1 %fusion.11 = (bf16[1,448,256]{2,1,0:T(8,128)(2,1)S(1)}, bf16[1,448,256]{2,1,0:T(8,128)(2,1)S(1)}) fusion(bf16[2,448,256]{2,1,0:T(8,128)(2,1)} %param.18), kind=kLoop, calls=%fused_computation.45 | loop fusion | bytes 917504 | tf_op jit(solution)/shard_map/slice | solution.py:346
  11.6 0.1 copy.51
  11.8 0.1 copy.50
  12.0 0.1 pad_bitcast_fusion
  12.0 0.0 copy-start.12
  12.0 0.7 fusion.13
  12.7 0.2 copy-done.12
  12.9 0.7 fusion.12
  13.6 0.0 copy-start.1
  13.6 0.8 copy-done.1
  14.5 0.0 copy-start.13
  14.5 0.7 copy-done.13
  15.2 1.6 %convolution_multiply_fusion.cpart = f32[64,256]{1,0:T(8,128)} fusion(f32[64,256]{1,0:T(8,128)S(1)} %copy-done, f32[64,512]{1,0:T(8,128)} %param.11), kind=kOutput, calls=%fused_computation | convolution fusion | flops 12599296 | bytes 163840 | tf_op jit(solution)/shard_map/fc,fl->cl/dot_general | solution.py:333
  16.8 0.7 pad_maximum_fusion.1.lat1t_ref
  17.5 0.1 copy.42
  17.7 0.8 fusion.5.rad_ref
  18.5 0.0 collective-permute-done.t3
  18.5 0.0 collective-permute-start.1
  18.5 3.0 %collective-permute-start.5 = (f32[67,512]{1,0:T(8,128)S(1)}, f32[67,512]{1,0:T(8,128)S(1)}, u32[]{:S(2)}, u32[]{:S(2)}) collective-permute-start(f32[67,512]{1,0:T(8,128)S(1)} %collective-permute-done.t3), channel_id=1, source_target_pairs={{0,224},{32,0},{64,32},{96,64},{128,96},{160,128},{192,160},{224,1... | collective-permute-start | bytes 411656 | tf_op jit(solution)/shard_map/ppermute | solution.py:363
  21.4 0.0 collective-permute-done.3.t5
  21.4 0.0 collective-permute-start.4
  21.4 0.0 collective-permute-done.2.t1
  21.5 2.9 %collective-permute-start.7 = (f32[67,512]{1,0:T(8,128)S(1)}, f32[67,512]{1,0:T(8,128)S(1)}, u32[]{:S(2)}, u32[]{:S(2)}) collective-permute-start(f32[67,512]{1,0:T(8,128)S(1)} %collective-permute-done.3.t5), channel_id=1, source_target_pairs={{0,224},{32,0},{64,32},{96,64},{128,96},{160,128},{192,160},{224,1... | collective-permute-start | bytes 411656 | tf_op jit(solution)/shard_map/ppermute | solution.py:363
  24.4 0.1 copy.56
  24.6 0.1 copy.57
  24.7 0.4 copy-done.3
  25.1 0.7 concatenate.23.clone.wl0_ref
  25.8 0.7 concatenate.24.clone.wl1_ref
  26.5 0.8 copy.43.we0_ref
  27.3 0.7 copy.44.we1_ref
  28.0 0.7 pad_maximum_fusion.lat0t_ref
  28.8 0.0 collective-permute-done.6.t7
  28.8 0.0 collective-permute-done.1.t0
  28.8 0.0 collective-permute-done.4.t2
  28.8 0.0 copy-start.10
  28.8 0.0 collective-permute-done.5.t6
  28.8 0.0 collective-permute-done.7.t8
  28.9 0.6 copy-done.7
  29.4 0.1 copy-done.8
  29.5 0.1 copy-done.10
  29.6 0.1 copy-done.9
  29.6 0.1 copy-done.11
  29.7 36.5 %shard_map.121 = (f32[36,128]{1,0:T(8,128)}, f32[36,128]{1,0:T(8,128)}, f32[36,128]{1,0:T(8,128)}, f32[1,64]{1,0:T(1,128)}, f32[32,128]{1,0:T(8,128)}) custom-call(s32[32,128]{1,0:T(8,128)} %idx_v.1, s32[1,32]{1,0:T(1,128)} %slot_s.1, s32[32,128]{1,0:T(8,128)} %idx_v.1, f32[67,512]{1,0:T(8,128)} %copy-done.8, f32[67,512]{1,0:T(8,128)} %copy-done.6, ...), custom_call_target="tpu_custom_call" | custom-call | tf_op jit(solution)/shard_map/pallas_call | solution.py:307
  66.2 0.0 collective-permute-start.8
  66.2 2.9 %collective-permute-start.9 = (f32[36,128]{1,0:T(8,128)}, f32[36,128]{1,0:T(8,128)S(1)}, u32[]{:S(2)}, u32[]{:S(2)}) collective-permute-start(f32[36,128]{1,0:T(8,128)} %get-tuple-element.10), channel_id=1, source_target_pairs={{0,224},{32,0},{64,32},{96,64},{128,96},{160,128},{192,160},{224,1... | collective-permute-start | bytes 55304 | tf_op jit(solution)/shard_map/ppermute | solution.py:363
  69.2 1.7 %collective-permute-done.8 = f32[36,128]{1,0:T(8,128)S(1)} collective-permute-done((f32[36,128]{1,0:T(8,128)}, f32[36,128]{1,0:T(8,128)S(1)}, u32[]{:S(2)}, u32[]{:S(2)}) %collective-permute-start.8) | collective-permute-done | bytes 18464 | tf_op jit(solution)/shard_map/ppermute | solution.py:363
  70.9 0.0 collective-permute-done.9
  70.9 0.7 add_add_fusion
  71.6 0.1 collective-permute-start.10
  71.7 4.1 %collective-permute-start.11 = (f32[3,4,128]{2,1,0:T(4,128)S(1)}, f32[3,4,128]{2,1,0:T(4,128)S(1)}, u32[]{:S(2)}, u32[]{:S(2)}) collective-permute-start(f32[3,4,128]{2,1,0:T(4,128)S(1)} %get-tuple-element.24), channel_id=1, source_target_pairs={{0,31},{1,0},{2,1},{3,2},{4,3},{5,4},{6,5},{7,6},{8,7},{9,8},{10,9... | collective-permute-start | bytes 18440 | tf_op jit(solution)/shard_map/ppermute | solution.py:363
  75.8 8.2 %all-to-all-start = ((f32[32,1,128]{2,1,0:T(1,128)}), f32[32,1,128]{2,1,0:T(1,128)S(1)}, u32[]{:S(2)}, u32[]{:S(2)}) async-start(f32[32,1,128]{2,1,0:T(1,128)} %bitcast.17), calls=%async_computation | async-start | bytes 32768 | tf_op jit(solution)/shard_map/all_to_all | solution.py:378
  84.1 0.0 collective-permute-done.10
  84.1 0.0 collective-permute-done.11
  84.1 0.6 copy.58
  84.7 7.9 %all-to-all-done = f32[32,1,128]{2,1,0:T(1,128)S(1)} async-done(((f32[32,1,128]{2,1,0:T(1,128)}), f32[32,1,128]{2,1,0:T(1,128)S(1)}, u32[]{:S(2)}, u32[]{:S(2)}) %all-to-all-start) | async-done | bytes 16416 | tf_op jit(solution)/shard_map/all_to_all | solution.py:378
  92.6 0.6 copy.71
  (36 shorter events, 0.2 us)
Async XLA Ops:
  0.6 14.6 %copy-start = (f32[64,256]{1,0:T(8,128)S(1)}, f32[64,256]{1,0:T(8,128)}, u32[]{:S(2)}) copy-start(f32[64,256]{1,0:T(8,128)} %param.14) | copy-start | bytes 196612
  0.6 1.0 %copy-start.14 = (f32[3,512]{1,0:T(4,128)S(1)}, f32[3,512]{1,0:T(4,128)}, u32[]{:S(2)}) copy-start(f32[3,512]{1,0:T(4,128)} %param.10) | copy-start | bytes 18436
  1.6 10.0 %copy-start.2 = (f32[67,512]{1,0:T(8,128)}, f32[67,512]{1,0:T(8,128)S(1)}, u32[]{:S(2)}) copy-start(f32[67,512]{1,0:T(8,128)S(1)} %constant_dynamic-update-slice_fusion.t4) | copy-start | bytes 411652
  1.6 16.8 %collective-permute-start = (f32[67,512]{1,0:T(8,128)S(1)}, f32[67,512]{1,0:T(8,128)S(1)}, u32[]{:S(2)}, u32[]{:S(2)}) collective-permute-start(f32[67,512]{1,0:T(8,128)S(1)} %constant_dynamic-update-slice_fusion.t4), channel_id=1, source_target_pairs={{0,1},{1,2},{2,3},{3,4},{4,5},{5,6},{6,7},{7,8},{8,9},{9,10},{10,1... | collective-permute-start | bytes 411656 | tf_op jit(solution)/shard_map/ppermute | solution.py:363
  3.6 17.8 %collective-permute-start.3 = (f32[67,512]{1,0:T(8,128)S(1)}, f32[67,512]{1,0:T(8,128)S(1)}, u32[]{:S(2)}, u32[]{:S(2)}) collective-permute-start(f32[67,512]{1,0:T(8,128)S(1)} %constant_dynamic-update-slice_fusion.t4), channel_id=1, source_target_pairs={{0,31},{1,0},{2,1},{3,2},{4,3},{5,4},{6,5},{7,6},{8,7},{9,8},{10,9... | collective-permute-start | bytes 411656 | tf_op jit(solution)/shard_map/ppermute | solution.py:363
  7.6 13.9 %collective-permute-start.2 = (f32[67,512]{1,0:T(8,128)S(1)}, f32[67,512]{1,0:T(8,128)S(1)}, u32[]{:S(2)}, u32[]{:S(2)}) collective-permute-start(f32[67,512]{1,0:T(8,128)S(1)} %constant_dynamic-update-slice_fusion.t4), channel_id=1, source_target_pairs={{0,32},{32,64},{64,96},{96,128},{128,160},{160,192},{192,224},{224... | collective-permute-start | bytes 411656 | tf_op jit(solution)/shard_map/ppermute | solution.py:363
  7.6 21.2 %collective-permute-start.6 = (f32[67,512]{1,0:T(8,128)S(1)}, f32[67,512]{1,0:T(8,128)S(1)}, u32[]{:S(2)}, u32[]{:S(2)}) collective-permute-start(f32[67,512]{1,0:T(8,128)S(1)} %constant_dynamic-update-slice_fusion.t4), channel_id=1, source_target_pairs={{0,224},{32,0},{64,32},{96,64},{128,96},{160,128},{192,160},{224,1... | collective-permute-start | bytes 411656 | tf_op jit(solution)/shard_map/ppermute | solution.py:363
  12.0 0.8 copy-start.12
  13.6 0.8 copy-start.1
  14.5 0.7 copy-start.13
  18.5 6.1 %copy-start.4 = (f32[67,512]{1,0:T(8,128)}, f32[67,512]{1,0:T(8,128)S(1)}, u32[]{:S(2)}) copy-start(f32[67,512]{1,0:T(8,128)S(1)} %collective-permute-done.t3) | copy-start | bytes 411652
  18.5 10.3 %collective-permute-start.1 = (f32[67,512]{1,0:T(8,128)S(1)}, f32[67,512]{1,0:T(8,128)S(1)}, u32[]{:S(2)}, u32[]{:S(2)}) collective-permute-start(f32[67,512]{1,0:T(8,128)S(1)} %collective-permute-done.t3), channel_id=1, source_target_pairs={{0,32},{32,64},{64,96},{96,128},{128,160},{160,192},{192,224},{224... | collective-permute-start | bytes 411656 | tf_op jit(solution)/shard_map/ppermute | solution.py:363
  18.5 10.3 %collective-permute-start.5 = (f32[67,512]{1,0:T(8,128)S(1)}, f32[67,512]{1,0:T(8,128)S(1)}, u32[]{:S(2)}, u32[]{:S(2)}) collective-permute-start(f32[67,512]{1,0:T(8,128)S(1)} %collective-permute-done.t3), channel_id=1, source_target_pairs={{0,224},{32,0},{64,32},{96,64},{128,96},{160,128},{192,160},{224,1... | collective-permute-start | bytes 411656 | tf_op jit(solution)/shard_map/ppermute | solution.py:363
  21.4 3.1 %copy-start.5 = (f32[67,512]{1,0:T(8,128)}, f32[67,512]{1,0:T(8,128)S(1)}, u32[]{:S(2)}) copy-start(f32[67,512]{1,0:T(8,128)S(1)} %collective-permute-done.3.t5) | copy-start | bytes 411652
  21.4 7.4 %collective-permute-start.4 = (f32[67,512]{1,0:T(8,128)S(1)}, f32[67,512]{1,0:T(8,128)S(1)}, u32[]{:S(2)}, u32[]{:S(2)}) collective-permute-start(f32[67,512]{1,0:T(8,128)S(1)} %collective-permute-done.3.t5), channel_id=1, source_target_pairs={{0,32},{32,64},{64,96},{96,128},{128,160},{160,192},{192,224},{224... | collective-permute-start | bytes 411656 | tf_op jit(solution)/shard_map/ppermute | solution.py:363
  21.4 3.1 %copy-start.6 = (f32[67,512]{1,0:T(8,128)}, f32[67,512]{1,0:T(8,128)S(1)}, u32[]{:S(2)}) copy-start(f32[67,512]{1,0:T(8,128)S(1)} %collective-permute-done.2.t1) | copy-start | bytes 411652
  21.5 7.4 %collective-permute-start.7 = (f32[67,512]{1,0:T(8,128)S(1)}, f32[67,512]{1,0:T(8,128)S(1)}, u32[]{:S(2)}, u32[]{:S(2)}) collective-permute-start(f32[67,512]{1,0:T(8,128)S(1)} %collective-permute-done.3.t5), channel_id=1, source_target_pairs={{0,224},{32,0},{64,32},{96,64},{128,96},{160,128},{192,160},{224,1... | collective-permute-start | bytes 411656 | tf_op jit(solution)/shard_map/ppermute | solution.py:363
  24.4 0.7 copy-start.3
  28.8 0.7 copy-start.7
  28.8 0.7 copy-start.8
  28.8 0.7 copy-start.10
  28.8 0.8 copy-start.9
  28.8 0.8 copy-start.11
  66.2 4.6 %collective-permute-start.8 = (f32[36,128]{1,0:T(8,128)}, f32[36,128]{1,0:T(8,128)S(1)}, u32[]{:S(2)}, u32[]{:S(2)}) collective-permute-start(f32[36,128]{1,0:T(8,128)} %get-tuple-element.9), channel_id=1, source_target_pairs={{0,32},{32,64},{64,96},{96,128},{128,160},{160,192},{192,224},{224... | collective-permute-start | bytes 55304 | tf_op jit(solution)/shard_map/ppermute | solution.py:363
  66.2 4.6 %collective-permute-start.9 = (f32[36,128]{1,0:T(8,128)}, f32[36,128]{1,0:T(8,128)S(1)}, u32[]{:S(2)}, u32[]{:S(2)}) collective-permute-start(f32[36,128]{1,0:T(8,128)} %get-tuple-element.10), channel_id=1, source_target_pairs={{0,224},{32,0},{64,32},{96,64},{128,96},{160,128},{192,160},{224,1... | collective-permute-start | bytes 55304 | tf_op jit(solution)/shard_map/ppermute | solution.py:363
  71.6 12.4 %collective-permute-start.10 = (f32[3,4,128]{2,1,0:T(4,128)S(1)}, f32[3,4,128]{2,1,0:T(4,128)S(1)}, u32[]{:S(2)}, u32[]{:S(2)}) collective-permute-start(f32[3,4,128]{2,1,0:T(4,128)S(1)} %get-tuple-element.23), channel_id=1, source_target_pairs={{0,1},{1,2},{2,3},{3,4},{4,5},{5,6},{6,7},{7,8},{8,9},{9,10},{10,1... | collective-permute-start | bytes 18440 | tf_op jit(solution)/shard_map/ppermute | solution.py:363
  71.7 12.4 %collective-permute-start.11 = (f32[3,4,128]{2,1,0:T(4,128)S(1)}, f32[3,4,128]{2,1,0:T(4,128)S(1)}, u32[]{:S(2)}, u32[]{:S(2)}) collective-permute-start(f32[3,4,128]{2,1,0:T(4,128)S(1)} %get-tuple-element.24), channel_id=1, source_target_pairs={{0,31},{1,0},{2,1},{3,2},{4,3},{5,4},{6,5},{7,6},{8,7},{9,8},{10,9... | collective-permute-start | bytes 18440 | tf_op jit(solution)/shard_map/ppermute | solution.py:363
  75.8 16.8 %all-to-all-start = ((f32[32,1,128]{2,1,0:T(1,128)}), f32[32,1,128]{2,1,0:T(1,128)S(1)}, u32[]{:S(2)}, u32[]{:S(2)}) async-start(f32[32,1,128]{2,1,0:T(1,128)} %bitcast.17), calls=%async_computation | async-start | bytes 32768 | tf_op jit(solution)/shard_map/all_to_all | solution.py:378

commit v2 on v1

--- a/solution.py
+++ b/solution.py
@@ -22,6 +22,7 @@
 M = NB * WIDTH
 NT = (((1,), (1,)), ((), ()))
 HPAD = 40
+LEAD = 8
 
 
 def mm(a, b):
@@ -41,15 +42,36 @@
     return hi, (x - hi.astype(F32)).astype(BF)
 
 
+def geometry(vx, vy, vz, index):
+    valid = (index >= 0).astype(F32)
+    dist = jnp.sqrt(vx * vx + vy * vy + vz * vz + SOFTEN)
+    inv = 1.0 / dist
+    scaled = dist * (1.0 / CUTOFF)
+    poly = 1.0 - scaled * scaled
+    env = valid * (poly * poly)
+    theta = math.pi * scaled
+    sins, coss = [jnp.sin(theta)], [jnp.cos(theta)]
+    twice = 2.0 * coss[0]
+    sprev, cprev = jnp.zeros_like(inv), jnp.ones_like(inv)
+    for _ in range(7):
+        snext = twice * sins[-1] - sprev
+        cnext = twice * coss[-1] - cprev
+        sprev, cprev = sins[-1], coss[-1]
+        sins.append(snext)
+        coss.append(cnext)
+    return vx * inv, vy * inv, vz * inv, inv, valid, poly, scaled, env, sins, coss
+
+
 def kernel(
     idx_s, slot_s, idx_v, t0, t1, t2, t3, t4, t5, t6, t7, t8, cpart, win_ref,
     we0_ref, we1_ref, wl0_ref, wl1_ref, wl0t_ref, wl1t_ref, lat0t_ref, lat1t_ref,
-    wout_ref, rad_ref,
-    left_ref, mid_ref, right_ref, ae_ref, placed_ref,
-    table, gbuf, pos, geo, bgeo, lhs, rhs,
+    rad_ref, wout_ref,
+    terms_ref, placed_ref,
+    table, gbuf, pos, geo, bgeo,
 ):
     tables = (t0, t1, t2, t3, t4, t5, t6, t7, t8)
     feats = 64
+    table[0:LEAD, :] = jnp.zeros((LEAD, 128), F32)
     for o in range(9):
         ref = tables[o]
         shift = jnp.concatenate(
@@ -60,62 +82,39 @@
             block = jnp.concatenate(
                 [ref[0:feats, q * 128:(q + 1) * 128], posr[:, q * 128:(q + 1) * 128],
                  jnp.zeros((61, 128), F32)], axis=0)
-            table[pl.ds(o * ATOMS + q * 128, 128), :] = block.T
-
-    def gather_row(b, carry):
-        base = b * WIDTH
-        for t in range(WIDTH):
-            n = jnp.maximum(idx_s[b, t], 0)
-            gbuf[pl.ds(base + t, 1), :] = table[pl.ds(n, 1), :]
-        gt = gbuf[pl.ds(pl.multiple_of(base, WIDTH), WIDTH), :].T
+            table[pl.ds(LEAD + o * ATOMS + q * 128, 128), :] = block.T
+
+    lane = lax.broadcasted_iota(jnp.int32, (NB, WIDTH), 1)
+    row_i = lax.broadcasted_iota(jnp.int32, (NB, WIDTH), 0)
+    own_t = table[pl.ds(LEAD + 4 * ATOMS, 128), :].T
+
+    def stage(i):
+        start = pl.multiple_of(i * M, M)
+        for b in range(NB):
+            for t in range(WIDTH):
+                gbuf[pl.ds(start + (b * WIDTH + t), 1), :] = table[pl.ds(idx_s[i * NB + b, t] + LEAD, 1), :]
+        turned = [gbuf[pl.ds(start + b * WIDTH, WIDTH), :].T for b in range(NB)]
+        some = pl.ds(pl.multiple_of(i * NB, NB), NB)
+        vec = []
         for c in range(3):
-            pos[c, pl.ds(b, 1), :] = gt[feats + c:feats + c + 1, :]
-        return carry
-
-    lax.fori_loop(0, ROWS, gather_row, 0)
-
-    lane = lax.broadcasted_iota(jnp.int32, (ROWS, WIDTH), 1)
-    own = table[pl.ds(4 * ATOMS, 128), :]
-    own_t = own.T
-    row_i = lax.broadcasted_iota(jnp.int32, (ROWS, WIDTH), 0)
-    vec = []
-    for c in range(3):
-        line = jnp.broadcast_to(own_t[feats + c:feats + c + 1, :], (ROWS, WIDTH))
-        first = jnp.sum(jnp.where(lane == 2 * row_i, line, 0.0), axis=1, keepdims=True)
-        second = jnp.sum(jnp.where(lane == 2 * row_i + 1, line, 0.0), axis=1, keepdims=True)
-        vec.append(pos[c] - jnp.where(lane < SLOTS, first, second))
-    vx, vy, vz = vec
-    index = idx_v[...]
-    valid = (index >= 0).astype(F32)
-    dist = jnp.sqrt(vx * vx + vy * vy + vz * vz + SOFTEN)
-    inv = 1.0 / dist
-    ux, uy, uz = vx * inv, vy * inv, vz * inv
-    scaled = dist * (1.0 / CUTOFF)
-    poly = 1.0 - scaled * scaled
-    env = valid * (poly * poly)
-    theta = math.pi * scaled
-    sin1, cos1 = jnp.sin(theta), jnp.cos(theta)
-    sins, coss = [sin1], [cos1]
-    sprev, cprev = jnp.zeros_like(sin1), jnp.ones_like(cos1)
-    for _ in range(7):
-        snext = 2.0 * cos1 * sins[-1] - sprev
-        cnext = 2.0 * cos1 * coss[-1] - cprev
-        sprev, cprev = sins[-1], coss[-1]
-        sins.append(snext)
-        coss.append(cnext)
-    sph = [
-        jnp.ones_like(ux), R3 * ux, R3 * uy, R3 * uz, R15 * ux * uy, R15 * uy * uz,
-        0.5 * R5 * (3.0 * uz * uz - 1.0), R15 * ux * uz, 0.5 * R15 * (ux * ux - uy * uy),
-    ]
-    zero = jnp.zeros_like(ux)
-    rows = sph + [zero] * 7
-    for s in sins:
-        rows.append(s * inv)
-    rows.append(env)
-    rows += [zero] * 7
-    for q in range(len(rows)):
-        for b in range(ROWS):
-            geo[b, q:q + 1, :] = rows[q][b:b + 1, :]
+            end = jnp.concatenate([x[feats + c:feats + c + 1] for x in turned], axis=0)
+            line = jnp.broadcast_to(own_t[feats + c:feats + c + 1, :], (NB, WIDTH))
+            at = 2 * (row_i + i * NB)
+            first = jnp.sum(jnp.where(lane == at, line, 0.0), axis=1, keepdims=True)
+            second = jnp.sum(jnp.where(lane == at + 1, line, 0.0), axis=1, keepdims=True)
+            vec.append(end - jnp.where(lane < SLOTS, first, second))
+            pos[c, some, :] = vec[-1]
+        ux, uy, uz, inv, _, _, _, env, sins, _ = geometry(*vec, idx_v[some, :])
+        zero = jnp.zeros_like(ux)
+        rows = [
+            jnp.ones_like(ux), R3 * ux, R3 * uy, R3 * uz, R15 * ux * uy, R15 * uy * uz,
+            0.5 * R5 * (3.0 * uz * uz - 1.0), R15 * ux * uz, 0.5 * R15 * (ux * ux - uy * uy),
+        ] + [zero] * 7 + [x * inv for x in sins] + [env] + [zero] * 7
+        for q in range(len(rows)):
+            for b in range(NB):
+                geo[i * NB + b, q:q + 1, :] = rows[q][b:b + 1, :]
+
+    stage(0)
 
     lane_b = lax.broadcasted_iota(jnp.int32, (16, WIDTH), 1)
     half0 = (lane_b < SLOTS).astype(F32)
@@ -167,6 +166,7 @@
             st.append(jnp.concatenate([s0, s1], axis=0).astype(BF))
             cadd.append(jnp.broadcast_to(centres[2 * b:2 * b + 1], (SLOTS, 256)))
             cadd.append(jnp.broadcast_to(centres[2 * b + 1:2 * b + 2], (SLOTS, 256)))
+        stage(jnp.minimum(i + 1, ROWS // NB - 1))
         trans = jnp.concatenate(tr, axis=0)
         env1 = jnp.broadcast_to(trans[:, 56:57], (M, 128))
         env2 = jnp.concatenate([env1, env1], axis=1)
@@ -252,6 +252,7 @@
 
     lax.fori_loop(0, ROWS // NB, chunk, 0)
 
+    ux, uy, uz, inv, valid, poly, scaled, env, sins, coss = geometry(pos[0], pos[1], pos[2], idx_v[...])
     back = []
     for q in range(26):
         back.append(jnp.concatenate([bgeo[b, q:q + 1, :] for b in range(ROWS)], axis=0))
@@ -267,27 +268,32 @@
     dd = dd - (dux * ux + duy * uy + duz * uz) * inv
     dv = [dux * inv + dd * ux, duy * inv + dd * uy, duz * inv + dd * uz]
 
-    safe = jnp.maximum(index, 0)
+    for c in range(3):
+        terms_ref[c] = dv[c]
+    terms_ref[3] = energy
+    for b in range(ROWS):
+        placed_ref[pl.ds(slot_s[0, b], 1), :] = energy[b:b + 1]
+
+
+def scatter_kernel(idx_v, terms_ref, left_ref, mid_ref, right_ref, ae_ref, lhs, rhs):
+    safe = jnp.maximum(idx_v[...], 0)
     nhi = safe // 128
     nlo = safe - nhi * 128
     sub_h = lax.broadcasted_iota(jnp.int32, (HPAD, WIDTH), 0)
     sub_l = lax.broadcasted_iota(jnp.int32, (128, WIDTH), 0)
+    sub_e = lax.broadcasted_iota(jnp.int32, (16, WIDTH), 0)
     half_i = lax.broadcasted_iota(jnp.int32, (128, WIDTH), 1) // SLOTS
-    ehi = energy.astype(BF).astype(F32)
-    elo = energy - ehi
-    dvh = [x.astype(BF).astype(F32) for x in dv]
-    dvl = [x - y for x, y in zip(dv, dvh)]
+    high = [terms_ref[c].astype(BF).astype(F32) for c in range(4)]
+    low = [terms_ref[c] - high[c] for c in range(4)]
     for b in range(ROWS):
         cols = slice(b * WIDTH, (b + 1) * WIDTH)
         pick = sub_h == nhi[b:b + 1]
-        parts = [jnp.where(pick, x[b:b + 1], 0.0) for x in dvh + dvl]
-        parts.append(jnp.where(lax.broadcasted_iota(jnp.int32, (16, WIDTH), 0) == 0, ehi[b:b + 1],
-                               jnp.where(lax.broadcasted_iota(jnp.int32, (16, WIDTH), 0) == 1, elo[b:b + 1], 0.0)))
+        parts = [jnp.where(pick, x[b:b + 1], 0.0) for x in high[:3] + low[:3]]
+        parts.append(jnp.where(sub_e == 0, high[3][b:b + 1], jnp.where(sub_e == 1, low[3][b:b + 1], 0.0)))
         lhs[:, cols] = jnp.concatenate(parts, axis=0).astype(BF)
-        low = (sub_l == nlo[b:b + 1]).astype(F32)
-        cen = (sub_l == 2 * b + half_i).astype(F32)
-        rhs[:, cols] = jnp.concatenate([low, cen], axis=0).astype(BF)
-        placed_ref[pl.ds(slot_s[0, b], 1), :] = energy[b:b + 1]
+        one_lo = (sub_l == nlo[b:b + 1]).astype(F32)
+        one_c = (sub_l == 2 * b + half_i).astype(F32)
+        rhs[:, cols] = jnp.concatenate([one_lo, one_c], axis=0).astype(BF)
     acc = mm_nt(lhs[...], rhs[...])
     for c in range(3):
         both = acc[c * HPAD:(c + 1) * HPAD] + acc[(3 + c) * HPAD:(4 + c) * HPAD]
@@ -304,54 +310,90 @@
     sm = pl.BlockSpec(memory_space=pltpu.SMEM)
     operands = [pair_neighbor, offload_slot, pair_neighbor, *tables, cpart, *weights]
     specs = [sm, sm] + [vm] * (len(operands) - 2)
-    return pl.pallas_call(
+    terms, placed = pl.pallas_call(
         kernel,
         out_shape=[
-            jax.ShapeDtypeStruct((36, 128), F32),
-            jax.ShapeDtypeStruct((36, 128), F32),
-            jax.ShapeDtypeStruct((36, 128), F32),
-            jax.ShapeDtypeStruct((1, 64), F32),
+            jax.ShapeDtypeStruct((4, ROWS, WIDTH), F32),
             jax.ShapeDtypeStruct((ROWS, WIDTH), F32),
         ],
         in_specs=specs,
-        out_specs=[vm] * 5,
+        out_specs=[vm] * 2,
         scratch_shapes=[
-            pltpu.VMEM((9 * ATOMS, 128), F32),
+            pltpu.VMEM((LEAD + 9 * ATOMS, 128), F32),
             pltpu.VMEM((ROWS * WIDTH, 128), F32),
             pltpu.VMEM((3, ROWS, WIDTH), F32),
             pltpu.VMEM((ROWS, 32, WIDTH), F32),
             pltpu.VMEM((ROWS, 32, WIDTH), F32),
-            pltpu.VMEM((256, ROWS * WIDTH), BF),
-            pltpu.VMEM((256, ROWS * WIDTH), BF),
         ],
         compiler_params=pltpu.CompilerParams(vmem_limit_bytes=56 * 1024 * 1024),
+        cost_estimate=pl.CostEstimate(flops=20_000_000_000, bytes_accessed=4_000_000, transcendentals=0),
     )(*operands)
+    ghost = jax.ShapeDtypeStruct((36, 128), F32)
+    left, mid, right, ae = pl.pallas_call(
+        scatter_kernel,
+        out_shape=[ghost, ghost, ghost, jax.ShapeDtypeStruct((1, 2 * ROWS), F32)],
+        in_specs=[vm] * 2,
+        out_specs=[vm] * 4,
+        scratch_shapes=[pltpu.VMEM((256, ROWS * WIDTH), BF)] * 2,
+        compiler_params=pltpu.CompilerParams(vmem_limit_bytes=24 * 1024 * 1024),
+        cost_estimate=pl.CostEstimate(flops=5_000_000_000, bytes_accessed=1_000_000, transcendentals=0),
+    )(pair_neighbor, terms)
+    return left, mid, right, ae, placed
+
+
+def prepare_kernel(
+    feat, wc_ref, wn_ref, wr_ref, we_ref, wl_ref,
+    cpart, win, we0, we1, wl0, wl1, wl0t, wl1t, lat0t, lat1t, rad,
+):
+    own = feat[:, 0:128].T[0:2 * ROWS]
+    fhi, flo = split2(own)
+    chi, clo = split2(0.5 * wc_ref[...])
+    cpart[...] = mm(fhi, chi) + mm(flo, chi) + mm(fhi, clo)
+    nhi, nlo = split2(0.5 * wn_ref[...])
+    rhi, rlo = split2(0.5 * wr_ref[...])
+    rhi, rlo = rhi.astype(F32), rlo.astype(F32)
+    pad = jnp.zeros((64, 256), BF)
+    radial = jnp.concatenate(
+        [jnp.zeros((32, 256), F32), rhi, rhi, rlo, jnp.zeros((72, 256), F32)], axis=0)
+    win[...] = jnp.concatenate([nhi, pad, nhi, pad, nlo, pad, radial.astype(BF)], axis=0)
+    rt = jnp.concatenate([rhi, jnp.zeros((120, 256), F32)], axis=0).T
+    lanes = lax.broadcasted_iota(jnp.int32, (256, 128), 1)
+    rad[0:256] = rt.astype(BF)
+    rad[256:512] = (lanes == 8).astype(F32).astype(BF)
+    rad[512:768] = (lanes == 9).astype(F32).astype(BF)
+    tile = (
+        lax.broadcasted_iota(jnp.int32, (64, 256), 0)
+        == lax.broadcasted_iota(jnp.int32, (64, 256), 1) % 64
+    ).astype(F32).astype(BF)
+    for layer, (we, wl, wlt, latt) in enumerate(
+        ((we0, wl0, wl0t, lat0t), (we1, wl1, wl1t, lat1t))
+    ):
+        tiled = mm(we_ref[layer], tile)
+        we[...] = tiled.astype(BF)
+        halved = jnp.concatenate(
+            [0.5 * wl_ref[layer].astype(F32), jnp.zeros((64, 256), F32)], axis=0)
+        wl[...] = halved.astype(BF)
+        wlt[...] = halved[256:512].T.astype(BF)
+        latt[0:256] = halved[0:256].T.astype(BF)
+        latt[256:] = tiled.T[0:latt.shape[0] - 256].astype(BF)
 
 
 def prepare(atom_features, w_center, w_neigh, w_radial, w_env, w_latent, w_out):
-    highest = lax.Precision.HIGHEST
-    cpart = 0.5 * jnp.einsum("fc,fl->cl", atom_features[:, : 2 * ROWS], w_center, precision=highest)
-    wn = 0.5 * w_neigh
-    wn_hi, wn_lo = split2(wn)
-    wr = 0.5 * w_radial
-    wr_hi, wr_lo = split2(wr)
-    z64 = jnp.zeros((64, 256), BF)
-    win = jnp.concatenate(
-        [wn_hi, z64, wn_hi, z64, wn_lo, z64, jnp.zeros((32, 256), BF), wr_hi, wr_hi, wr_lo, jnp.zeros((72, 256), BF)], axis=0)
-    we0 = jnp.tile(w_env[0], (1, 4))
-    we1 = jnp.tile(w_env[1], (1, 4))
-    half = jnp.asarray(0.5, BF)
-    pad = jnp.zeros((64, 256), BF)
-    wl0 = jnp.concatenate([w_latent[0] * half, pad], axis=0)
-    wl1 = jnp.concatenate([w_latent[1] * half, pad], axis=0)
-    wl0t, wl1t = wl0.T, wl1.T
-    lat0t = jnp.concatenate([wl0t[:, 0:256], we0.T], axis=0)
-    lat1t = jnp.concatenate([wl1t[:, 0:256], we1.T[0:128]], axis=0)
-    ones = jnp.ones((256, 1), BF)
-    col = lambda j: jnp.pad(ones, ((0, 0), (j, 127 - j)))
-    rad = jnp.pad(wr_hi.T, ((0, 0), (0, 120)))
-    rad = jnp.concatenate([rad, col(8), col(9)], axis=0)
-    return cpart, (win, we0, we1, wl0, wl1, wl0t[:, 256:512], wl1t[:, 256:512], lat0t, lat1t, w_out[None, :], rad)
+    vm = pl.BlockSpec(memory_space=pltpu.VMEM)
+    sd = jax.ShapeDtypeStruct
+    sq = sd((256, 256), BF)
+    shapes = [
+        sd((2 * ROWS, 256), F32), sd((512, 256), BF), sq, sq, sd((512, 256), BF),
+        sd((512, 256), BF), sq, sq, sd((512, 256), BF), sd((384, 256), BF), sd((768, 128), BF),
+    ]
+    cpart, *weights = pl.pallas_call(
+        prepare_kernel,
+        out_shape=shapes,
+        in_specs=[vm] * 6,
+        out_specs=[vm] * len(shapes),
+        cost_estimate=pl.CostEstimate(flops=80_000_000, bytes_accessed=4_000_000, transcendentals=0),
+    )(atom_features, w_center, w_neigh, w_radial, w_env, w_latent)
+    return cpart, (*weights, w_out[None, :])
 
 
 def per_device(
@@ -379,7 +421,8 @@
         placed.reshape(peers, ROWS // peers, WIDTH), "gy", split_axis=0, concat_axis=0, tiled=True
     ).reshape(ROWS, WIDTH)
     total = (g_mid + from_left + from_right).reshape(3, 3, 4, 128)
-    forces = total[:, 1] + shift(total[:, 2], "gy", 1) + shift(total[:, 0], "gy", -1)
+    up, down, pair_energy = lax.optimization_barrier((shift(total[:, 2], "gy", 1), shift(total[:, 0], "gy", -1), pair_energy))
+    forces = total[:, 1] + up + down
     return forces.reshape(3, ATOMS), ae.reshape(2 * ROWS), pair_energy
 
 

time: 93.6 us -> 76.7 us (0.82)
  local copies, waits for them, and re-layouts: 11.2 us -> 4.57 us
  waiting for transfers between devices: 9.62 us -> 5.08 us
  other arithmetic: 3.06 us -> 0.01 us
  matrix products: 1.64 us -> 0 us
  Pallas kernels: 36.5 us -> 35.1 us
    all_to_all x1, waiting for transfers between devices: 7.9 us -> 2.65 us  [per_device(): lax.all_to_all(placed.reshape(peers, ROWS // peers, WIDTH), 'gy', split_a...]
    slice x4 -> x0, local copies, waits for them, and re-layouts: 2.41 us -> none  [the longest x1 1.08 us: prepare(): wl1 = jnp.concatenate([w_latent[1] * half, pad], axis=0)]
    concatenate x3 -> x0, other arithmetic: 2.23 us -> none  [the longest x1 0.79 us: prepare(): rad = jnp.concatenate([rad, col(8), col(9)], axis=0)]
    dot_general x1 -> x0, matrix products: 1.64 us -> none  [prepare(): jnp.einsum('fc,fl->cl', atom_features[:, :2 * ROWS], w_center, precision=...]
    another operation x5 -> x0, local copies, waits for them, and re-layouts: 1.52 us -> none  [the longest x2 0.76 us: prepare(): we0 = jnp.tile(w_env[0], (1, 4))]
    pallas_call x1 -> x3, Pallas kernels: 36.5 us -> 35.1 us  [the longest x1 30.1 us: local_terms(): pl.pallas_call(kernel, out_shape=[jax.ShapeDtypeStruct((4, ROWS, WIDTH),...]
    concatenate x3 -> x0, local copies, waits for them, and re-layouts: 1.44 us -> none  [the longest x1 0.72 us: prepare(): wl0 = jnp.concatenate([w_latent[0] * half, pad], axis=0)]
    unnamed x42 -> x30, local copies, waits for them, and re-layouts: 5.64 us -> 4.54 us
  transfers between devices with their start and end apart: 13 -> 13, of which waited for: 2 -> 3; matrix products, arithmetic and copies ran while one was open for 11% -> 1% of each run, Pallas kernels for 0% -> 4%
where the time goes in v2:
time: 76.7 us; the launch traced here: 76.4 us
  Pallas kernels  35.1 us (46%)
  starting transfers between devices  30.8 us (40%)
  waiting for transfers between devices  5.08 us (7%)
  local copies, waits for them, and re-layouts  4.57 us (6%)
  between operations  0.87 us (1%)
    pallas_call x1, Pallas kernels, local_terms(): pl.pallas_call(kernel, out_shape=[jax.ShapeDtypeStruct((4, ROWS, WIDTH),...  30.1 us
    ppermute x12, starting transfers between devices, shift(): return lax.ppermute(x, axis, [(i, (i + step) % n) for i in range(n)])  21.9 us
    all_to_all x1, starting transfers between devices, per_device(): lax.all_to_all(placed.reshape(peers, ROWS // peers, WIDTH), 'gy', split_a...  8.9 us
    unnamed x30, local copies, waits for them, and re-layouts  4.54 us
    pallas_call x1, Pallas kernels, prepare(): pl.pallas_call(prepare_kernel, out_shape=shapes, in_specs=[vm] * 6, out_s...  2.81 us
    all_to_all x1, waiting for transfers between devices, per_device(): lax.all_to_all(placed.reshape(peers, ROWS // peers, WIDTH), 'gy', split_a...  2.65 us
    ppermute x12, waiting for transfers between devices, shift(): return lax.ppermute(x, axis, [(i, (i + step) % n) for i in range(n)])  2.43 us
    pallas_call x1, Pallas kernels, local_terms(): pl.pallas_call(scatter_kernel, out_shape=[ghost, ghost, ghost, jax.ShapeD...  2.19 us
  transfers between devices with their start and end apart: 13, of which 3 were waited for; matrix products, arithmetic and copies ran while one was open for 1% of the time, Pallas kernels for 4%

profile of v2, /device:TPU:8, one launch (start us, length us, event | category | flops | bytes accessed | tf_op | source)
XLA Modules:
  0.0 76.4 jit_solution(8685488681270421039)
XLA Ops:
  0.6 0.0 copy-start.4
  0.6 0.0 copy-start.3
  0.6 0.9 %constant_dynamic-update-slice_fusion.1 = f32[67,512]{1,0:T(8,128)S(1)} fusion(f32[64,512]{1,0:T(8,128)} %feat.1), kind=kLoop, calls=%fused_computation.9 | loop fusion | bytes 262144
  1.6 0.0 copy-done.4
  1.6 0.0 copy-start.2
  1.6 2.0 %collective-permute-start = (f32[67,512]{1,0:T(8,128)S(1)}, f32[67,512]{1,0:T(8,128)S(1)}, u32[]{:S(2)}, u32[]{:S(2)}) collective-permute-start(f32[67,512]{1,0:T(8,128)S(1)} %constant_dynamic-update-slice_fusion.t4), channel_id=1, source_target_pairs={{0,1},{1,2},{2,3},{3,4},{4,5},{5,6},{6,7},{7,8},{8,9},{9,10},{10,1... | collective-permute-start | bytes 411656 | tf_op jit(solution)/shard_map/ppermute | solution.py:405
  3.6 3.9 %collective-permute-start.3 = (f32[67,512]{1,0:T(8,128)S(1)}, f32[67,512]{1,0:T(8,128)S(1)}, u32[]{:S(2)}, u32[]{:S(2)}) collective-permute-start(f32[67,512]{1,0:T(8,128)S(1)} %constant_dynamic-update-slice_fusion.t4), channel_id=1, source_target_pairs={{0,31},{1,0},{2,1},{3,2},{4,3},{5,4},{6,5},{7,6},{8,7},{9,8},{10,9... | collective-permute-start | bytes 411656 | tf_op jit(solution)/shard_map/ppermute | solution.py:405
  7.5 0.0 collective-permute-start.2
  7.5 3.0 %collective-permute-start.6 = (f32[67,512]{1,0:T(8,128)S(1)}, f32[67,512]{1,0:T(8,128)S(1)}, u32[]{:S(2)}, u32[]{:S(2)}) collective-permute-start(f32[67,512]{1,0:T(8,128)S(1)} %constant_dynamic-update-slice_fusion.t4), channel_id=1, source_target_pairs={{0,224},{32,0},{64,32},{96,64},{128,96},{160,128},{192,160},{224,1... | collective-permute-start | bytes 411656 | tf_op jit(solution)/shard_map/ppermute | solution.py:405
  10.5 0.8 %collective-permute-done.t3 = f32[67,512]{1,0:T(8,128)S(1)} collective-permute-done((f32[67,512]{1,0:T(8,128)S(1)}, f32[67,512]{1,0:T(8,128)S(1)}, u32[]{:S(2)}, u32[]{:S(2)}) %collective-permute-start) | collective-permute-done | bytes 137248 | tf_op jit(solution)/shard_map/ppermute | solution.py:405
  11.3 0.0 copy-start.5
  11.3 0.0 collective-permute-start.1
  11.3 3.0 %collective-permute-start.5 = (f32[67,512]{1,0:T(8,128)S(1)}, f32[67,512]{1,0:T(8,128)S(1)}, u32[]{:S(2)}, u32[]{:S(2)}) collective-permute-start(f32[67,512]{1,0:T(8,128)S(1)} %collective-permute-done.t3), channel_id=1, source_target_pairs={{0,224},{32,0},{64,32},{96,64},{128,96},{160,128},{192,160},{224,1... | collective-permute-start | bytes 411656 | tf_op jit(solution)/shard_map/ppermute | solution.py:405
  14.3 0.0 collective-permute-done.3.t5
  14.3 0.0 copy-start.6
  14.3 0.0 collective-permute-start.4
  14.3 0.0 collective-permute-done.2.t1
  14.3 0.0 copy-start.7
  14.3 2.9 %collective-permute-start.7 = (f32[67,512]{1,0:T(8,128)S(1)}, f32[67,512]{1,0:T(8,128)S(1)}, u32[]{:S(2)}, u32[]{:S(2)}) collective-permute-start(f32[67,512]{1,0:T(8,128)S(1)} %collective-permute-done.3.t5), channel_id=1, source_target_pairs={{0,224},{32,0},{64,32},{96,64},{128,96},{160,128},{192,160},{224,1... | collective-permute-start | bytes 411656 | tf_op jit(solution)/shard_map/ppermute | solution.py:405
  17.2 0.0 copy-done.3
  17.2 0.8 copy.16.we_ref
  18.0 2.8 %shard_map.121 = (f32[64,256]{1,0:T(8,128)}, bf16[512,256]{1,0:T(8,128)(2,1)}, bf16[256,256]{1,0:T(8,128)(2,1)}, bf16[256,256]{1,0:T(8,128)(2,1)}, bf16[512,256]...) custom-call(f32[64,512]{1,0:T(8,128)} %feat.1, ...), custom_call_target="tpu_custom_call" | custom-call | flops 80000000 | bytes 4000000 | tf_op jit(solution)/shard_map/pallas_call | solution.py:389
  20.8 0.0 copy-done.2
  20.8 0.0 copy-done.5
  20.8 0.0 copy-done.6
  20.8 0.0 copy-done.7
  20.8 0.0 collective-permute-done.6.t7
  20.8 0.0 copy-start.8
  20.8 0.0 collective-permute-done.1.t0
  20.9 0.0 copy-start.9
  20.9 0.0 collective-permute-done.4.t2
  20.9 0.0 copy-start.11
  20.9 0.0 collective-permute-done.5.t6
  20.9 0.0 copy-start.10
  20.9 0.0 collective-permute-done.7.t8
  20.9 0.0 copy-start.12
  20.9 0.6 copy-done.8
  21.5 0.1 copy-done.9
  21.6 0.1 copy-done.11
  21.6 0.0 copy-done.10
  21.7 0.0 copy-done.12
  21.7 0.0 copy-start
  21.7 30.1 %shard_map.122 = (f32[4,32,128]{2,1,0:T(8,128)}, f32[32,128]{1,0:T(8,128)}) custom-call(s32[32,128]{1,0:T(8,128)} %idx_v.3, s32[1,32]{1,0:T(1,128)} %slot_s.1, s32[32,128]{1,0:T(8,128)} %idx_v.3, f32[67,512]{1,0:T(8,128)} %copy-done.9, f32[67,512]{1,0:T(8,128)} %copy-done.7, f32[67,512]{1,0:T(8,128)} %copy-done.11, f32[67,512]{1,0:T(8,128)} %copy-done.5, ...), custom_call_target="tpu_custom_call" | custom-call | flops 20000000000 | bytes 4000000 | tf_op jit(solution)/shard_map/pallas_call | solution.py:313
  51.7 0.0 copy-done
  51.8 0.0 copy-start.1
  51.8 0.8 %copy-done.1 = f32[4,32,128]{2,1,0:T(8,128)S(1)} copy-done((f32[4,32,128]{2,1,0:T(8,128)S(1)}, f32[4,32,128]{2,1,0:T(8,128)}, u32[]{:S(2)}) %copy-start.1) | copy-done | bytes 65560
  52.6 2.2 %shard_map.123 = (f32[36,128]{1,0:T(8,128)S(1)}, f32[36,128]{1,0:T(8,128)S(1)}, f32[36,128]{1,0:T(8,128)S(1)}, f32[1,64]{1,0:T(1,128)}) custom-call(s32[32,128]{1,0:T(8,128)S(1)} %copy-done, f32[4,32,128]{2,1,0:T(8,128)S(1)} %copy-done.1), custom_call_target="tpu_custom_call" | custom-call | flops 5000000000 | bytes 1000000 | tf_op jit(solution)/shard_map/pallas_call | solution.py:332
  54.8 0.0 collective-permute-start.8
  54.8 3.0 %collective-permute-start.9 = (f32[36,128]{1,0:T(8,128)S(1)}, f32[36,128]{1,0:T(8,128)S(1)}, u32[]{:S(2)}, u32[]{:S(2)}) collective-permute-start(f32[36,128]{1,0:T(8,128)S(1)} %get-tuple-element.37), channel_id=1, source_target_pairs={{0,224},{32,0},{64,32},{96,64},{128,96},{160,128},{192,160},{224,1... | collective-permute-start | bytes 55304 | tf_op jit(solution)/shard_map/ppermute | solution.py:405
  57.8 8.9 %all-to-all-start = ((f32[32,1,128]{2,1,0:T(1,128)}), f32[32,1,128]{2,1,0:T(1,128)S(1)}, u32[]{:S(2)}, u32[]{:S(2)}) async-start(f32[32,1,128]{2,1,0:T(1,128)} %bitcast.5), calls=%async_computation | async-start | bytes 32768 | tf_op jit(solution)/shard_map/all_to_all | solution.py:420
  66.7 0.0 collective-permute-done.8
  66.7 0.0 collective-permute-done.9
  66.7 1.5 %collective-permute-start.10 = (f32[3,4,128]{2,1,0:T(4,128)S(1)}, f32[3,4,128]{2,1,0:T(4,128)S(1)}, u32[]{:S(2)}, u32[]{:S(2)}) collective-permute-start(f32[3,4,128]{2,1,0:T(4,128)S(1)} %get-tuple-element.44), channel_id=1, source_target_pairs={{0,1},{1,2},{2,3},{3,4},{4,5},{5,6},{6,7},{7,8},{8,9},{9,10},{10,1... | collective-permute-start | bytes 18440 | tf_op jit(solution)/shard_map/ppermute | solution.py:405
  68.3 2.7 %collective-permute-start.11 = (f32[3,4,128]{2,1,0:T(4,128)S(1)}, f32[3,4,128]{2,1,0:T(4,128)S(1)}, u32[]{:S(2)}, u32[]{:S(2)}) collective-permute-start(f32[3,4,128]{2,1,0:T(4,128)S(1)} %get-tuple-element.43), channel_id=1, source_target_pairs={{0,31},{1,0},{2,1},{3,2},{4,3},{5,4},{6,5},{7,6},{8,7},{9,8},{10,9... | collective-permute-start | bytes 18440 | tf_op jit(solution)/shard_map/ppermute | solution.py:405
  70.9 1.6 %collective-permute-done.10 = f32[3,4,128]{2,1,0:T(4,128)S(1)} collective-permute-done((f32[3,4,128]{2,1,0:T(4,128)S(1)}, f32[3,4,128]{2,1,0:T(4,128)S(1)}, u32[]{:S(2)}, u32[]{:S(2)}) %collective-permute-start.10) | collective-permute-done | bytes 6176 | tf_op jit(solution)/shard_map/ppermute | solution.py:405
  72.5 0.0 collective-permute-done.11
  72.5 2.7 %all-to-all-done = f32[32,1,128]{2,1,0:T(1,128)S(1)} async-done(((f32[32,1,128]{2,1,0:T(1,128)}), f32[32,1,128]{2,1,0:T(1,128)S(1)}, u32[]{:S(2)}, u32[]{:S(2)}) %all-to-all-start) | async-done | bytes 16416 | tf_op jit(solution)/shard_map/all_to_all | solution.py:420
  75.2 0.6 copy.24
  75.8 0.6 copy.27
  (5 shorter events, 0.0 us)
Async XLA Ops:
  0.6 1.0 %copy-start.4 = (f32[3,512]{1,0:T(4,128)S(1)}, f32[3,512]{1,0:T(4,128)}, u32[]{:S(2)}) copy-start(f32[3,512]{1,0:T(4,128)} %param.10) | copy-start | bytes 18436
  0.6 16.6 %copy-start.3 = (bf16[2,256,64]{1,2,0:T(8,128)(2,1)S(1)}, bf16[2,256,64]{1,2,0:T(8,128)(2,1)}, u32[]{:S(2)}) copy-start(bf16[2,256,64]{1,2,0:T(8,128)(2,1)} %param.17) | copy-start | bytes 196612
  1.6 19.2 %copy-start.2 = (f32[67,512]{1,0:T(8,128)}, f32[67,512]{1,0:T(8,128)S(1)}, u32[]{:S(2)}) copy-start(f32[67,512]{1,0:T(8,128)S(1)} %constant_dynamic-update-slice_fusion.t4) | copy-start | bytes 411652
  1.6 9.7 %collective-permute-start = (f32[67,512]{1,0:T(8,128)S(1)}, f32[67,512]{1,0:T(8,128)S(1)}, u32[]{:S(2)}, u32[]{:S(2)}) collective-permute-start(f32[67,512]{1,0:T(8,128)S(1)} %constant_dynamic-update-slice_fusion.t4), channel_id=1, source_target_pairs={{0,1},{1,2},{2,3},{3,4},{4,5},{5,6},{6,7},{7,8},{8,9},{9,10},{10,1... | collective-permute-start | bytes 411656 | tf_op jit(solution)/shard_map/ppermute | solution.py:405
  3.6 10.6 %collective-permute-start.3 = (f32[67,512]{1,0:T(8,128)S(1)}, f32[67,512]{1,0:T(8,128)S(1)}, u32[]{:S(2)}, u32[]{:S(2)}) collective-permute-start(f32[67,512]{1,0:T(8,128)S(1)} %constant_dynamic-update-slice_fusion.t4), channel_id=1, source_target_pairs={{0,31},{1,0},{2,1},{3,2},{4,3},{5,4},{6,5},{7,6},{8,7},{9,8},{10,9... | collective-permute-start | bytes 411656 | tf_op jit(solution)/shard_map/ppermute | solution.py:405
  7.5 6.7 %collective-permute-start.2 = (f32[67,512]{1,0:T(8,128)S(1)}, f32[67,512]{1,0:T(8,128)S(1)}, u32[]{:S(2)}, u32[]{:S(2)}) collective-permute-start(f32[67,512]{1,0:T(8,128)S(1)} %constant_dynamic-update-slice_fusion.t4), channel_id=1, source_target_pairs={{0,32},{32,64},{64,96},{96,128},{128,160},{160,192},{192,224},{224... | collective-permute-start | bytes 411656 | tf_op jit(solution)/shard_map/ppermute | solution.py:405
  7.5 13.3 %collective-permute-start.6 = (f32[67,512]{1,0:T(8,128)S(1)}, f32[67,512]{1,0:T(8,128)S(1)}, u32[]{:S(2)}, u32[]{:S(2)}) collective-permute-start(f32[67,512]{1,0:T(8,128)S(1)} %constant_dynamic-update-slice_fusion.t4), channel_id=1, source_target_pairs={{0,224},{32,0},{64,32},{96,64},{128,96},{160,128},{192,160},{224,1... | collective-permute-start | bytes 411656 | tf_op jit(solution)/shard_map/ppermute | solution.py:405
  11.3 9.5 %copy-start.5 = (f32[67,512]{1,0:T(8,128)}, f32[67,512]{1,0:T(8,128)S(1)}, u32[]{:S(2)}) copy-start(f32[67,512]{1,0:T(8,128)S(1)} %collective-permute-done.t3) | copy-start | bytes 411652
  11.3 9.5 %collective-permute-start.1 = (f32[67,512]{1,0:T(8,128)S(1)}, f32[67,512]{1,0:T(8,128)S(1)}, u32[]{:S(2)}, u32[]{:S(2)}) collective-permute-start(f32[67,512]{1,0:T(8,128)S(1)} %collective-permute-done.t3), channel_id=1, source_target_pairs={{0,32},{32,64},{64,96},{96,128},{128,160},{160,192},{192,224},{224... | collective-permute-start | bytes 411656 | tf_op jit(solution)/shard_map/ppermute | solution.py:405
  11.3 9.6 %collective-permute-start.5 = (f32[67,512]{1,0:T(8,128)S(1)}, f32[67,512]{1,0:T(8,128)S(1)}, u32[]{:S(2)}, u32[]{:S(2)}) collective-permute-start(f32[67,512]{1,0:T(8,128)S(1)} %collective-permute-done.t3), channel_id=1, source_target_pairs={{0,224},{32,0},{64,32},{96,64},{128,96},{160,128},{192,160},{224,1... | collective-permute-start | bytes 411656 | tf_op jit(solution)/shard_map/ppermute | solution.py:405
  14.3 6.5 %copy-start.6 = (f32[67,512]{1,0:T(8,128)}, f32[67,512]{1,0:T(8,128)S(1)}, u32[]{:S(2)}) copy-start(f32[67,512]{1,0:T(8,128)S(1)} %collective-permute-done.3.t5) | copy-start | bytes 411652
  14.3 6.6 %collective-permute-start.4 = (f32[67,512]{1,0:T(8,128)S(1)}, f32[67,512]{1,0:T(8,128)S(1)}, u32[]{:S(2)}, u32[]{:S(2)}) collective-permute-start(f32[67,512]{1,0:T(8,128)S(1)} %collective-permute-done.3.t5), channel_id=1, source_target_pairs={{0,32},{32,64},{64,96},{96,128},{128,160},{160,192},{192,224},{224... | collective-permute-start | bytes 411656 | tf_op jit(solution)/shard_map/ppermute | solution.py:405
  14.3 6.5 %copy-start.7 = (f32[67,512]{1,0:T(8,128)}, f32[67,512]{1,0:T(8,128)S(1)}, u32[]{:S(2)}) copy-start(f32[67,512]{1,0:T(8,128)S(1)} %collective-permute-done.2.t1) | copy-start | bytes 411652
  14.3 6.6 %collective-permute-start.7 = (f32[67,512]{1,0:T(8,128)S(1)}, f32[67,512]{1,0:T(8,128)S(1)}, u32[]{:S(2)}, u32[]{:S(2)}) collective-permute-start(f32[67,512]{1,0:T(8,128)S(1)} %collective-permute-done.3.t5), channel_id=1, source_target_pairs={{0,224},{32,0},{64,32},{96,64},{128,96},{160,128},{192,160},{224,1... | collective-permute-start | bytes 411656 | tf_op jit(solution)/shard_map/ppermute | solution.py:405
  20.8 0.7 copy-start.8
  20.9 0.7 copy-start.9
  20.9 0.7 copy-start.11
  20.9 0.8 copy-start.10
  20.9 0.8 %copy-start.12 = (f32[67,512]{1,0:T(8,128)}, f32[67,512]{1,0:T(8,128)S(1)}, u32[]{:S(2)}) copy-start(f32[67,512]{1,0:T(8,128)S(1)} %collective-permute-done.7.t8) | copy-start | bytes 411652
  21.7 30.1 %copy-start = (s32[32,128]{1,0:T(8,128)S(1)}, s32[32,128]{1,0:T(8,128)}, u32[]{:S(2)}) copy-start(s32[32,128]{1,0:T(8,128)} %idx_v.3) | copy-start | bytes 49156
  51.8 0.8 %copy-start.1 = (f32[4,32,128]{2,1,0:T(8,128)S(1)}, f32[4,32,128]{2,1,0:T(8,128)}, u32[]{:S(2)}) copy-start(f32[4,32,128]{2,1,0:T(8,128)} %get-tuple-element.34.terms_ref) | copy-start | bytes 196612
  54.8 11.9 %collective-permute-start.8 = (f32[36,128]{1,0:T(8,128)S(1)}, f32[36,128]{1,0:T(8,128)S(1)}, u32[]{:S(2)}, u32[]{:S(2)}) collective-permute-start(f32[36,128]{1,0:T(8,128)S(1)} %get-tuple-element.36), channel_id=1, source_target_pairs={{0,32},{32,64},{64,96},{96,128},{128,160},{160,192},{192,224},{224... | collective-permute-start | bytes 55304 | tf_op jit(solution)/shard_map/ppermute | solution.py:405
  54.8 11.9 %collective-permute-start.9 = (f32[36,128]{1,0:T(8,128)S(1)}, f32[36,128]{1,0:T(8,128)S(1)}, u32[]{:S(2)}, u32[]{:S(2)}) collective-permute-start(f32[36,128]{1,0:T(8,128)S(1)} %get-tuple-element.37), channel_id=1, source_target_pairs={{0,224},{32,0},{64,32},{96,64},{128,96},{160,128},{192,160},{224,1... | collective-permute-start | bytes 55304 | tf_op jit(solution)/shard_map/ppermute | solution.py:405
  57.8 17.5 %all-to-all-start = ((f32[32,1,128]{2,1,0:T(1,128)}), f32[32,1,128]{2,1,0:T(1,128)S(1)}, u32[]{:S(2)}, u32[]{:S(2)}) async-start(f32[32,1,128]{2,1,0:T(1,128)} %bitcast.5), calls=%async_computation | async-start | bytes 32768 | tf_op jit(solution)/shard_map/all_to_all | solution.py:420
  66.7 5.8 %collective-permute-start.10 = (f32[3,4,128]{2,1,0:T(4,128)S(1)}, f32[3,4,128]{2,1,0:T(4,128)S(1)}, u32[]{:S(2)}, u32[]{:S(2)}) collective-permute-start(f32[3,4,128]{2,1,0:T(4,128)S(1)} %get-tuple-element.44), channel_id=1, source_target_pairs={{0,1},{1,2},{2,3},{3,4},{4,5},{5,6},{6,7},{7,8},{8,9},{9,10},{10,1... | collective-permute-start | bytes 18440 | tf_op jit(solution)/shard_map/ppermute | solution.py:405
  68.3 4.3 %collective-permute-start.11 = (f32[3,4,128]{2,1,0:T(4,128)S(1)}, f32[3,4,128]{2,1,0:T(4,128)S(1)}, u32[]{:S(2)}, u32[]{:S(2)}) collective-permute-start(f32[3,4,128]{2,1,0:T(4,128)S(1)} %get-tuple-element.43), channel_id=1, source_target_pairs={{0,31},{1,0},{2,1},{3,2},{4,3},{5,4},{6,5},{7,6},{8,7},{9,8},{10,9... | collective-permute-start | bytes 18440 | tf_op jit(solution)/shard_map/ppermute | solution.py:405

commit v3 on v2

--- a/solution.py
+++ b/solution.py
@@ -40,6 +40,43 @@
 def split2(x):
     hi = x.astype(BF)
     return hi, (x - hi.astype(F32)).astype(BF)
+
+
+def prepare_kernel(
+    feat, wc_ref, wn_ref, wr_ref, we_ref, wl_ref,
+    cpart, win, we0, we1, wl0, wl1, wl0t, wl1t, lat0t, lat1t, rad,
+):
+    own = feat[:, 0:128].T[0:2 * ROWS]
+    fhi, flo = split2(own)
+    chi, clo = split2(0.5 * wc_ref[...])
+    cpart[...] = mm(fhi, chi) + mm(flo, chi) + mm(fhi, clo)
+    nhi, nlo = split2(0.5 * wn_ref[...])
+    rhi, rlo = split2(0.5 * wr_ref[...])
+    rhi, rlo = rhi.astype(F32), rlo.astype(F32)
+    pad = jnp.zeros((64, 256), BF)
+    radial = jnp.concatenate(
+        [jnp.zeros((32, 256), F32), rhi, rhi, rlo, jnp.zeros((72, 256), F32)], axis=0)
+    win[...] = jnp.concatenate([nhi, pad, nhi, pad, nlo, pad, radial.astype(BF)], axis=0)
+    rt = jnp.concatenate([rhi, jnp.zeros((120, 256), F32)], axis=0).T
+    lanes = lax.broadcasted_iota(jnp.int32, (256, 128), 1)
+    rad[0:256] = rt.astype(BF)
+    rad[256:512] = (lanes == 8).astype(F32).astype(BF)
+    rad[512:768] = (lanes == 9).astype(F32).astype(BF)
+    tile = (
+        lax.broadcasted_iota(jnp.int32, (64, 256), 0)
+        == lax.broadcasted_iota(jnp.int32, (64, 256), 1) % 64
+    ).astype(F32).astype(BF)
+    for layer, (we, wl, wlt, latt) in enumerate(
+        ((we0, wl0, wl0t, lat0t), (we1, wl1, wl1t, lat1t))
+    ):
+        tiled = mm(we_ref[layer], tile)
+        we[...] = tiled.astype(BF)
+        halved = jnp.concatenate(
+            [0.5 * wl_ref[layer].astype(F32), jnp.zeros((64, 256), F32)], axis=0)
+        wl[...] = halved.astype(BF)
+        wlt[...] = halved[256:512].T.astype(BF)
+        latt[0:256] = halved[0:256].T.astype(BF)
+        latt[256:] = tiled.T[0:latt.shape[0] - 256].astype(BF)
 
 
 def geometry(vx, vy, vz, index):
@@ -63,11 +100,11 @@
 
 
 def kernel(
-    idx_s, slot_s, idx_v, t0, t1, t2, t3, t4, t5, t6, t7, t8, cpart, win_ref,
-    we0_ref, we1_ref, wl0_ref, wl1_ref, wl0t_ref, wl1t_ref, lat0t_ref, lat1t_ref,
+    idx_s, slot_s, idx_v, t0, t1, t2, t3, t4, t5, t6, t7, t8,
+    cpart, win_ref, we0_ref, we1_ref, wl0_ref, wl1_ref, wl0t_ref, wl1t_ref, lat0t_ref, lat1t_ref,
     rad_ref, wout_ref,
-    terms_ref, placed_ref,
-    table, gbuf, pos, geo, bgeo,
+    left_ref, mid_ref, right_ref, ae_ref, placed_ref,
+    table, gbuf, pos, geo, bgeo, lhs, rhs,
 ):
     tables = (t0, t1, t2, t3, t4, t5, t6, t7, t8)
     feats = 64
@@ -268,14 +305,6 @@
     dd = dd - (dux * ux + duy * uy + duz * uz) * inv
     dv = [dux * inv + dd * ux, duy * inv + dd * uy, duz * inv + dd * uz]
 
-    for c in range(3):
-        terms_ref[c] = dv[c]
-    terms_ref[3] = energy
-    for b in range(ROWS):
-        placed_ref[pl.ds(slot_s[0, b], 1), :] = energy[b:b + 1]
-
-
-def scatter_kernel(idx_v, terms_ref, left_ref, mid_ref, right_ref, ae_ref, lhs, rhs):
     safe = jnp.maximum(idx_v[...], 0)
     nhi = safe // 128
     nlo = safe - nhi * 128
@@ -283,8 +312,9 @@
     sub_l = lax.broadcasted_iota(jnp.int32, (128, WIDTH), 0)
     sub_e = lax.broadcasted_iota(jnp.int32, (16, WIDTH), 0)
     half_i = lax.broadcasted_iota(jnp.int32, (128, WIDTH), 1) // SLOTS
-    high = [terms_ref[c].astype(BF).astype(F32) for c in range(4)]
-    low = [terms_ref[c] - high[c] for c in range(4)]
+    terms = dv + [energy]
+    high = [x.astype(BF).astype(F32) for x in terms]
+    low = [x - y for x, y in zip(terms, high)]
     for b in range(ROWS):
         cols = slice(b * WIDTH, (b + 1) * WIDTH)
         pick = sub_h == nhi[b:b + 1]
@@ -294,6 +324,7 @@
         one_lo = (sub_l == nlo[b:b + 1]).astype(F32)
         one_c = (sub_l == 2 * b + half_i).astype(F32)
         rhs[:, cols] = jnp.concatenate([one_lo, one_c], axis=0).astype(BF)
+        placed_ref[pl.ds(slot_s[0, b], 1), :] = energy[b:b + 1]
     acc = mm_nt(lhs[...], rhs[...])
     for c in range(3):
         both = acc[c * HPAD:(c + 1) * HPAD] + acc[(3 + c) * HPAD:(4 + c) * HPAD]
@@ -305,95 +336,49 @@
     ae_ref[...] = acc[240:241, 128:192] + acc[241:242, 128:192]
 
 
-def local_terms(tables, pair_neighbor, offload_slot, cpart, weights):
+def local_terms(tables, pair_neighbor, offload_slot, weights):
     vm = pl.BlockSpec(memory_space=pltpu.VMEM)
     sm = pl.BlockSpec(memory_space=pltpu.SMEM)
-    operands = [pair_neighbor, offload_slot, pair_neighbor, *tables, cpart, *weights]
-    specs = [sm, sm] + [vm] * (len(operands) - 2)
-    terms, placed = pl.pallas_call(
+    operands = [pair_neighbor, offload_slot, pair_neighbor, *tables, *weights]
+    ghost = jax.ShapeDtypeStruct((36, 128), F32)
+    return pl.pallas_call(
         kernel,
         out_shape=[
-            jax.ShapeDtypeStruct((4, ROWS, WIDTH), F32),
+            ghost, ghost, ghost, jax.ShapeDtypeStruct((1, 2 * ROWS), F32),
             jax.ShapeDtypeStruct((ROWS, WIDTH), F32),
         ],
-        in_specs=specs,
-        out_specs=[vm] * 2,
+        in_specs=[sm, sm] + [vm] * (len(operands) - 2),
+        out_specs=[vm] * 5,
         scratch_shapes=[
             pltpu.VMEM((LEAD + 9 * ATOMS, 128), F32),
             pltpu.VMEM((ROWS * WIDTH, 128), F32),
             pltpu.VMEM((3, ROWS, WIDTH), F32),
             pltpu.VMEM((ROWS, 32, WIDTH), F32),
             pltpu.VMEM((ROWS, 32, WIDTH), F32),
+            pltpu.VMEM((256, ROWS * WIDTH), BF),
+            pltpu.VMEM((256, ROWS * WIDTH), BF),
         ],
         compiler_params=pltpu.CompilerParams(vmem_limit_bytes=56 * 1024 * 1024),
         cost_estimate=pl.CostEstimate(flops=20_000_000_000, bytes_accessed=4_000_000, transcendentals=0),
     )(*operands)
-    ghost = jax.ShapeDtypeStruct((36, 128), F32)
-    left, mid, right, ae = pl.pallas_call(
-        scatter_kernel,
-        out_shape=[ghost, ghost, ghost, jax.ShapeDtypeStruct((1, 2 * ROWS), F32)],
-        in_specs=[vm] * 2,
-        out_specs=[vm] * 4,
-        scratch_shapes=[pltpu.VMEM((256, ROWS * WIDTH), BF)] * 2,
-        compiler_params=pltpu.CompilerParams(vmem_limit_bytes=24 * 1024 * 1024),
-        cost_estimate=pl.CostEstimate(flops=5_000_000_000, bytes_accessed=1_000_000, transcendentals=0),
-    )(pair_neighbor, terms)
-    return left, mid, right, ae, placed
-
-
-def prepare_kernel(
-    feat, wc_ref, wn_ref, wr_ref, we_ref, wl_ref,
-    cpart, win, we0, we1, wl0, wl1, wl0t, wl1t, lat0t, lat1t, rad,
-):
-    own = feat[:, 0:128].T[0:2 * ROWS]
-    fhi, flo = split2(own)
-    chi, clo = split2(0.5 * wc_ref[...])
-    cpart[...] = mm(fhi, chi) + mm(flo, chi) + mm(fhi, clo)
-    nhi, nlo = split2(0.5 * wn_ref[...])
-    rhi, rlo = split2(0.5 * wr_ref[...])
-    rhi, rlo = rhi.astype(F32), rlo.astype(F32)
-    pad = jnp.zeros((64, 256), BF)
-    radial = jnp.concatenate(
-        [jnp.zeros((32, 256), F32), rhi, rhi, rlo, jnp.zeros((72, 256), F32)], axis=0)
-    win[...] = jnp.concatenate([nhi, pad, nhi, pad, nlo, pad, radial.astype(BF)], axis=0)
-    rt = jnp.concatenate([rhi, jnp.zeros((120, 256), F32)], axis=0).T
-    lanes = lax.broadcasted_iota(jnp.int32, (256, 128), 1)
-    rad[0:256] = rt.astype(BF)
-    rad[256:512] = (lanes == 8).astype(F32).astype(BF)
-    rad[512:768] = (lanes == 9).astype(F32).astype(BF)
-    tile = (
-        lax.broadcasted_iota(jnp.int32, (64, 256), 0)
-        == lax.broadcasted_iota(jnp.int32, (64, 256), 1) % 64
-    ).astype(F32).astype(BF)
-    for layer, (we, wl, wlt, latt) in enumerate(
-        ((we0, wl0, wl0t, lat0t), (we1, wl1, wl1t, lat1t))
-    ):
-        tiled = mm(we_ref[layer], tile)
-        we[...] = tiled.astype(BF)
-        halved = jnp.concatenate(
-            [0.5 * wl_ref[layer].astype(F32), jnp.zeros((64, 256), F32)], axis=0)
-        wl[...] = halved.astype(BF)
-        wlt[...] = halved[256:512].T.astype(BF)
-        latt[0:256] = halved[0:256].T.astype(BF)
-        latt[256:] = tiled.T[0:latt.shape[0] - 256].astype(BF)
 
 
 def prepare(atom_features, w_center, w_neigh, w_radial, w_env, w_latent, w_out):
     vm = pl.BlockSpec(memory_space=pltpu.VMEM)
     sd = jax.ShapeDtypeStruct
-    sq = sd((256, 256), BF)
+    square, tall = sd((256, 256), BF), sd((512, 256), BF)
     shapes = [
-        sd((2 * ROWS, 256), F32), sd((512, 256), BF), sq, sq, sd((512, 256), BF),
-        sd((512, 256), BF), sq, sq, sd((512, 256), BF), sd((384, 256), BF), sd((768, 128), BF),
+        sd((2 * ROWS, 256), F32), tall, square, square, tall, tall, square, square, tall,
+        sd((384, 256), BF), sd((768, 128), BF),
     ]
-    cpart, *weights = pl.pallas_call(
+    weights = pl.pallas_call(
         prepare_kernel,
         out_shape=shapes,
         in_specs=[vm] * 6,
         out_specs=[vm] * len(shapes),
         cost_estimate=pl.CostEstimate(flops=80_000_000, bytes_accessed=4_000_000, transcendentals=0),
     )(atom_features, w_center, w_neigh, w_radial, w_env, w_latent)
-    return cpart, (*weights, w_out[None, :])
+    return (*weights, w_out[None, :])
 
 
 def per_device(
@@ -411,15 +396,12 @@
     for oy in (0, 2):
         left[oy] = shift(col[oy], "gx", 1)
         right[oy] = shift(col[oy], "gx", -1)
-    cpart, weights = prepare(atom_features, w_center, w_neigh, w_radial, w_env, w_latent, w_out)
+    weights = prepare(atom_features, w_center, w_neigh, w_radial, w_env, w_latent, w_out)
     g_left, g_mid, g_right, ae, placed = local_terms(
-        left + col + right, pair_neighbor, offload_slot, cpart, weights)
+        left + col + right, pair_neighbor, offload_slot, weights)
     from_left = shift(g_right, "gx", 1)
     from_right = shift(g_left, "gx", -1)
-    peers = lax.axis_size("gy")
-    pair_energy = lax.all_to_all(
-        placed.reshape(peers, ROWS // peers, WIDTH), "gy", split_axis=0, concat_axis=0, tiled=True
-    ).reshape(ROWS, WIDTH)
+    pair_energy = lax.all_to_all(placed, "gy", split_axis=0, concat_axis=0, tiled=True)
     total = (g_mid + from_left + from_right).reshape(3, 3, 4, 128)
     up, down, pair_energy = lax.optimization_barrier((shift(total[:, 2], "gy", 1), shift(total[:, 0], "gy", -1), pair_energy))
     forces = total[:, 1] + up + down

time: 76.7 us -> 75.3 us (0.982)
  local copies, waits for them, and re-layouts: 4.57 us -> 3.75 us
    unnamed x30 -> x28, local copies, waits for them, and re-layouts: 4.54 us -> 3.73 us
    pallas_call x2 -> x1, Pallas kernels: 32.2 us -> 31.7 us  [local_terms(): pl.pallas_call(kernel, out_shape=[ghost, ghost, ghost, jax.ShapeDtypeStru...]
where the time goes in v3:
time: 75.3 us; the launch traced here: 75.1 us
  Pallas kernels  34.5 us (46%)
  starting transfers between devices  30.8 us (41%)
  waiting for transfers between devices  5.07 us (7%)
  local copies, waits for them, and re-layouts  3.75 us (5%)
  between operations  0.87 us (1%)
    pallas_call x1, Pallas kernels, local_terms(): pl.pallas_call(kernel, out_shape=[ghost, ghost, ghost, jax.ShapeDtypeStru...  31.7 us
    ppermute x12, starting transfers between devices, shift(): return lax.ppermute(x, axis, [(i, (i + step) % n) for i in range(n)])  21.9 us
    all_to_all x1, starting transfers between devices, per_device(): lax.all_to_all(placed, 'gy', split_axis=0, concat_axis=0, tiled=True)  8.9 us
    unnamed x28, local copies, waits for them, and re-layouts  3.73 us
    pallas_call x1, Pallas kernels, prepare(): pl.pallas_call(prepare_kernel, out_shape=shapes, in_specs=[vm] * 6, out_s...  2.82 us
    all_to_all x1, waiting for transfers between devices, per_device(): lax.all_to_all(placed, 'gy', split_axis=0, concat_axis=0, tiled=True)  2.64 us
    ppermute x12, waiting for transfers between devices, shift(): return lax.ppermute(x, axis, [(i, (i + step) % n) for i in range(n)])  2.43 us
  transfers between devices with their start and end apart: 13, of which 3 were waited for; matrix products, arithmetic and copies ran while one was open for 1% of the time, Pallas kernels for 4%

profile of v3, /device:TPU:8, one launch (start us, length us, event | category | flops | bytes accessed | tf_op | source)
XLA Modules:
  0.0 75.1 jit_solution(12423851949747723091)
XLA Ops:
  0.6 0.0 copy-start.3
  0.6 0.0 copy-start.1
  0.6 0.9 %constant_dynamic-update-slice_fusion.1 = f32[67,512]{1,0:T(8,128)S(1)} fusion(f32[64,512]{1,0:T(8,128)} %feat.1), kind=kLoop, calls=%fused_computation.9 | loop fusion | bytes 262144
  1.6 0.0 copy-done.3
  1.6 0.0 copy-start
  1.6 2.0 %collective-permute-start = (f32[67,512]{1,0:T(8,128)S(1)}, f32[67,512]{1,0:T(8,128)S(1)}, u32[]{:S(2)}, u32[]{:S(2)}) collective-permute-start(f32[67,512]{1,0:T(8,128)S(1)} %constant_dynamic-update-slice_fusion.t4), channel_id=1, source_target_pairs={{0,1},{1,2},{2,3},{3,4},{4,5},{5,6},{6,7},{7,8},{8,9},{9,10},{10,1... | collective-permute-start | bytes 411656 | tf_op jit(solution)/shard_map/ppermute | solution.py:390
  3.6 3.9 %collective-permute-start.3 = (f32[67,512]{1,0:T(8,128)S(1)}, f32[67,512]{1,0:T(8,128)S(1)}, u32[]{:S(2)}, u32[]{:S(2)}) collective-permute-start(f32[67,512]{1,0:T(8,128)S(1)} %constant_dynamic-update-slice_fusion.t4), channel_id=1, source_target_pairs={{0,31},{1,0},{2,1},{3,2},{4,3},{5,4},{6,5},{7,6},{8,7},{9,8},{10,9... | collective-permute-start | bytes 411656 | tf_op jit(solution)/shard_map/ppermute | solution.py:390
  7.5 0.0 collective-permute-start.2
  7.5 3.0 %collective-permute-start.6 = (f32[67,512]{1,0:T(8,128)S(1)}, f32[67,512]{1,0:T(8,128)S(1)}, u32[]{:S(2)}, u32[]{:S(2)}) collective-permute-start(f32[67,512]{1,0:T(8,128)S(1)} %constant_dynamic-update-slice_fusion.t4), channel_id=1, source_target_pairs={{0,224},{32,0},{64,32},{96,64},{128,96},{160,128},{192,160},{224,1... | collective-permute-start | bytes 411656 | tf_op jit(solution)/shard_map/ppermute | solution.py:390
  10.5 0.8 %collective-permute-done.t3 = f32[67,512]{1,0:T(8,128)S(1)} collective-permute-done((f32[67,512]{1,0:T(8,128)S(1)}, f32[67,512]{1,0:T(8,128)S(1)}, u32[]{:S(2)}, u32[]{:S(2)}) %collective-permute-start) | collective-permute-done | bytes 137248 | tf_op jit(solution)/shard_map/ppermute | solution.py:390
  11.3 0.0 copy-start.4
  11.3 0.0 collective-permute-start.1
  11.3 3.0 %collective-permute-start.5 = (f32[67,512]{1,0:T(8,128)S(1)}, f32[67,512]{1,0:T(8,128)S(1)}, u32[]{:S(2)}, u32[]{:S(2)}) collective-permute-start(f32[67,512]{1,0:T(8,128)S(1)} %collective-permute-done.t3), channel_id=1, source_target_pairs={{0,224},{32,0},{64,32},{96,64},{128,96},{160,128},{192,160},{224,1... | collective-permute-start | bytes 411656 | tf_op jit(solution)/shard_map/ppermute | solution.py:390
  14.3 0.0 collective-permute-done.3.t5
  14.3 0.0 copy-start.5
  14.3 0.0 collective-permute-start.4
  14.3 0.0 collective-permute-done.2.t1
  14.3 0.0 copy-start.6
  14.3 2.9 %collective-permute-start.7 = (f32[67,512]{1,0:T(8,128)S(1)}, f32[67,512]{1,0:T(8,128)S(1)}, u32[]{:S(2)}, u32[]{:S(2)}) collective-permute-start(f32[67,512]{1,0:T(8,128)S(1)} %collective-permute-done.3.t5), channel_id=1, source_target_pairs={{0,224},{32,0},{64,32},{96,64},{128,96},{160,128},{192,160},{224,1... | collective-permute-start | bytes 411656 | tf_op jit(solution)/shard_map/ppermute | solution.py:390
  17.2 0.0 copy-done.1
  17.2 0.8 %copy.16.we_ref = bf16[2,256,64]{2,1,0:T(8,128)(2,1)} copy(bf16[2,256,64]{1,2,0:T(8,128)(2,1)S(1)} %copy-done.1) | data formatting | bytes 131072 | tf_op args[7]
  18.0 2.8 %shard_map.121 = (f32[64,256]{1,0:T(8,128)}, bf16[512,256]{1,0:T(8,128)(2,1)}, bf16[256,256]{1,0:T(8,128)(2,1)}, bf16[256,256]{1,0:T(8,128)(2,1)}, bf16[512,256]...) custom-call(f32[64,512]{1,0:T(8,128)} %feat.1, ...), custom_call_target="tpu_custom_call" | custom-call | flops 80000000 | bytes 4000000 | tf_op jit(solution)/shard_map/pallas_call | solution.py:374
  20.8 0.0 copy-done
  20.8 0.0 copy-done.4
  20.8 0.0 copy-done.5
  20.8 0.0 copy-done.6
  20.8 0.0 collective-permute-done.6.t7
  20.9 0.0 copy-start.7
  20.9 0.0 collective-permute-done.1.t0
  20.9 0.0 copy-start.8
  20.9 0.0 collective-permute-done.4.t2
  20.9 0.0 copy-start.10
  20.9 0.0 collective-permute-done.5.t6
  20.9 0.0 copy-start.9
  20.9 0.0 collective-permute-done.7.t8
  20.9 0.0 copy-start.11
  20.9 0.6 copy-done.7
  21.5 0.1 copy-done.8
  21.6 0.1 copy-done.10
  21.6 0.0 copy-done.9
  21.7 0.0 copy-done.11
  21.7 31.7 %shard_map.122 = (f32[36,128]{1,0:T(8,128)}, f32[36,128]{1,0:T(8,128)}, f32[36,128]{1,0:T(8,128)}, f32[1,64]{1,0:T(1,128)}, f32[32,128]{1,0:T(8,128)}) custom-call(s32[32,128]{1,0:T(8,128)} %idx_v.1, s32[1,32]{1,0:T(1,128)} %slot_s.1, s32[32,128]{1,0:T(8,128)} %idx_v.1, f32[67,512]{1,0:T(8,128)} %copy-done.8, f32[67,512]{1,0:T(8,128)} %copy-done.6, ...), custom_call_target="tpu_custom_call" | custom-call | flops 20000000000 | bytes 4000000 | tf_op jit(solution)/shard_map/pallas_call | solution.py:344
  53.4 0.0 copy-start.2
  53.5 0.0 collective-permute-start.8
  53.5 2.9 %collective-permute-start.9 = (f32[36,128]{1,0:T(8,128)}, f32[36,128]{1,0:T(8,128)S(1)}, u32[]{:S(2)}, u32[]{:S(2)}) collective-permute-start(f32[36,128]{1,0:T(8,128)} %get-tuple-element.35), channel_id=1, source_target_pairs={{0,224},{32,0},{64,32},{96,64},{128,96},{160,128},{192,160},{224,1... | collective-permute-start | bytes 55304 | tf_op jit(solution)/shard_map/ppermute | solution.py:390
  56.4 8.9 %all-to-all-start = ((f32[32,1,128]{2,1,0:T(1,128)}), f32[32,1,128]{2,1,0:T(1,128)S(1)}, u32[]{:S(2)}, u32[]{:S(2)}) async-start(f32[32,1,128]{2,1,0:T(1,128)} %bitcast.28), calls=%async_computation | async-start | bytes 32768 | tf_op jit(solution)/shard_map/all_to_all | solution.py:404
  65.3 0.0 collective-permute-done.8
  65.3 0.0 collective-permute-done.9
  65.4 0.0 copy-done.2
  65.4 1.5 %collective-permute-start.10 = (f32[3,4,128]{2,1,0:T(4,128)S(1)}, f32[3,4,128]{2,1,0:T(4,128)S(1)}, u32[]{:S(2)}, u32[]{:S(2)}) collective-permute-start(f32[3,4,128]{2,1,0:T(4,128)S(1)} %get-tuple-element.42), channel_id=1, source_target_pairs={{0,1},{1,2},{2,3},{3,4},{4,5},{5,6},{6,7},{7,8},{8,9},{9,10},{10,1... | collective-permute-start | bytes 18440 | tf_op jit(solution)/shard_map/ppermute | solution.py:390
  67.0 2.7 %collective-permute-start.11 = (f32[3,4,128]{2,1,0:T(4,128)S(1)}, f32[3,4,128]{2,1,0:T(4,128)S(1)}, u32[]{:S(2)}, u32[]{:S(2)}) collective-permute-start(f32[3,4,128]{2,1,0:T(4,128)S(1)} %get-tuple-element.41), channel_id=1, source_target_pairs={{0,31},{1,0},{2,1},{3,2},{4,3},{5,4},{6,5},{7,6},{8,7},{9,8},{10,9... | collective-permute-start | bytes 18440 | tf_op jit(solution)/shard_map/ppermute | solution.py:390
  69.6 1.6 %collective-permute-done.10 = f32[3,4,128]{2,1,0:T(4,128)S(1)} collective-permute-done((f32[3,4,128]{2,1,0:T(4,128)S(1)}, f32[3,4,128]{2,1,0:T(4,128)S(1)}, u32[]{:S(2)}, u32[]{:S(2)}) %collective-permute-start.10) | collective-permute-done | bytes 6176 | tf_op jit(solution)/shard_map/ppermute | solution.py:390
  71.2 0.0 collective-permute-done.11
  71.2 2.6 %all-to-all-done = f32[32,1,128]{2,1,0:T(1,128)S(1)} async-done(((f32[32,1,128]{2,1,0:T(1,128)}), f32[32,1,128]{2,1,0:T(1,128)S(1)}, u32[]{:S(2)}, u32[]{:S(2)}) %all-to-all-start) | async-done | bytes 16416 | tf_op jit(solution)/shard_map/all_to_all | solution.py:404
  73.9 0.6 copy.24
  74.5 0.6 copy.27
  (5 shorter events, 0.0 us)
Async XLA Ops:
  0.6 1.0 %copy-start.3 = (f32[3,512]{1,0:T(4,128)S(1)}, f32[3,512]{1,0:T(4,128)}, u32[]{:S(2)}) copy-start(f32[3,512]{1,0:T(4,128)} %param.10) | copy-start | bytes 18436
  0.6 16.6 %copy-start.1 = (bf16[2,256,64]{1,2,0:T(8,128)(2,1)S(1)}, bf16[2,256,64]{1,2,0:T(8,128)(2,1)}, u32[]{:S(2)}) copy-start(bf16[2,256,64]{1,2,0:T(8,128)(2,1)} %param.17) | copy-start | bytes 196612
  1.6 19.2 %copy-start = (f32[67,512]{1,0:T(8,128)}, f32[67,512]{1,0:T(8,128)S(1)}, u32[]{:S(2)}) copy-start(f32[67,512]{1,0:T(8,128)S(1)} %constant_dynamic-update-slice_fusion.t4) | copy-start | bytes 411652
  1.6 9.7 %collective-permute-start = (f32[67,512]{1,0:T(8,128)S(1)}, f32[67,512]{1,0:T(8,128)S(1)}, u32[]{:S(2)}, u32[]{:S(2)}) collective-permute-start(f32[67,512]{1,0:T(8,128)S(1)} %constant_dynamic-update-slice_fusion.t4), channel_id=1, source_target_pairs={{0,1},{1,2},{2,3},{3,4},{4,5},{5,6},{6,7},{7,8},{8,9},{9,10},{10,1... | collective-permute-start | bytes 411656 | tf_op jit(solution)/shard_map/ppermute | solution.py:390
  3.6 10.6 %collective-permute-start.3 = (f32[67,512]{1,0:T(8,128)S(1)}, f32[67,512]{1,0:T(8,128)S(1)}, u32[]{:S(2)}, u32[]{:S(2)}) collective-permute-start(f32[67,512]{1,0:T(8,128)S(1)} %constant_dynamic-update-slice_fusion.t4), channel_id=1, source_target_pairs={{0,31},{1,0},{2,1},{3,2},{4,3},{5,4},{6,5},{7,6},{8,7},{9,8},{10,9... | collective-permute-start | bytes 411656 | tf_op jit(solution)/shard_map/ppermute | solution.py:390
  7.5 6.7 %collective-permute-start.2 = (f32[67,512]{1,0:T(8,128)S(1)}, f32[67,512]{1,0:T(8,128)S(1)}, u32[]{:S(2)}, u32[]{:S(2)}) collective-permute-start(f32[67,512]{1,0:T(8,128)S(1)} %constant_dynamic-update-slice_fusion.t4), channel_id=1, source_target_pairs={{0,32},{32,64},{64,96},{96,128},{128,160},{160,192},{192,224},{224... | collective-permute-start | bytes 411656 | tf_op jit(solution)/shard_map/ppermute | solution.py:390
  7.5 13.3 %collective-permute-start.6 = (f32[67,512]{1,0:T(8,128)S(1)}, f32[67,512]{1,0:T(8,128)S(1)}, u32[]{:S(2)}, u32[]{:S(2)}) collective-permute-start(f32[67,512]{1,0:T(8,128)S(1)} %constant_dynamic-update-slice_fusion.t4), channel_id=1, source_target_pairs={{0,224},{32,0},{64,32},{96,64},{128,96},{160,128},{192,160},{224,1... | collective-permute-start | bytes 411656 | tf_op jit(solution)/shard_map/ppermute | solution.py:390
  11.3 9.5 %copy-start.4 = (f32[67,512]{1,0:T(8,128)}, f32[67,512]{1,0:T(8,128)S(1)}, u32[]{:S(2)}) copy-start(f32[67,512]{1,0:T(8,128)S(1)} %collective-permute-done.t3) | copy-start | bytes 411652
  11.3 9.6 %collective-permute-start.1 = (f32[67,512]{1,0:T(8,128)S(1)}, f32[67,512]{1,0:T(8,128)S(1)}, u32[]{:S(2)}, u32[]{:S(2)}) collective-permute-start(f32[67,512]{1,0:T(8,128)S(1)} %collective-permute-done.t3), channel_id=1, source_target_pairs={{0,32},{32,64},{64,96},{96,128},{128,160},{160,192},{192,224},{224... | collective-permute-start | bytes 411656 | tf_op jit(solution)/shard_map/ppermute | solution.py:390
  11.3 9.6 %collective-permute-start.5 = (f32[67,512]{1,0:T(8,128)S(1)}, f32[67,512]{1,0:T(8,128)S(1)}, u32[]{:S(2)}, u32[]{:S(2)}) collective-permute-start(f32[67,512]{1,0:T(8,128)S(1)} %collective-permute-done.t3), channel_id=1, source_target_pairs={{0,224},{32,0},{64,32},{96,64},{128,96},{160,128},{192,160},{224,1... | collective-permute-start | bytes 411656 | tf_op jit(solution)/shard_map/ppermute | solution.py:390
  14.3 6.6 %copy-start.5 = (f32[67,512]{1,0:T(8,128)}, f32[67,512]{1,0:T(8,128)S(1)}, u32[]{:S(2)}) copy-start(f32[67,512]{1,0:T(8,128)S(1)} %collective-permute-done.3.t5) | copy-start | bytes 411652
  14.3 6.6 %collective-permute-start.4 = (f32[67,512]{1,0:T(8,128)S(1)}, f32[67,512]{1,0:T(8,128)S(1)}, u32[]{:S(2)}, u32[]{:S(2)}) collective-permute-start(f32[67,512]{1,0:T(8,128)S(1)} %collective-permute-done.3.t5), channel_id=1, source_target_pairs={{0,32},{32,64},{64,96},{96,128},{128,160},{160,192},{192,224},{224... | collective-permute-start | bytes 411656 | tf_op jit(solution)/shard_map/ppermute | solution.py:390
  14.3 6.6 %copy-start.6 = (f32[67,512]{1,0:T(8,128)}, f32[67,512]{1,0:T(8,128)S(1)}, u32[]{:S(2)}) copy-start(f32[67,512]{1,0:T(8,128)S(1)} %collective-permute-done.2.t1) | copy-start | bytes 411652
  14.3 6.6 %collective-permute-start.7 = (f32[67,512]{1,0:T(8,128)S(1)}, f32[67,512]{1,0:T(8,128)S(1)}, u32[]{:S(2)}, u32[]{:S(2)}) collective-permute-start(f32[67,512]{1,0:T(8,128)S(1)} %collective-permute-done.3.t5), channel_id=1, source_target_pairs={{0,224},{32,0},{64,32},{96,64},{128,96},{160,128},{192,160},{224,1... | collective-permute-start | bytes 411656 | tf_op jit(solution)/shard_map/ppermute | solution.py:390
  20.9 0.7 copy-start.7
  20.9 0.7 copy-start.8
  20.9 0.7 copy-start.10
  20.9 0.8 %copy-start.9 = (f32[67,512]{1,0:T(8,128)}, f32[67,512]{1,0:T(8,128)S(1)}, u32[]{:S(2)}) copy-start(f32[67,512]{1,0:T(8,128)S(1)} %collective-permute-done.5.t6) | copy-start | bytes 411652
  20.9 0.8 %copy-start.11 = (f32[67,512]{1,0:T(8,128)}, f32[67,512]{1,0:T(8,128)S(1)}, u32[]{:S(2)}) copy-start(f32[67,512]{1,0:T(8,128)S(1)} %collective-permute-done.7.t8) | copy-start | bytes 411652
  53.4 11.9 %copy-start.2 = (f32[36,128]{1,0:T(8,128)S(1)}, f32[36,128]{1,0:T(8,128)}, u32[]{:S(2)}) copy-start(f32[36,128]{1,0:T(8,128)} %get-tuple-element.33) | copy-start | bytes 55300
  53.5 11.9 %collective-permute-start.8 = (f32[36,128]{1,0:T(8,128)}, f32[36,128]{1,0:T(8,128)S(1)}, u32[]{:S(2)}, u32[]{:S(2)}) collective-permute-start(f32[36,128]{1,0:T(8,128)} %get-tuple-element.34), channel_id=1, source_target_pairs={{0,32},{32,64},{64,96},{96,128},{128,160},{160,192},{192,224},{224... | collective-permute-start | bytes 55304 | tf_op jit(solution)/shard_map/ppermute | solution.py:390
  53.5 11.9 %collective-permute-start.9 = (f32[36,128]{1,0:T(8,128)}, f32[36,128]{1,0:T(8,128)S(1)}, u32[]{:S(2)}, u32[]{:S(2)}) collective-permute-start(f32[36,128]{1,0:T(8,128)} %get-tuple-element.35), channel_id=1, source_target_pairs={{0,224},{32,0},{64,32},{96,64},{128,96},{160,128},{192,160},{224,1... | collective-permute-start | bytes 55304 | tf_op jit(solution)/shard_map/ppermute | solution.py:390
  56.4 17.5 %all-to-all-start = ((f32[32,1,128]{2,1,0:T(1,128)}), f32[32,1,128]{2,1,0:T(1,128)S(1)}, u32[]{:S(2)}, u32[]{:S(2)}) async-start(f32[32,1,128]{2,1,0:T(1,128)} %bitcast.28), calls=%async_computation | async-start | bytes 32768 | tf_op jit(solution)/shard_map/all_to_all | solution.py:404
  65.4 5.8 %collective-permute-start.10 = (f32[3,4,128]{2,1,0:T(4,128)S(1)}, f32[3,4,128]{2,1,0:T(4,128)S(1)}, u32[]{:S(2)}, u32[]{:S(2)}) collective-permute-start(f32[3,4,128]{2,1,0:T(4,128)S(1)} %get-tuple-element.42), channel_id=1, source_target_pairs={{0,1},{1,2},{2,3},{3,4},{4,5},{5,6},{6,7},{7,8},{8,9},{9,10},{10,1... | collective-permute-start | bytes 18440 | tf_op jit(solution)/shard_map/ppermute | solution.py:390
  67.0 4.3 %collective-permute-start.11 = (f32[3,4,128]{2,1,0:T(4,128)S(1)}, f32[3,4,128]{2,1,0:T(4,128)S(1)}, u32[]{:S(2)}, u32[]{:S(2)}) collective-permute-start(f32[3,4,128]{2,1,0:T(4,128)S(1)} %get-tuple-element.41), channel_id=1, source_target_pairs={{0,31},{1,0},{2,1},{3,2},{4,3},{5,4},{6,5},{7,6},{8,7},{9,8},{10,9... | collective-permute-start | bytes 18440 | tf_op jit(solution)/shard_map/ppermute | solution.py:390

commit v4 on v3

--- a/solution.py
+++ b/solution.py
@@ -50,13 +50,12 @@
     fhi, flo = split2(own)
     chi, clo = split2(0.5 * wc_ref[...])
     cpart[...] = mm(fhi, chi) + mm(flo, chi) + mm(fhi, clo)
-    nhi, nlo = split2(0.5 * wn_ref[...])
     rhi, rlo = split2(0.5 * wr_ref[...])
     rhi, rlo = rhi.astype(F32), rlo.astype(F32)
     pad = jnp.zeros((64, 256), BF)
     radial = jnp.concatenate(
         [jnp.zeros((32, 256), F32), rhi, rhi, rlo, jnp.zeros((72, 256), F32)], axis=0)
-    win[...] = jnp.concatenate([nhi, pad, nhi, pad, nlo, pad, radial.astype(BF)], axis=0)
+    win[...] = jnp.concatenate([(0.5 * wn_ref[...]).astype(BF), pad, radial.astype(BF)], axis=0)
     rt = jnp.concatenate([rhi, jnp.zeros((120, 256), F32)], axis=0).T
     lanes = lax.broadcasted_iota(jnp.int32, (256, 128), 1)
     rad[0:256] = rt.astype(BF)
@@ -188,7 +187,7 @@
     def chunk(i, carry):
         first = pl.multiple_of(i * M, M)
         g = gbuf[pl.ds(first, M), :]
-        ghi, glo = split2(g)
+        ghi = g.astype(BF)
         st, tr, cadd = [], [], []
         centres = cpart[pl.ds(pl.multiple_of(i * 2 * NB, 2 * NB), 2 * NB), :]
         for b in range(NB):
@@ -210,7 +209,7 @@
         tb = trans.astype(BF)
         sbd = tb[:, 0:32]
         h0 = (
-            mm(cat(ghi, glo, ghi, tb), win_ref[...])
+            mm(cat(ghi, tb), win_ref[...])
             + jnp.concatenate(cadd, axis=0)
         )
         a0, d0 = act(h0)
@@ -368,7 +367,7 @@
     sd = jax.ShapeDtypeStruct
     square, tall = sd((256, 256), BF), sd((512, 256), BF)
     shapes = [
-        sd((2 * ROWS, 256), F32), tall, square, square, tall, tall, square, square, tall,
+        sd((2 * ROWS, 256), F32), square, square, square, tall, tall, square, square, tall,
         sd((384, 256), BF), sd((768, 128), BF),
     ]
     weights = pl.pallas_call(

time: 75.3 us -> 73.9 us (0.981)
  Pallas kernels: 34.5 us -> 33.1 us
    pallas_call x1, Pallas kernels: 31.7 us -> 30.4 us  [local_terms(): pl.pallas_call(kernel, out_shape=[ghost, ghost, ghost, jax.ShapeDtypeStru...]
where the time goes in v4:
time: 73.9 us; the launch traced here: 73.7 us
  Pallas kernels  33.1 us (45%)
  starting transfers between devices  30.8 us (42%)
  waiting for transfers between devices  5.07 us (7%)
  local copies, waits for them, and re-layouts  3.74 us (5%)
  between operations  0.87 us (1%)
    pallas_call x1, Pallas kernels, local_terms(): pl.pallas_call(kernel, out_shape=[ghost, ghost, ghost, jax.ShapeDtypeStru...  30.4 us
    ppermute x12, starting transfers between devices, shift(): return lax.ppermute(x, axis, [(i, (i + step) % n) for i in range(n)])  21.9 us
    all_to_all x1, starting transfers between devices, per_device(): lax.all_to_all(placed, 'gy', split_axis=0, concat_axis=0, tiled=True)  8.9 us
    unnamed x28, local copies, waits for them, and re-layouts  3.71 us
    pallas_call x1, Pallas kernels, prepare(): pl.pallas_call(prepare_kernel, out_shape=shapes, in_specs=[vm] * 6, out_s...  2.75 us
    all_to_all x1, waiting for transfers between devices, per_device(): lax.all_to_all(placed, 'gy', split_axis=0, concat_axis=0, tiled=True)  2.64 us
    ppermute x12, waiting for transfers between devices, shift(): return lax.ppermute(x, axis, [(i, (i + step) % n) for i in range(n)])  2.43 us
  transfers between devices with their start and end apart: 13, of which 3 were waited for; matrix products, arithmetic and copies ran while one was open for 1% of the time, Pallas kernels for 4%

profile of v4, /device:TPU:8, one launch (start us, length us, event | category | flops | bytes accessed | tf_op | source)
XLA Modules:
  0.0 73.7 jit_solution(909286574061074909)
XLA Ops:
  0.6 0.0 copy-start.3
  0.6 0.0 copy-start.1
  0.6 0.9 %constant_dynamic-update-slice_fusion.1 = f32[67,512]{1,0:T(8,128)S(1)} fusion(f32[64,512]{1,0:T(8,128)} %feat.1), kind=kLoop, calls=%fused_computation.9 | loop fusion | bytes 262144
  1.6 0.0 copy-done.3
  1.6 0.0 copy-start
  1.6 2.0 %collective-permute-start = (f32[67,512]{1,0:T(8,128)S(1)}, f32[67,512]{1,0:T(8,128)S(1)}, u32[]{:S(2)}, u32[]{:S(2)}) collective-permute-start(f32[67,512]{1,0:T(8,128)S(1)} %constant_dynamic-update-slice_fusion.t4), channel_id=1, source_target_pairs={{0,1},{1,2},{2,3},{3,4},{4,5},{5,6},{6,7},{7,8},{8,9},{9,10},{10,1... | collective-permute-start | bytes 411656 | tf_op jit(solution)/shard_map/ppermute | solution.py:389
  3.6 3.9 %collective-permute-start.3 = (f32[67,512]{1,0:T(8,128)S(1)}, f32[67,512]{1,0:T(8,128)S(1)}, u32[]{:S(2)}, u32[]{:S(2)}) collective-permute-start(f32[67,512]{1,0:T(8,128)S(1)} %constant_dynamic-update-slice_fusion.t4), channel_id=1, source_target_pairs={{0,31},{1,0},{2,1},{3,2},{4,3},{5,4},{6,5},{7,6},{8,7},{9,8},{10,9... | collective-permute-start | bytes 411656 | tf_op jit(solution)/shard_map/ppermute | solution.py:389
  7.5 0.0 collective-permute-start.2
  7.5 3.0 %collective-permute-start.6 = (f32[67,512]{1,0:T(8,128)S(1)}, f32[67,512]{1,0:T(8,128)S(1)}, u32[]{:S(2)}, u32[]{:S(2)}) collective-permute-start(f32[67,512]{1,0:T(8,128)S(1)} %constant_dynamic-update-slice_fusion.t4), channel_id=1, source_target_pairs={{0,224},{32,0},{64,32},{96,64},{128,96},{160,128},{192,160},{224,1... | collective-permute-start | bytes 411656 | tf_op jit(solution)/shard_map/ppermute | solution.py:389
  10.5 0.8 %collective-permute-done.t3 = f32[67,512]{1,0:T(8,128)S(1)} collective-permute-done((f32[67,512]{1,0:T(8,128)S(1)}, f32[67,512]{1,0:T(8,128)S(1)}, u32[]{:S(2)}, u32[]{:S(2)}) %collective-permute-start) | collective-permute-done | bytes 137248 | tf_op jit(solution)/shard_map/ppermute | solution.py:389
  11.3 0.0 copy-start.4
  11.3 0.0 collective-permute-start.1
  11.3 3.0 %collective-permute-start.5 = (f32[67,512]{1,0:T(8,128)S(1)}, f32[67,512]{1,0:T(8,128)S(1)}, u32[]{:S(2)}, u32[]{:S(2)}) collective-permute-start(f32[67,512]{1,0:T(8,128)S(1)} %collective-permute-done.t3), channel_id=1, source_target_pairs={{0,224},{32,0},{64,32},{96,64},{128,96},{160,128},{192,160},{224,1... | collective-permute-start | bytes 411656 | tf_op jit(solution)/shard_map/ppermute | solution.py:389
  14.3 0.0 collective-permute-done.3.t5
  14.3 0.0 copy-start.5
  14.3 0.0 collective-permute-start.4
  14.3 0.0 collective-permute-done.2.t1
  14.3 0.0 copy-start.6
  14.3 2.9 %collective-permute-start.7 = (f32[67,512]{1,0:T(8,128)S(1)}, f32[67,512]{1,0:T(8,128)S(1)}, u32[]{:S(2)}, u32[]{:S(2)}) collective-permute-start(f32[67,512]{1,0:T(8,128)S(1)} %collective-permute-done.3.t5), channel_id=1, source_target_pairs={{0,224},{32,0},{64,32},{96,64},{128,96},{160,128},{192,160},{224,1... | collective-permute-start | bytes 411656 | tf_op jit(solution)/shard_map/ppermute | solution.py:389
  17.2 0.0 copy-done.1
  17.2 0.8 %copy.16.we_ref = bf16[2,256,64]{2,1,0:T(8,128)(2,1)} copy(bf16[2,256,64]{1,2,0:T(8,128)(2,1)S(1)} %copy-done.1) | data formatting | bytes 131072 | tf_op args[7]
  18.0 2.7 %shard_map.121 = (f32[64,256]{1,0:T(8,128)}, bf16[256,256]{1,0:T(8,128)(2,1)}, bf16[256,256]{1,0:T(8,128)(2,1)}, bf16[256,256]{1,0:T(8,128)(2,1)}, bf16[512,256]...) custom-call(f32[64,512]{1,0:T(8,128)} %feat.1, ...), custom_call_target="tpu_custom_call" | custom-call | flops 80000000 | bytes 4000000 | tf_op jit(solution)/shard_map/pallas_call | solution.py:373
  20.7 0.0 copy-done
  20.7 0.0 copy-done.4
  20.7 0.0 copy-done.5
  20.8 0.0 copy-done.6
  20.8 0.0 collective-permute-done.6.t7
  20.8 0.0 copy-start.7
  20.8 0.0 collective-permute-done.1.t0
  20.8 0.0 copy-start.8
  20.8 0.0 collective-permute-done.4.t2
  20.8 0.0 copy-start.10
  20.8 0.0 collective-permute-done.5.t6
  20.8 0.0 copy-start.9
  20.8 0.0 collective-permute-done.7.t8
  20.9 0.0 copy-start.11
  20.9 0.6 copy-done.7
  21.4 0.1 copy-done.8
  21.5 0.1 copy-done.10
  21.6 0.0 copy-done.9
  21.6 0.0 copy-done.11
  21.6 30.4 %shard_map.122 = (f32[36,128]{1,0:T(8,128)}, f32[36,128]{1,0:T(8,128)}, f32[36,128]{1,0:T(8,128)}, f32[1,64]{1,0:T(1,128)}, f32[32,128]{1,0:T(8,128)}) custom-call(s32[32,128]{1,0:T(8,128)} %idx_v.1, s32[1,32]{1,0:T(1,128)} %slot_s.1, s32[32,128]{1,0:T(8,128)} %idx_v.1, f32[67,512]{1,0:T(8,128)} %copy-done.8, f32[67,512]{1,0:T(8,128)} %copy-done.6, ...), custom_call_target="tpu_custom_call" | custom-call | flops 20000000000 | bytes 4000000 | tf_op jit(solution)/shard_map/pallas_call | solution.py:343
  52.0 0.0 copy-start.2
  52.0 0.0 collective-permute-start.8
  52.1 2.9 %collective-permute-start.9 = (f32[36,128]{1,0:T(8,128)}, f32[36,128]{1,0:T(8,128)S(1)}, u32[]{:S(2)}, u32[]{:S(2)}) collective-permute-start(f32[36,128]{1,0:T(8,128)} %get-tuple-element.35), channel_id=1, source_target_pairs={{0,224},{32,0},{64,32},{96,64},{128,96},{160,128},{192,160},{224,1... | collective-permute-start | bytes 55304 | tf_op jit(solution)/shard_map/ppermute | solution.py:389
  55.0 8.9 %all-to-all-start = ((f32[32,1,128]{2,1,0:T(1,128)}), f32[32,1,128]{2,1,0:T(1,128)S(1)}, u32[]{:S(2)}, u32[]{:S(2)}) async-start(f32[32,1,128]{2,1,0:T(1,128)} %bitcast.28), calls=%async_computation | async-start | bytes 32768 | tf_op jit(solution)/shard_map/all_to_all | solution.py:403
  63.9 0.0 collective-permute-done.8
  63.9 0.0 collective-permute-done.9
  63.9 0.0 copy-done.2
  64.0 1.5 %collective-permute-start.10 = (f32[3,4,128]{2,1,0:T(4,128)S(1)}, f32[3,4,128]{2,1,0:T(4,128)S(1)}, u32[]{:S(2)}, u32[]{:S(2)}) collective-permute-start(f32[3,4,128]{2,1,0:T(4,128)S(1)} %get-tuple-element.42), channel_id=1, source_target_pairs={{0,1},{1,2},{2,3},{3,4},{4,5},{5,6},{6,7},{7,8},{8,9},{9,10},{10,1... | collective-permute-start | bytes 18440 | tf_op jit(solution)/shard_map/ppermute | solution.py:389
  65.5 2.7 %collective-permute-start.11 = (f32[3,4,128]{2,1,0:T(4,128)S(1)}, f32[3,4,128]{2,1,0:T(4,128)S(1)}, u32[]{:S(2)}, u32[]{:S(2)}) collective-permute-start(f32[3,4,128]{2,1,0:T(4,128)S(1)} %get-tuple-element.41), channel_id=1, source_target_pairs={{0,31},{1,0},{2,1},{3,2},{4,3},{5,4},{6,5},{7,6},{8,7},{9,8},{10,9... | collective-permute-start | bytes 18440 | tf_op jit(solution)/shard_map/ppermute | solution.py:389
  68.2 1.6 %collective-permute-done.10 = f32[3,4,128]{2,1,0:T(4,128)S(1)} collective-permute-done((f32[3,4,128]{2,1,0:T(4,128)S(1)}, f32[3,4,128]{2,1,0:T(4,128)S(1)}, u32[]{:S(2)}, u32[]{:S(2)}) %collective-permute-start.10) | collective-permute-done | bytes 6176 | tf_op jit(solution)/shard_map/ppermute | solution.py:389
  69.8 0.0 collective-permute-done.11
  69.8 2.6 %all-to-all-done = f32[32,1,128]{2,1,0:T(1,128)S(1)} async-done(((f32[32,1,128]{2,1,0:T(1,128)}), f32[32,1,128]{2,1,0:T(1,128)S(1)}, u32[]{:S(2)}, u32[]{:S(2)}) %all-to-all-start) | async-done | bytes 16416 | tf_op jit(solution)/shard_map/all_to_all | solution.py:403
  72.5 0.6 copy.24
  73.1 0.6 copy.27
  (5 shorter events, 0.0 us)
Async XLA Ops:
  0.6 1.0 %copy-start.3 = (f32[3,512]{1,0:T(4,128)S(1)}, f32[3,512]{1,0:T(4,128)}, u32[]{:S(2)}) copy-start(f32[3,512]{1,0:T(4,128)} %param.10) | copy-start | bytes 18436
  0.6 16.6 %copy-start.1 = (bf16[2,256,64]{1,2,0:T(8,128)(2,1)S(1)}, bf16[2,256,64]{1,2,0:T(8,128)(2,1)}, u32[]{:S(2)}) copy-start(bf16[2,256,64]{1,2,0:T(8,128)(2,1)} %param.17) | copy-start | bytes 196612
  1.6 19.1 %copy-start = (f32[67,512]{1,0:T(8,128)}, f32[67,512]{1,0:T(8,128)S(1)}, u32[]{:S(2)}) copy-start(f32[67,512]{1,0:T(8,128)S(1)} %constant_dynamic-update-slice_fusion.t4) | copy-start | bytes 411652
  1.6 9.7 %collective-permute-start = (f32[67,512]{1,0:T(8,128)S(1)}, f32[67,512]{1,0:T(8,128)S(1)}, u32[]{:S(2)}, u32[]{:S(2)}) collective-permute-start(f32[67,512]{1,0:T(8,128)S(1)} %constant_dynamic-update-slice_fusion.t4), channel_id=1, source_target_pairs={{0,1},{1,2},{2,3},{3,4},{4,5},{5,6},{6,7},{7,8},{8,9},{9,10},{10,1... | collective-permute-start | bytes 411656 | tf_op jit(solution)/shard_map/ppermute | solution.py:389
  3.6 10.6 %collective-permute-start.3 = (f32[67,512]{1,0:T(8,128)S(1)}, f32[67,512]{1,0:T(8,128)S(1)}, u32[]{:S(2)}, u32[]{:S(2)}) collective-permute-start(f32[67,512]{1,0:T(8,128)S(1)} %constant_dynamic-update-slice_fusion.t4), channel_id=1, source_target_pairs={{0,31},{1,0},{2,1},{3,2},{4,3},{5,4},{6,5},{7,6},{8,7},{9,8},{10,9... | collective-permute-start | bytes 411656 | tf_op jit(solution)/shard_map/ppermute | solution.py:389
  7.5 6.7 %collective-permute-start.2 = (f32[67,512]{1,0:T(8,128)S(1)}, f32[67,512]{1,0:T(8,128)S(1)}, u32[]{:S(2)}, u32[]{:S(2)}) collective-permute-start(f32[67,512]{1,0:T(8,128)S(1)} %constant_dynamic-update-slice_fusion.t4), channel_id=1, source_target_pairs={{0,32},{32,64},{64,96},{96,128},{128,160},{160,192},{192,224},{224... | collective-permute-start | bytes 411656 | tf_op jit(solution)/shard_map/ppermute | solution.py:389
  7.5 13.2 %collective-permute-start.6 = (f32[67,512]{1,0:T(8,128)S(1)}, f32[67,512]{1,0:T(8,128)S(1)}, u32[]{:S(2)}, u32[]{:S(2)}) collective-permute-start(f32[67,512]{1,0:T(8,128)S(1)} %constant_dynamic-update-slice_fusion.t4), channel_id=1, source_target_pairs={{0,224},{32,0},{64,32},{96,64},{128,96},{160,128},{192,160},{224,1... | collective-permute-start | bytes 411656 | tf_op jit(solution)/shard_map/ppermute | solution.py:389
  11.3 9.4 %copy-start.4 = (f32[67,512]{1,0:T(8,128)}, f32[67,512]{1,0:T(8,128)S(1)}, u32[]{:S(2)}) copy-start(f32[67,512]{1,0:T(8,128)S(1)} %collective-permute-done.t3) | copy-start | bytes 411652
  11.3 9.5 %collective-permute-start.1 = (f32[67,512]{1,0:T(8,128)S(1)}, f32[67,512]{1,0:T(8,128)S(1)}, u32[]{:S(2)}, u32[]{:S(2)}) collective-permute-start(f32[67,512]{1,0:T(8,128)S(1)} %collective-permute-done.t3), channel_id=1, source_target_pairs={{0,32},{32,64},{64,96},{96,128},{128,160},{160,192},{192,224},{224... | collective-permute-start | bytes 411656 | tf_op jit(solution)/shard_map/ppermute | solution.py:389
  11.3 9.5 %collective-permute-start.5 = (f32[67,512]{1,0:T(8,128)S(1)}, f32[67,512]{1,0:T(8,128)S(1)}, u32[]{:S(2)}, u32[]{:S(2)}) collective-permute-start(f32[67,512]{1,0:T(8,128)S(1)} %collective-permute-done.t3), channel_id=1, source_target_pairs={{0,224},{32,0},{64,32},{96,64},{128,96},{160,128},{192,160},{224,1... | collective-permute-start | bytes 411656 | tf_op jit(solution)/shard_map/ppermute | solution.py:389
  14.3 6.5 %copy-start.5 = (f32[67,512]{1,0:T(8,128)}, f32[67,512]{1,0:T(8,128)S(1)}, u32[]{:S(2)}) copy-start(f32[67,512]{1,0:T(8,128)S(1)} %collective-permute-done.3.t5) | copy-start | bytes 411652
  14.3 6.5 %collective-permute-start.4 = (f32[67,512]{1,0:T(8,128)S(1)}, f32[67,512]{1,0:T(8,128)S(1)}, u32[]{:S(2)}, u32[]{:S(2)}) collective-permute-start(f32[67,512]{1,0:T(8,128)S(1)} %collective-permute-done.3.t5), channel_id=1, source_target_pairs={{0,32},{32,64},{64,96},{96,128},{128,160},{160,192},{192,224},{224... | collective-permute-start | bytes 411656 | tf_op jit(solution)/shard_map/ppermute | solution.py:389
  14.3 6.5 %copy-start.6 = (f32[67,512]{1,0:T(8,128)}, f32[67,512]{1,0:T(8,128)S(1)}, u32[]{:S(2)}) copy-start(f32[67,512]{1,0:T(8,128)S(1)} %collective-permute-done.2.t1) | copy-start | bytes 411652
  14.3 6.6 %collective-permute-start.7 = (f32[67,512]{1,0:T(8,128)S(1)}, f32[67,512]{1,0:T(8,128)S(1)}, u32[]{:S(2)}, u32[]{:S(2)}) collective-permute-start(f32[67,512]{1,0:T(8,128)S(1)} %collective-permute-done.3.t5), channel_id=1, source_target_pairs={{0,224},{32,0},{64,32},{96,64},{128,96},{160,128},{192,160},{224,1... | collective-permute-start | bytes 411656 | tf_op jit(solution)/shard_map/ppermute | solution.py:389
  20.8 0.7 copy-start.7
  20.8 0.7 copy-start.8
  20.8 0.7 %copy-start.10 = (f32[67,512]{1,0:T(8,128)}, f32[67,512]{1,0:T(8,128)S(1)}, u32[]{:S(2)}) copy-start(f32[67,512]{1,0:T(8,128)S(1)} %collective-permute-done.4.t2) | copy-start | bytes 411652
  20.8 0.8 %copy-start.9 = (f32[67,512]{1,0:T(8,128)}, f32[67,512]{1,0:T(8,128)S(1)}, u32[]{:S(2)}) copy-start(f32[67,512]{1,0:T(8,128)S(1)} %collective-permute-done.5.t6) | copy-start | bytes 411652
  20.9 0.8 %copy-start.11 = (f32[67,512]{1,0:T(8,128)}, f32[67,512]{1,0:T(8,128)S(1)}, u32[]{:S(2)}) copy-start(f32[67,512]{1,0:T(8,128)S(1)} %collective-permute-done.7.t8) | copy-start | bytes 411652
  52.0 11.9 %copy-start.2 = (f32[36,128]{1,0:T(8,128)S(1)}, f32[36,128]{1,0:T(8,128)}, u32[]{:S(2)}) copy-start(f32[36,128]{1,0:T(8,128)} %get-tuple-element.33) | copy-start | bytes 55300
  52.0 11.9 %collective-permute-start.8 = (f32[36,128]{1,0:T(8,128)}, f32[36,128]{1,0:T(8,128)S(1)}, u32[]{:S(2)}, u32[]{:S(2)}) collective-permute-start(f32[36,128]{1,0:T(8,128)} %get-tuple-element.34), channel_id=1, source_target_pairs={{0,32},{32,64},{64,96},{96,128},{128,160},{160,192},{192,224},{224... | collective-permute-start | bytes 55304 | tf_op jit(solution)/shard_map/ppermute | solution.py:389
  52.1 11.9 %collective-permute-start.9 = (f32[36,128]{1,0:T(8,128)}, f32[36,128]{1,0:T(8,128)S(1)}, u32[]{:S(2)}, u32[]{:S(2)}) collective-permute-start(f32[36,128]{1,0:T(8,128)} %get-tuple-element.35), channel_id=1, source_target_pairs={{0,224},{32,0},{64,32},{96,64},{128,96},{160,128},{192,160},{224,1... | collective-permute-start | bytes 55304 | tf_op jit(solution)/shard_map/ppermute | solution.py:389
  55.0 17.4 %all-to-all-start = ((f32[32,1,128]{2,1,0:T(1,128)}), f32[32,1,128]{2,1,0:T(1,128)S(1)}, u32[]{:S(2)}, u32[]{:S(2)}) async-start(f32[32,1,128]{2,1,0:T(1,128)} %bitcast.28), calls=%async_computation | async-start | bytes 32768 | tf_op jit(solution)/shard_map/all_to_all | solution.py:403
  64.0 5.8 %collective-permute-start.10 = (f32[3,4,128]{2,1,0:T(4,128)S(1)}, f32[3,4,128]{2,1,0:T(4,128)S(1)}, u32[]{:S(2)}, u32[]{:S(2)}) collective-permute-start(f32[3,4,128]{2,1,0:T(4,128)S(1)} %get-tuple-element.42), channel_id=1, source_target_pairs={{0,1},{1,2},{2,3},{3,4},{4,5},{5,6},{6,7},{7,8},{8,9},{9,10},{10,1... | collective-permute-start | bytes 18440 | tf_op jit(solution)/shard_map/ppermute | solution.py:389
  65.5 4.3 %collective-permute-start.11 = (f32[3,4,128]{2,1,0:T(4,128)S(1)}, f32[3,4,128]{2,1,0:T(4,128)S(1)}, u32[]{:S(2)}, u32[]{:S(2)}) collective-permute-start(f32[3,4,128]{2,1,0:T(4,128)S(1)} %get-tuple-element.41), channel_id=1, source_target_pairs={{0,31},{1,0},{2,1},{3,2},{4,3},{5,4},{6,5},{7,6},{8,7},{9,8},{10,9... | collective-permute-start | bytes 18440 | tf_op jit(solution)/shard_map/ppermute | solution.py:389

commit v5 on v4

--- a/solution.py
+++ b/solution.py
@@ -57,10 +57,10 @@
         [jnp.zeros((32, 256), F32), rhi, rhi, rlo, jnp.zeros((72, 256), F32)], axis=0)
     win[...] = jnp.concatenate([(0.5 * wn_ref[...]).astype(BF), pad, radial.astype(BF)], axis=0)
     rt = jnp.concatenate([rhi, jnp.zeros((120, 256), F32)], axis=0).T
-    lanes = lax.broadcasted_iota(jnp.int32, (256, 128), 1)
+    lanes = lax.broadcasted_iota(jnp.int32, (128, 128), 1)
     rad[0:256] = rt.astype(BF)
-    rad[256:512] = (lanes == 8).astype(F32).astype(BF)
-    rad[512:768] = (lanes == 9).astype(F32).astype(BF)
+    rad[256:384] = (lanes == 8).astype(F32).astype(BF)
+    rad[384:512] = (lanes == 9).astype(F32).astype(BF)
     tile = (
         lax.broadcasted_iota(jnp.int32, (64, 256), 0)
         == lax.broadcasted_iota(jnp.int32, (64, 256), 1) % 64
@@ -241,7 +241,7 @@
         a2, d2 = act(h2)
         wo = wout_ref[...]
         pq = (lat1 + a2) * wo
-        pqh, pql = split2(pq[:, 0:128] + pq[:, 128:256])
+        pqh = (pq[:, 0:128] + pq[:, 128:256]).astype(BF)
         dlat2 = env2 * wo
         dz1 = (dlat2 * d2).astype(BF)
         dsc1 = mm(dz1, wl1t_ref[...])
@@ -277,9 +277,9 @@
         dlat0 = dlat1 + mm(cat(dz0, (dw0 * env2).astype(BF)), lat0t_ref[...])
         evl = dlat0 * a0 + dw0 * y0
         ev = ev + evl[:, 0:128] + evl[:, 128:256]
-        evh, evo = split2(ev)
+        evh = ev.astype(BF)
         dx0 = (dlat0 * env2 * d0).astype(BF)
-        res = mm(cat(dx0, pqh, pql, evh, evo), rad_ref[...])
+        res = mm(cat(dx0, pqh, evh), rad_ref[...])
         for b in range(NB):
             dst = ds[b].T
             bgeo[i * NB + b, 0:16, :] = dst[0:16] * half0 + dst[16:32] * half1
@@ -368,7 +368,7 @@
     square, tall = sd((256, 256), BF), sd((512, 256), BF)
     shapes = [
         sd((2 * ROWS, 256), F32), square, square, square, tall, tall, square, square, tall,
-        sd((384, 256), BF), sd((768, 128), BF),
+        sd((384, 256), BF), sd((512, 128), BF),
     ]
     weights = pl.pallas_call(
         prepare_kernel,

time: 73.9 us -> 73.7 us (level)
  no operation moved by 1% of the time
where the time goes in v5:
time: 73.7 us; the launch traced here: 73.5 us
  Pallas kernels  33 us (45%)
  starting transfers between devices  30.8 us (42%)
  waiting for transfers between devices  5.07 us (7%)
  local copies, waits for them, and re-layouts  3.76 us (5%)
  between operations  0.87 us (1%)
    pallas_call x1, Pallas kernels, local_terms(): pl.pallas_call(kernel, out_shape=[ghost, ghost, ghost, jax.ShapeDtypeStru...  30.3 us
    ppermute x12, starting transfers between devices, shift(): return lax.ppermute(x, axis, [(i, (i + step) % n) for i in range(n)])  21.9 us
    all_to_all x1, starting transfers between devices, per_device(): lax.all_to_all(placed, 'gy', split_axis=0, concat_axis=0, tiled=True)  8.9 us
    unnamed x28, local copies, waits for them, and re-layouts  3.74 us
    pallas_call x1, Pallas kernels, prepare(): pl.pallas_call(prepare_kernel, out_shape=shapes, in_specs=[vm] * 6, out_s...  2.72 us
    all_to_all x1, waiting for transfers between devices, per_device(): lax.all_to_all(placed, 'gy', split_axis=0, concat_axis=0, tiled=True)  2.64 us
    ppermute x12, waiting for transfers between devices, shift(): return lax.ppermute(x, axis, [(i, (i + step) % n) for i in range(n)])  2.43 us
  transfers between devices with their start and end apart: 13, of which 3 were waited for; matrix products, arithmetic and copies ran while one was open for 1% of the time, Pallas kernels for 4%

profile of v5, /device:TPU:8, one launch (start us, length us, event | category | flops | bytes accessed | tf_op | source)
XLA Modules:
  0.0 73.5 jit_solution(3180703193115238254)
XLA Ops:
  0.6 0.0 copy-start.3
  0.6 0.0 copy-start.1
  0.6 0.9 %constant_dynamic-update-slice_fusion.1 = f32[67,512]{1,0:T(8,128)S(1)} fusion(f32[64,512]{1,0:T(8,128)} %feat.1), kind=kLoop, calls=%fused_computation.9 | loop fusion | bytes 262144
  1.6 0.0 copy-done.3
  1.6 0.0 copy-start
  1.6 2.0 %collective-permute-start = (f32[67,512]{1,0:T(8,128)S(1)}, f32[67,512]{1,0:T(8,128)S(1)}, u32[]{:S(2)}, u32[]{:S(2)}) collective-permute-start(f32[67,512]{1,0:T(8,128)S(1)} %constant_dynamic-update-slice_fusion.t4), channel_id=1, source_target_pairs={{0,1},{1,2},{2,3},{3,4},{4,5},{5,6},{6,7},{7,8},{8,9},{9,10},{10,1... | collective-permute-start | bytes 411656 | tf_op jit(solution)/shard_map/ppermute | solution.py:389
  3.6 3.9 %collective-permute-start.3 = (f32[67,512]{1,0:T(8,128)S(1)}, f32[67,512]{1,0:T(8,128)S(1)}, u32[]{:S(2)}, u32[]{:S(2)}) collective-permute-start(f32[67,512]{1,0:T(8,128)S(1)} %constant_dynamic-update-slice_fusion.t4), channel_id=1, source_target_pairs={{0,31},{1,0},{2,1},{3,2},{4,3},{5,4},{6,5},{7,6},{8,7},{9,8},{10,9... | collective-permute-start | bytes 411656 | tf_op jit(solution)/shard_map/ppermute | solution.py:389
  7.5 0.0 collective-permute-start.2
  7.5 3.0 %collective-permute-start.6 = (f32[67,512]{1,0:T(8,128)S(1)}, f32[67,512]{1,0:T(8,128)S(1)}, u32[]{:S(2)}, u32[]{:S(2)}) collective-permute-start(f32[67,512]{1,0:T(8,128)S(1)} %constant_dynamic-update-slice_fusion.t4), channel_id=1, source_target_pairs={{0,224},{32,0},{64,32},{96,64},{128,96},{160,128},{192,160},{224,1... | collective-permute-start | bytes 411656 | tf_op jit(solution)/shard_map/ppermute | solution.py:389
  10.5 0.8 %collective-permute-done.t3 = f32[67,512]{1,0:T(8,128)S(1)} collective-permute-done((f32[67,512]{1,0:T(8,128)S(1)}, f32[67,512]{1,0:T(8,128)S(1)}, u32[]{:S(2)}, u32[]{:S(2)}) %collective-permute-start) | collective-permute-done | bytes 137248 | tf_op jit(solution)/shard_map/ppermute | solution.py:389
  11.3 0.0 copy-start.4
  11.3 0.0 collective-permute-start.1
  11.3 3.0 %collective-permute-start.5 = (f32[67,512]{1,0:T(8,128)S(1)}, f32[67,512]{1,0:T(8,128)S(1)}, u32[]{:S(2)}, u32[]{:S(2)}) collective-permute-start(f32[67,512]{1,0:T(8,128)S(1)} %collective-permute-done.t3), channel_id=1, source_target_pairs={{0,224},{32,0},{64,32},{96,64},{128,96},{160,128},{192,160},{224,1... | collective-permute-start | bytes 411656 | tf_op jit(solution)/shard_map/ppermute | solution.py:389
  14.3 0.0 collective-permute-done.3.t5
  14.3 0.0 copy-start.5
  14.3 0.0 collective-permute-start.4
  14.3 0.0 collective-permute-done.2.t1
  14.3 0.0 copy-start.6
  14.3 2.9 %collective-permute-start.7 = (f32[67,512]{1,0:T(8,128)S(1)}, f32[67,512]{1,0:T(8,128)S(1)}, u32[]{:S(2)}, u32[]{:S(2)}) collective-permute-start(f32[67,512]{1,0:T(8,128)S(1)} %collective-permute-done.3.t5), channel_id=1, source_target_pairs={{0,224},{32,0},{64,32},{96,64},{128,96},{160,128},{192,160},{224,1... | collective-permute-start | bytes 411656 | tf_op jit(solution)/shard_map/ppermute | solution.py:389
  17.2 0.0 copy-done.1
  17.2 0.8 %copy.16.we_ref = bf16[2,256,64]{2,1,0:T(8,128)(2,1)} copy(bf16[2,256,64]{1,2,0:T(8,128)(2,1)S(1)} %copy-done.1) | data formatting | bytes 131072 | tf_op args[7]
  18.0 2.7 %shard_map.121 = (f32[64,256]{1,0:T(8,128)}, bf16[256,256]{1,0:T(8,128)(2,1)}, bf16[256,256]{1,0:T(8,128)(2,1)}, bf16[256,256]{1,0:T(8,128)(2,1)}, bf16[512,256]...) custom-call(f32[64,512]{1,0:T(8,128)} %feat.1, ...), custom_call_target="tpu_custom_call" | custom-call | flops 80000000 | bytes 4000000 | tf_op jit(solution)/shard_map/pallas_call | solution.py:373
  20.7 0.0 copy-done
  20.7 0.0 copy-done.4
  20.7 0.0 copy-done.5
  20.7 0.0 copy-done.6
  20.7 0.0 collective-permute-done.6.t7
  20.8 0.0 copy-start.7
  20.8 0.0 collective-permute-done.1.t0
  20.8 0.0 copy-start.8
  20.8 0.0 collective-permute-done.4.t2
  20.8 0.0 copy-start.10
  20.8 0.0 collective-permute-done.5.t6
  20.8 0.0 copy-start.9
  20.8 0.0 collective-permute-done.7.t8
  20.8 0.0 copy-start.11
  20.8 0.6 copy-done.7
  21.4 0.1 copy-done.8
  21.5 0.1 copy-done.10
  21.5 0.1 copy-done.9
  21.6 0.0 copy-done.11
  21.6 30.3 %shard_map.122 = (f32[36,128]{1,0:T(8,128)}, f32[36,128]{1,0:T(8,128)}, f32[36,128]{1,0:T(8,128)}, f32[1,64]{1,0:T(1,128)}, f32[32,128]{1,0:T(8,128)}) custom-call(s32[32,128]{1,0:T(8,128)} %idx_v.1, s32[1,32]{1,0:T(1,128)} %slot_s.1, s32[32,128]{1,0:T(8,128)} %idx_v.1, f32[67,512]{1,0:T(8,128)} %copy-done.8, f32[67,512]{1,0:T(8,128)} %copy-done.6, ...), custom_call_target="tpu_custom_call" | custom-call | flops 20000000000 | bytes 4000000 | tf_op jit(solution)/shard_map/pallas_call | solution.py:343
  51.9 0.0 copy-start.2
  51.9 0.0 collective-permute-start.8
  51.9 2.9 %collective-permute-start.9 = (f32[36,128]{1,0:T(8,128)}, f32[36,128]{1,0:T(8,128)S(1)}, u32[]{:S(2)}, u32[]{:S(2)}) collective-permute-start(f32[36,128]{1,0:T(8,128)} %get-tuple-element.35), channel_id=1, source_target_pairs={{0,224},{32,0},{64,32},{96,64},{128,96},{160,128},{192,160},{224,1... | collective-permute-start | bytes 55304 | tf_op jit(solution)/shard_map/ppermute | solution.py:389
  54.9 8.9 %all-to-all-start = ((f32[32,1,128]{2,1,0:T(1,128)}), f32[32,1,128]{2,1,0:T(1,128)S(1)}, u32[]{:S(2)}, u32[]{:S(2)}) async-start(f32[32,1,128]{2,1,0:T(1,128)} %bitcast.28), calls=%async_computation | async-start | bytes 32768 | tf_op jit(solution)/shard_map/all_to_all | solution.py:403
  63.8 0.0 collective-permute-done.8
  63.8 0.0 collective-permute-done.9
  63.8 0.0 copy-done.2
  63.8 1.5 %collective-permute-start.10 = (f32[3,4,128]{2,1,0:T(4,128)S(1)}, f32[3,4,128]{2,1,0:T(4,128)S(1)}, u32[]{:S(2)}, u32[]{:S(2)}) collective-permute-start(f32[3,4,128]{2,1,0:T(4,128)S(1)} %get-tuple-element.42), channel_id=1, source_target_pairs={{0,1},{1,2},{2,3},{3,4},{4,5},{5,6},{6,7},{7,8},{8,9},{9,10},{10,1... | collective-permute-start | bytes 18440 | tf_op jit(solution)/shard_map/ppermute | solution.py:389
  65.4 2.7 %collective-permute-start.11 = (f32[3,4,128]{2,1,0:T(4,128)S(1)}, f32[3,4,128]{2,1,0:T(4,128)S(1)}, u32[]{:S(2)}, u32[]{:S(2)}) collective-permute-start(f32[3,4,128]{2,1,0:T(4,128)S(1)} %get-tuple-element.41), channel_id=1, source_target_pairs={{0,31},{1,0},{2,1},{3,2},{4,3},{5,4},{6,5},{7,6},{8,7},{9,8},{10,9... | collective-permute-start | bytes 18440 | tf_op jit(solution)/shard_map/ppermute | solution.py:389
  68.1 1.6 %collective-permute-done.10 = f32[3,4,128]{2,1,0:T(4,128)S(1)} collective-permute-done((f32[3,4,128]{2,1,0:T(4,128)S(1)}, f32[3,4,128]{2,1,0:T(4,128)S(1)}, u32[]{:S(2)}, u32[]{:S(2)}) %collective-permute-start.10) | collective-permute-done | bytes 6176 | tf_op jit(solution)/shard_map/ppermute | solution.py:389
  69.7 0.0 collective-permute-done.11
  69.7 2.6 %all-to-all-done = f32[32,1,128]{2,1,0:T(1,128)S(1)} async-done(((f32[32,1,128]{2,1,0:T(1,128)}), f32[32,1,128]{2,1,0:T(1,128)S(1)}, u32[]{:S(2)}, u32[]{:S(2)}) %all-to-all-start) | async-done | bytes 16416 | tf_op jit(solution)/shard_map/all_to_all | solution.py:403
  72.3 0.6 copy.24
  72.9 0.6 copy.27
  (5 shorter events, 0.0 us)
Async XLA Ops:
  0.6 1.0 %copy-start.3 = (f32[3,512]{1,0:T(4,128)S(1)}, f32[3,512]{1,0:T(4,128)}, u32[]{:S(2)}) copy-start(f32[3,512]{1,0:T(4,128)} %param.10) | copy-start | bytes 18436
  0.6 16.6 %copy-start.1 = (bf16[2,256,64]{1,2,0:T(8,128)(2,1)S(1)}, bf16[2,256,64]{1,2,0:T(8,128)(2,1)}, u32[]{:S(2)}) copy-start(bf16[2,256,64]{1,2,0:T(8,128)(2,1)} %param.17) | copy-start | bytes 196612
  1.6 19.1 %copy-start = (f32[67,512]{1,0:T(8,128)}, f32[67,512]{1,0:T(8,128)S(1)}, u32[]{:S(2)}) copy-start(f32[67,512]{1,0:T(8,128)S(1)} %constant_dynamic-update-slice_fusion.t4) | copy-start | bytes 411652
  1.6 9.7 %collective-permute-start = (f32[67,512]{1,0:T(8,128)S(1)}, f32[67,512]{1,0:T(8,128)S(1)}, u32[]{:S(2)}, u32[]{:S(2)}) collective-permute-start(f32[67,512]{1,0:T(8,128)S(1)} %constant_dynamic-update-slice_fusion.t4), channel_id=1, source_target_pairs={{0,1},{1,2},{2,3},{3,4},{4,5},{5,6},{6,7},{7,8},{8,9},{9,10},{10,1... | collective-permute-start | bytes 411656 | tf_op jit(solution)/shard_map/ppermute | solution.py:389
  3.6 10.6 %collective-permute-start.3 = (f32[67,512]{1,0:T(8,128)S(1)}, f32[67,512]{1,0:T(8,128)S(1)}, u32[]{:S(2)}, u32[]{:S(2)}) collective-permute-start(f32[67,512]{1,0:T(8,128)S(1)} %constant_dynamic-update-slice_fusion.t4), channel_id=1, source_target_pairs={{0,31},{1,0},{2,1},{3,2},{4,3},{5,4},{6,5},{7,6},{8,7},{9,8},{10,9... | collective-permute-start | bytes 411656 | tf_op jit(solution)/shard_map/ppermute | solution.py:389
  7.5 6.7 %collective-permute-start.2 = (f32[67,512]{1,0:T(8,128)S(1)}, f32[67,512]{1,0:T(8,128)S(1)}, u32[]{:S(2)}, u32[]{:S(2)}) collective-permute-start(f32[67,512]{1,0:T(8,128)S(1)} %constant_dynamic-update-slice_fusion.t4), channel_id=1, source_target_pairs={{0,32},{32,64},{64,96},{96,128},{128,160},{160,192},{192,224},{224... | collective-permute-start | bytes 411656 | tf_op jit(solution)/shard_map/ppermute | solution.py:389
  7.5 13.2 %collective-permute-start.6 = (f32[67,512]{1,0:T(8,128)S(1)}, f32[67,512]{1,0:T(8,128)S(1)}, u32[]{:S(2)}, u32[]{:S(2)}) collective-permute-start(f32[67,512]{1,0:T(8,128)S(1)} %constant_dynamic-update-slice_fusion.t4), channel_id=1, source_target_pairs={{0,224},{32,0},{64,32},{96,64},{128,96},{160,128},{192,160},{224,1... | collective-permute-start | bytes 411656 | tf_op jit(solution)/shard_map/ppermute | solution.py:389
  11.3 9.4 %copy-start.4 = (f32[67,512]{1,0:T(8,128)}, f32[67,512]{1,0:T(8,128)S(1)}, u32[]{:S(2)}) copy-start(f32[67,512]{1,0:T(8,128)S(1)} %collective-permute-done.t3) | copy-start | bytes 411652
  11.3 9.5 %collective-permute-start.1 = (f32[67,512]{1,0:T(8,128)S(1)}, f32[67,512]{1,0:T(8,128)S(1)}, u32[]{:S(2)}, u32[]{:S(2)}) collective-permute-start(f32[67,512]{1,0:T(8,128)S(1)} %collective-permute-done.t3), channel_id=1, source_target_pairs={{0,32},{32,64},{64,96},{96,128},{128,160},{160,192},{192,224},{224... | collective-permute-start | bytes 411656 | tf_op jit(solution)/shard_map/ppermute | solution.py:389
  11.3 9.5 %collective-permute-start.5 = (f32[67,512]{1,0:T(8,128)S(1)}, f32[67,512]{1,0:T(8,128)S(1)}, u32[]{:S(2)}, u32[]{:S(2)}) collective-permute-start(f32[67,512]{1,0:T(8,128)S(1)} %collective-permute-done.t3), channel_id=1, source_target_pairs={{0,224},{32,0},{64,32},{96,64},{128,96},{160,128},{192,160},{224,1... | collective-permute-start | bytes 411656 | tf_op jit(solution)/shard_map/ppermute | solution.py:389
  14.3 6.5 %copy-start.5 = (f32[67,512]{1,0:T(8,128)}, f32[67,512]{1,0:T(8,128)S(1)}, u32[]{:S(2)}) copy-start(f32[67,512]{1,0:T(8,128)S(1)} %collective-permute-done.3.t5) | copy-start | bytes 411652
  14.3 6.5 %collective-permute-start.4 = (f32[67,512]{1,0:T(8,128)S(1)}, f32[67,512]{1,0:T(8,128)S(1)}, u32[]{:S(2)}, u32[]{:S(2)}) collective-permute-start(f32[67,512]{1,0:T(8,128)S(1)} %collective-permute-done.3.t5), channel_id=1, source_target_pairs={{0,32},{32,64},{64,96},{96,128},{128,160},{160,192},{192,224},{224... | collective-permute-start | bytes 411656 | tf_op jit(solution)/shard_map/ppermute | solution.py:389
  14.3 6.5 %copy-start.6 = (f32[67,512]{1,0:T(8,128)}, f32[67,512]{1,0:T(8,128)S(1)}, u32[]{:S(2)}) copy-start(f32[67,512]{1,0:T(8,128)S(1)} %collective-permute-done.2.t1) | copy-start | bytes 411652
  14.3 6.5 %collective-permute-start.7 = (f32[67,512]{1,0:T(8,128)S(1)}, f32[67,512]{1,0:T(8,128)S(1)}, u32[]{:S(2)}, u32[]{:S(2)}) collective-permute-start(f32[67,512]{1,0:T(8,128)S(1)} %collective-permute-done.3.t5), channel_id=1, source_target_pairs={{0,224},{32,0},{64,32},{96,64},{128,96},{160,128},{192,160},{224,1... | collective-permute-start | bytes 411656 | tf_op jit(solution)/shard_map/ppermute | solution.py:389
  20.8 0.7 copy-start.7
  20.8 0.7 copy-start.8
  20.8 0.7 %copy-start.10 = (f32[67,512]{1,0:T(8,128)}, f32[67,512]{1,0:T(8,128)S(1)}, u32[]{:S(2)}) copy-start(f32[67,512]{1,0:T(8,128)S(1)} %collective-permute-done.4.t2) | copy-start | bytes 411652
  20.8 0.8 %copy-start.9 = (f32[67,512]{1,0:T(8,128)}, f32[67,512]{1,0:T(8,128)S(1)}, u32[]{:S(2)}) copy-start(f32[67,512]{1,0:T(8,128)S(1)} %collective-permute-done.5.t6) | copy-start | bytes 411652
  20.8 0.8 %copy-start.11 = (f32[67,512]{1,0:T(8,128)}, f32[67,512]{1,0:T(8,128)S(1)}, u32[]{:S(2)}) copy-start(f32[67,512]{1,0:T(8,128)S(1)} %collective-permute-done.7.t8) | copy-start | bytes 411652
  51.9 11.9 %copy-start.2 = (f32[36,128]{1,0:T(8,128)S(1)}, f32[36,128]{1,0:T(8,128)}, u32[]{:S(2)}) copy-start(f32[36,128]{1,0:T(8,128)} %get-tuple-element.33) | copy-start | bytes 55300
  51.9 11.9 %collective-permute-start.8 = (f32[36,128]{1,0:T(8,128)}, f32[36,128]{1,0:T(8,128)S(1)}, u32[]{:S(2)}, u32[]{:S(2)}) collective-permute-start(f32[36,128]{1,0:T(8,128)} %get-tuple-element.34), channel_id=1, source_target_pairs={{0,32},{32,64},{64,96},{96,128},{128,160},{160,192},{192,224},{224... | collective-permute-start | bytes 55304 | tf_op jit(solution)/shard_map/ppermute | solution.py:389
  51.9 11.9 %collective-permute-start.9 = (f32[36,128]{1,0:T(8,128)}, f32[36,128]{1,0:T(8,128)S(1)}, u32[]{:S(2)}, u32[]{:S(2)}) collective-permute-start(f32[36,128]{1,0:T(8,128)} %get-tuple-element.35), channel_id=1, source_target_pairs={{0,224},{32,0},{64,32},{96,64},{128,96},{160,128},{192,160},{224,1... | collective-permute-start | bytes 55304 | tf_op jit(solution)/shard_map/ppermute | solution.py:389
  54.9 17.4 %all-to-all-start = ((f32[32,1,128]{2,1,0:T(1,128)}), f32[32,1,128]{2,1,0:T(1,128)S(1)}, u32[]{:S(2)}, u32[]{:S(2)}) async-start(f32[32,1,128]{2,1,0:T(1,128)} %bitcast.28), calls=%async_computation | async-start | bytes 32768 | tf_op jit(solution)/shard_map/all_to_all | solution.py:403
  63.8 5.8 %collective-permute-start.10 = (f32[3,4,128]{2,1,0:T(4,128)S(1)}, f32[3,4,128]{2,1,0:T(4,128)S(1)}, u32[]{:S(2)}, u32[]{:S(2)}) collective-permute-start(f32[3,4,128]{2,1,0:T(4,128)S(1)} %get-tuple-element.42), channel_id=1, source_target_pairs={{0,1},{1,2},{2,3},{3,4},{4,5},{5,6},{6,7},{7,8},{8,9},{9,10},{10,1... | collective-permute-start | bytes 18440 | tf_op jit(solution)/shard_map/ppermute | solution.py:389
  65.4 4.3 %collective-permute-start.11 = (f32[3,4,128]{2,1,0:T(4,128)S(1)}, f32[3,4,128]{2,1,0:T(4,128)S(1)}, u32[]{:S(2)}, u32[]{:S(2)}) collective-permute-start(f32[3,4,128]{2,1,0:T(4,128)S(1)} %get-tuple-element.41), channel_id=1, source_target_pairs={{0,31},{1,0},{2,1},{3,2},{4,3},{5,4},{6,5},{7,6},{8,7},{9,8},{10,9... | collective-permute-start | bytes 18440 | tf_op jit(solution)/shard_map/ppermute | solution.py:389
